TPU v7x, 128 devices: a whole 4x4x4 slice. The times are simulated.
128 devices in a mesh: blk: 4 (over x_lo, core), dom: 32 (over z, y, x_hi).
Axes of the slice: x: 4 (x_hi: 2, x_lo: 2; x = x_hi * 2 + x_lo), y: 4, z: 4, core: 2. Of those that a mesh axis runs over, the one named last changes fastest.
Arguments:
- node_feats: bfloat16 [65536, 512], P(('blk', 'dom')), may hold values from -6 to 6
- send_rows: int32 [128, 32, 32], P(('blk', 'dom')), may hold values from 0 to 511
- neighbour_slots: int32 [65536, 8], P(('blk', 'dom')), may hold values from 0 to 1535
- slot_mask: int32 [65536, 8], P(('blk', 'dom')), may hold values 0 or 1
- gate_weight: bfloat16 [512, 512], replicated, may hold values from -0.25 to 0.25
- source_weight: bfloat16 [512, 1024], replicated, may hold values from -0.25 to 0.25
- qkv_weight: bfloat16 [512, 1536], replicated, may hold values from -0.26516504 to 0.26516504
- out_weight: bfloat16 [512, 512], replicated, may hold values from -0.25 to 0.25
- cotangent: bfloat16 [65536, 512], P(('blk', 'dom')), may hold values from -6 to 6
Outputs:
- layer_out: bfloat16 [65536, 512], P(('blk', 'dom'))
- feats_grad: bfloat16 [65536, 512], P(('blk', 'dom'))
- gate_grad: float32 [512, 512], replicated
- source_grad: float32 [512, 1024], replicated
- qkv_grad: float32 [512, 1536], replicated
- out_grad: float32 [512, 512], replicated
Inputs may be any that keep to these rules, and one draw needn't show every extreme that they name: `send_rows`: local node indices of the sending device. `neighbour_slots`: rows below 512 are the device's own nodes, the others received rows.
All inputs are finite; a program needn't handle non-finite values. No bound on the sum of `slot_mask` on one device may be relied on, other than what follows from the above.
Results may differ from a plain program's by a relative error of at most 0.035.
Values may be sent and summed in bfloat16 or wider, within the bound.
No kernel may reach another device: no remote copies, remote signals or barrier semaphores. Data moves between devices by JAX's collectives and lax.ppermute only.
A program may use at most 256 MiB of HBM per device.

v0:
```python
import math

import jax
import jax.numpy as jnp
from jax import lax
from jax.sharding import PartitionSpec as P

HEADS = 8
HDIM = 64


def body(
    node_feats,
    send_rows,
    neighbour_slots,
    slot_mask,
    gate_weight,
    source_weight,
    qkv_weight,
    out_weight,
    cotangent,
):
    node_count, feat_width = node_feats.shape
    head_count = HEADS
    head_width = HDIM
    score_scale = 1.0 / math.sqrt(HDIM)
    peer_count = lax.axis_size("dom")
    outgoing = node_feats[send_rows[0]]
    incoming = lax.all_to_all(outgoing, "dom", split_axis=0, concat_axis=0, tiled=True)
    table = jnp.concatenate([node_feats, incoming.reshape(-1, feat_width)], axis=0)
    table_rows = table.shape[0]
    gate_term = jnp.dot(node_feats, gate_weight, preferred_element_type=jnp.float32)
    source_terms = jnp.dot(table, source_weight, preferred_element_type=jnp.float32)
    edge_source = source_terms[neighbour_slots]
    gate_open = jax.nn.sigmoid(gate_term[:, None, :] + edge_source[:, :, :feat_width])
    edge_value = edge_source[:, :, feat_width:]
    mask_float = slot_mask.astype(jnp.float32)
    slot_weight = mask_float / jnp.maximum(jnp.sum(mask_float, axis=1, keepdims=True), 1.0)
    message = jnp.sum(slot_weight[:, :, None] * gate_open * edge_value, axis=1)
    qkv = jnp.dot(node_feats, qkv_weight, preferred_element_type=jnp.float32).astype(jnp.bfloat16)
    queries = qkv[:, :feat_width].reshape(node_count, head_count, head_width)
    keys_vals = lax.all_gather(qkv[:, feat_width:], "blk", axis=0, tiled=True)
    seq_len = keys_vals.shape[0]
    all_keys = keys_vals[:, :feat_width].reshape(seq_len, head_count, head_width)
    all_values = keys_vals[:, feat_width:].reshape(seq_len, head_count, head_width)
    scores = (
        jnp.einsum("ihe,jhe->hij", queries, all_keys, preferred_element_type=jnp.float32)
        * score_scale
    )
    row_top = jnp.max(scores, axis=2, keepdims=True)
    raw_weights = jnp.exp(scores - row_top)
    row_total = jnp.sum(raw_weights, axis=2, keepdims=True)
    prob_weights = raw_weights / row_total
    prob_half = prob_weights.astype(jnp.bfloat16)
    mixed = (
        jnp.einsum("hij,jhe->ihe", prob_half, all_values, preferred_element_type=jnp.float32)
        .astype(jnp.bfloat16)
        .reshape(node_count, feat_width)
    )
    attended = jnp.dot(mixed, out_weight, preferred_element_type=jnp.float32)
    layer_out = (node_feats.astype(jnp.float32) + message + attended).astype(jnp.bfloat16)
    upstream = cotangent.astype(jnp.float32)
    grad_out_w = jnp.einsum("nd,ne->de", mixed, cotangent, preferred_element_type=jnp.float32)
    d_mixed = jnp.einsum(
        "ne,de->nd", cotangent, out_weight, preferred_element_type=jnp.float32
    ).astype(jnp.bfloat16)
    d_heads = d_mixed.reshape(node_count, head_count, head_width)
    row_delta = jnp.sum(
        d_heads.astype(jnp.float32)
        * mixed.reshape(node_count, head_count, head_width).astype(jnp.float32),
        axis=2,
    )
    d_probs = jnp.einsum("ihe,jhe->hij", d_heads, all_values, preferred_element_type=jnp.float32)
    d_scores = (prob_weights * (d_probs - row_delta.T[:, :, None]) * score_scale).astype(
        jnp.bfloat16
    )
    d_query = jnp.einsum(
        "hij,jhe->ihe", d_scores, all_keys, preferred_element_type=jnp.float32
    ).reshape(node_count, feat_width)
    count = node_count * lax.axis_size("blk")
    d_key = jnp.einsum("hij,ihe->jhe", d_scores, queries, preferred_element_type=jnp.float32)
    d_value = jnp.einsum("hij,ihe->jhe", prob_half, d_heads, preferred_element_type=jnp.float32)
    d_keyval = lax.psum_scatter(
        jnp.concatenate(
            [d_key.reshape(count, feat_width), d_value.reshape(count, feat_width)], axis=1
        ),
        "blk",
        scatter_dimension=0,
        tiled=True,
    )
    d_qkv = jnp.concatenate([d_query, d_keyval], axis=1).astype(jnp.bfloat16)
    grad_qkv_w = jnp.einsum("nd,nf->df", node_feats, d_qkv, preferred_element_type=jnp.float32)
    d_attn_input = jnp.einsum("nf,df->nd", d_qkv, qkv_weight, preferred_element_type=jnp.float32)
    edge_up = slot_weight[:, :, None] * upstream[:, None, :]
    d_edge_value = edge_up * gate_open
    d_edge_logit = edge_up * edge_value * gate_open * (1.0 - gate_open)
    d_gate = jnp.sum(d_edge_logit, axis=1).astype(jnp.bfloat16)
    edge_terms = jnp.concatenate([d_edge_logit, d_edge_value], axis=2).reshape(-1, 2 * feat_width)
    d_source = jax.ops.segment_sum(
        edge_terms, neighbour_slots.reshape(-1), num_segments=table_rows
    ).astype(jnp.bfloat16)
    grad_source_w = jnp.einsum("td,tf->df", table, d_source, preferred_element_type=jnp.float32)
    grad_gate_w = jnp.einsum("nd,nf->df", node_feats, d_gate, preferred_element_type=jnp.float32)
    d_table = jnp.einsum("tf,df->td", d_source, source_weight, preferred_element_type=jnp.float32)
    returned = lax.all_to_all(
        d_table[node_count:].reshape(peer_count, -1, feat_width).astype(jnp.bfloat16),
        "dom",
        split_axis=0,
        concat_axis=0,
        tiled=True,
    ).astype(jnp.float32)
    d_sent = jax.ops.segment_sum(
        returned.reshape(-1, feat_width), send_rows[0].reshape(-1), num_segments=node_count
    )
    d_gate_input = jnp.einsum("nf,df->nd", d_gate, gate_weight, preferred_element_type=jnp.float32)
    feats_grad = (upstream + d_attn_input + d_table[:node_count] + d_gate_input + d_sent).astype(
        jnp.bfloat16
    )
    weight_sums = lax.psum((grad_gate_w, grad_source_w, grad_qkv_w, grad_out_w), ("blk", "dom"))
    return (layer_out, feats_grad, weight_sums[0], weight_sums[1], weight_sums[2], weight_sums[3])


def solution(mesh):
    return jax.shard_map(
        body,
        mesh=mesh,
        in_specs=(
            P(("blk", "dom"), None),
            P(("blk", "dom"), None, None),
            P(("blk", "dom"), None),
            P(("blk", "dom"), None),
            P(),
            P(),
            P(),
            P(),
            P(("blk", "dom"), None),
        ),
        out_specs=(P(("blk", "dom"), None), P(("blk", "dom"), None), P(), P(), P(), P()),
        check_vma=False,
    )
```

profile of v0, /device:TPU:1, one launch (start us, length us, event | category | flops | bytes accessed | tf_op | source)
XLA Modules:
  0.0 508.1 jit_solution(13844792690348114465)
XLA Ops:
  7.2 0.0 all-gather.2.cloned.1.call-start
  7.2 1.3 copy-done
  8.6 2.0 convolution_convert_fusion
  10.6 1.1 copy-done.9
  11.8 1.1 slice.39
  12.8 0.0 all-gather.2.cloned.1.call-update
  12.9 0.0 reduce-scatter.2.cloned.1.call-start
  12.9 1.1 slice.41
  14.0 1.0 copy.27
  15.0 0.5 convolution_convert_fusion.1
  15.5 47.7 %all-gather.2.cloned.1.call-done = bf16[2048,1024]{1,0:T(8,128)(2,1)} async-done(((bf16[512,1024]{1,0:T(8,128)(2,1)}), bf16[2048,1024]{1,0:T(8,128)(2,1)}) %all-gather.2.cloned.1.call-update) | async-done | bytes 4194320 | tf_op jit(solution)/shard_map/all_gather | solution.py:42
  63.2 4.5 fusion.36
  67.7 4.0 copy.28
  71.7 3.9 copy.26
  75.6 16.6 %fusion.37 = (f32[8,512]{1,0:T(8,128)S(1)}, f32[8,512,2048]{2,1,0:T(8,128)}) fusion(bf16[512,8,64]{0,2,1:T(8,128)(2,1)S(1)} %bitcast.82, bf16[2048,8,64]{0,2,1:T(8,128)(2,1)} %bitcast.71), kind=kOutput, calls=%fused_computation.67 | convolution fusion | flops 1098909696 | bytes 36192256 | tf_op jit(solution)/shard_map/sub | solution.py:51
  92.2 19.0 %fusion.8 = bf16[8,512,2048]{2,1,0:T(8,128)(2,1)} fusion(f32[8,512,2048]{2,1,0:T(8,128)} %get-tuple-element.29, f32[8,512]{1,0:T(8,128)S(1)} %get-tuple-element.28), kind=kLoop, calls=%fused_computation.15 | loop fusion | flops 16777216 | bytes 50348032 | tf_op jit(solution)/shard_map/convert_element_type | solution.py:54
  111.3 13.0 %multiply_reduce_fusion.2 = (f32[512,8]{0,1:T(8,128)}, bf16[8,64,512]{2,1,0:T(8,128)(2,1)}) fusion(bf16[512,512]{0,1:T(8,128)(2,1)S(1)} %convolution_convert_fusion.1, bf16[2048,8,64]{0,2,1:T(8,128)(2,1)} %bitcast.73, bf16[8,512,2048]{2,1,0:T(8,128)(2,1)} %fusion.8), kind=kOutput, calls=%fused_computation.49 | convolution fusion | flops 1075048448 | bytes 19939328 | tf_op jit(solution)/shard_map/hij,jhe->ihe/dot_general | solution.py:56
  124.3 10.8 %fusion.40 = f32[8,64,2048]{2,1,0:T(8,128)} fusion(bf16[512,8,64]{0,2,1:T(8,128)(2,1)S(1)} %bitcast.77, bf16[8,512,2048]{2,1,0:T(8,128)(2,1)} %fusion.8), kind=kOutput, calls=%fused_computation.70 | convolution fusion | flops 1073741824 | bytes 21495808 | tf_op jit(solution)/shard_map/hij,ihe->jhe/dot_general | solution.py:82
  135.1 13.4 %multiply_convert_fusion = bf16[8,512,2048]{2,1,0:T(8,128)(2,1)S(1)} fusion(bf16[512,8,64]{0,2,1:T(8,128)(2,1)S(1)} %bitcast.78, bf16[2048,8,64]{0,2,1:T(8,128)(2,1)} %bitcast.74, f32[8,512]{1,0:T(8,128)} %bitcast.85, f32[8,512,2048]{2,1,0:T(8,128)} %get-tuple-element.29, f32[8,512]{1,0:T(8,128)S(1)} %get-tuple-element.28), kind=kOutput, calls=%fused_computation.5 | convolution fusion | flops 1115684864 | bytes 52985856 | tf_op jit(solution)/shard_map/ihe,jhe->hij/dot_general | solution.py:73
  148.5 7.0 %fusion.39 = f32[8,64,2048]{2,1,0:T(8,128)} fusion(bf16[512,8,64]{0,2,1:T(8,128)(2,1)} %bitcast.81, bf16[8,512,2048]{2,1,0:T(8,128)(2,1)S(1)} %multiply_convert_fusion), kind=kOutput, calls=%fused_computation.69 | convolution fusion | flops 1073741824 | bytes 21495808 | tf_op jit(solution)/shard_map/hij,ihe->jhe/dot_general | solution.py:81
  155.5 0.0 copy-done.2
  155.5 7.8 %pad_maximum_fusion = f32[2048,1024]{0,1:T(8,128)} fusion(f32[2048,512]{0,1:T(8,128)} %bitcast.69, f32[2048,512]{0,1:T(8,128)} %bitcast.70), kind=kLoop, calls=%fused_computation.25 | loop fusion | flops 2097152 | bytes 16777216 | tf_op jit(solution)/shard_map/concatenate | solution.py:84
  163.3 0.7 copy-done.14
  164.0 0.1 reshape.105
  164.1 0.3 copy-done.1
  164.3 5.1 gather_fusion
  169.4 9.2 %all-to-all-start = ((bf16[32,32,512]{2,1,0:T(8,128)(2,1)}), bf16[32,32,512]{2,1,0:T(8,128)(2,1)}, u32[]{:S(2)}, u32[]{:S(2)}) async-start(bf16[32,32,512]{2,1,0:T(8,128)(2,1)} %bitcast.79), calls=%async_computation | async-start | bytes 2097152 | tf_op jit(solution)/shard_map/all_to_all | solution.py:29
  178.7 0.2 all-reduce.3.cloned.1.call-start
  178.9 1.1 convert_element_type.58
  180.0 0.8 copy.29
  180.8 0.1 copy.25
  181.0 0.2 reshape.113
  181.2 0.1 copy.24
  181.3 1.1 reshape.121
  182.4 1.4 fusion.38
  183.8 25.8 %all-to-all-done = bf16[32,32,512]{2,1,0:T(8,128)(2,1)} async-done(((bf16[32,32,512]{2,1,0:T(8,128)(2,1)}), bf16[32,32,512]{2,1,0:T(8,128)(2,1)}, u32[]{:S(2)}, u32[]{:S(2)}) %all-to-all-start) | async-done | bytes 1048608 | tf_op jit(solution)/shard_map/all_to_all | solution.py:29
  209.6 6.0 %fusion.26 = f32[1536,1024]{1,0:T(8,128)} fusion(bf16[512,1024]{1,0:T(8,128)(2,1)} %param.14, bf16[1024,512]{1,0:T(8,128)(2,1)} %bitcast.2, bf16[512,512]{1,0:T(8,128)(2,1)S(1)} %copy-done.1), kind=kOutput, calls=%fused_computation.50 | convolution fusion | flops 1613758464 | bytes 8912896 | tf_op jit(solution)/shard_map/dot_general | solution.py:33
  215.6 25.1 %gather_fusion.1 = f32[4096,1024]{1,0:T(8,128)} fusion(f32[1536,1024]{1,0:T(8,128)} %fusion.26, s32[4096]{0:T(1024)S(1)} %broadcast_clamp_fusion), kind=kCustom, calls=%fused_computation.1 | custom fusion | bytes 33570816 | tf_op jit(solution)/shard_map/gather | solution.py:34
  240.7 18.9 %fusion.34 = (bf16[512,512]{1,0:T(8,128)(2,1)S(1)}, f32[512,8,512]{2,1,0:T(8,128)}, f32[512,8,512]{2,1,0:T(8,128)}, f32[512,512]{1,0:T(8,128)}) fusion(f32[512,8,1024]{2,1,0:T(8,128)} %bitcast.68, f32[512,512]{1,0:T(8,128)} %fusion.38, f32[512,512]{1,0:T(8,128)} %convert_element_type.58, f32[512,8]{1,0:T(8,128)S(1)} %copy.24), kind=kLoop, calls=%fused_computation.65 | loop fusion | flops 28835840 | bytes 37240832 | tf_op jit(solution)/shard_map/reduce_sum | solution.py:97
  259.6 38.4 %scatter_custom_fusion = f32[1536,1024]{1,0:T(8,128)} fusion(s32[4096]{0:T(1024)S(1)} %reshape.121, f32[512,8,512]{2,1,0:T(8,128)} %get-tuple-element.24, f32[]{:T(128)} %constant.2.clone.1, f32[512,8,512]{2,1,0:T(8,128)} %get-tuple-element.23, f32[]{:T(128)} %constant.7.clone.1), kind=kCustom, calls=%fused_computation.10 | custom fusion | flops 8388608 | bytes 23068680 | tf_op jit(solution)/shard_map/scatter-add | solution.py:99
  298.1 1.4 convolution_bitcast_fusion.1
  299.5 6.2 %fusion.20 = f32[512,1024]{1,0:T(8,128)} fusion(f32[1536,1024]{1,0:T(8,128)} %scatter_custom_fusion, bf16[1024,512]{1,0:T(8,128)(2,1)} %bitcast.2, bf16[512,512]{1,0:T(8,128)(2,1)S(1)} %copy-done.1), kind=kOutput, calls=%fused_computation.36 | convolution fusion | flops 1615331328 | bytes 9961472 | tf_op jit(solution)/shard_map/td,tf->df/dot_general | solution.py:102
  305.8 1.4 fusion.41
  307.2 12.4 %convolution_convert_fusion.2 = bf16[8,64,512]{2,1,0:T(8,128)(2,1)} fusion(bf16[2048,8,64]{0,2,1:T(8,128)(2,1)} %bitcast.72, bf16[8,512,2048]{2,1,0:T(8,128)(2,1)} %copy-done.2), kind=kOutput, calls=%fused_computation.47 | convolution fusion | flops 1074003968 | bytes 19398656 | tf_op jit(solution)/shard_map/hij,jhe->ihe/dot_general | solution.py:77
  319.6 1.7 convert.13
  321.4 1.0 copy-done.10
  322.3 3.7 convolution_bitcast_fusion
  326.0 0.0 all-reduce.3.cloned.1.call-update
  326.0 4.9 fusion.22
  331.0 1.7 copy-done.12
  332.6 1.1 slice.64
  333.8 4.9 all-to-all-start.1
  338.7 0.1 reshape.129
  338.8 2.9 fusion.25
  341.7 2.8 fusion.24
  344.5 1.4 convolution_add_fusion
  346.0 13.1 %all-to-all-done.1 = bf16[32,32,512]{2,1,0:T(8,128)(2,1)} async-done(((bf16[32,32,512]{2,1,0:T(8,128)(2,1)}), bf16[32,32,512]{2,1,0:T(8,128)(2,1)}, u32[]{:S(2)}, u32[]{:S(2)}) %all-to-all-start.1) | async-done | bytes 1048608 | tf_op jit(solution)/shard_map/all_to_all | solution.py:105
  359.0 9.4 %scatter_custom_fusion.1 = f32[512,512]{1,0:T(8,128)} fusion(f32[512,512]{1,0:T(8,128)} %convolution_add_fusion, s32[1024]{0:T(1024)S(1)} %reshape.129, bf16[1024,512]{1,0:T(8,128)(2,1)} %bitcast.26), kind=kCustom, calls=%fused_computation.32 | custom fusion | flops 1048576 | bytes 2097152 | tf_op jit(solution)/shard_map/scatter-add | solution.py:112
  368.4 2.1 convert_element_type.66
  370.6 120.5 %all-reduce.3.cloned.1.call-done = (f32[512,512]{0,1:T(8,128)}, f32[512,1024]{1,0:T(8,128)}, f32[512,1536]{0,1:T(8,128)}, f32[512,512]{1,0:T(8,128)}) async-done(((f32[512,512]{0,1:T(8,128)}, f32[512,1024]{1,0:T(8,128)}, f32[512,1536]{0,1:T(8,128)}, f32[512,512]{1,0:T(8,128)}), (f32[512,512]{0,1:T(8,128)}, f32[512,1024]{1,0:T(8,128)}, f32[512,1536]{0,1:T(8,128)}, ...) | async-done | bytes 7340048 | tf_op jit(solution)/shard_map/psum | solution.py:119
  491.0 2.6 copy.30
  493.6 3.5 copy.31
  497.2 3.2 copy.37
  500.3 1.0 copy.38
  (34 shorter events, 0.1 us)
Async XLA Ops:
  7.2 1.4 copy-start
  7.2 7.8 %copy-start.3 = (bf16[512,512]{1,0:T(8,128)(2,1)S(1)}, bf16[512,512]{1,0:T(8,128)(2,1)}, u32[]{:S(2)}) copy-start(bf16[512,512]{1,0:T(8,128)(2,1)} %param.17) | copy-start | bytes 1572868
  7.2 7.8 %copy-start.5 = (bf16[512,512]{1,0:T(8,128)(2,1)S(1)}, bf16[512,512]{1,0:T(8,128)(2,1)}, u32[]{:S(2)}) copy-start(bf16[512,512]{1,0:T(8,128)(2,1)} %param.16) | copy-start | bytes 1572868
  7.2 56.0 %all-gather.2.cloned.1.call-start = ((), (), s32[]{:S(2)}) async-start(), calls=%async_computation.3 | async-start | bytes 5242880 | tf_op jit(solution)/shard_map/all_gather | solution.py:42
  10.6 1.1 copy-start.9
  12.9 306.7 %reduce-scatter.2.cloned.1.call-start = ((), (), s32[]{:S(2)}) async-start(), calls=%async_computation.4 | async-start | bytes 10485760 | tf_op jit(solution)/shard_map/reduce_scatter | solution.py:83
  67.7 7.9 %copy-start.8 = (bf16[512,512]{0,1:T(8,128)(2,1)S(1)}, bf16[512,512]{0,1:T(8,128)(2,1)}, u32[]{:S(2)}) copy-start(bf16[512,512]{0,1:T(8,128)(2,1)} %copy.27) | copy-start | bytes 1572868
  148.5 7.0 %copy-start.2 = (bf16[8,512,2048]{2,1,0:T(8,128)(2,1)}, bf16[8,512,2048]{2,1,0:T(8,128)(2,1)S(1)}, u32[]{:S(2)}) copy-start(bf16[8,512,2048]{2,1,0:T(8,128)(2,1)S(1)} %multiply_convert_fusion) | copy-start | bytes 50331652
  163.3 0.7 copy-start.14
  163.3 1.1 copy-start.1
  164.3 15.7 %copy-start.13 = (s32[512,8]{0,1:T(8,128)S(1)}, s32[512,8]{0,1:T(8,128)}, u32[]{:S(2)}) copy-start(s32[512,8]{0,1:T(8,128)} %param.11) | copy-start | bytes 49156
  164.3 16.8 %copy-start.15 = (s32[512,8]{0,1:T(8,128)S(1)}, s32[512,8]{0,1:T(8,128)}, u32[]{:S(2)}) copy-start(s32[512,8]{0,1:T(8,128)} %param.12) | copy-start | bytes 49156
  164.3 18.1 %copy-start.6 = (bf16[512,512]{1,0:T(8,128)(2,1)S(1)}, bf16[512,512]{1,0:T(8,128)(2,1)}, u32[]{:S(2)}) copy-start(bf16[512,512]{1,0:T(8,128)(2,1)} %param.13) | copy-start | bytes 1572868
  169.4 40.2 %all-to-all-start = ((bf16[32,32,512]{2,1,0:T(8,128)(2,1)}), bf16[32,32,512]{2,1,0:T(8,128)(2,1)}, u32[]{:S(2)}, u32[]{:S(2)}) async-start(bf16[32,32,512]{2,1,0:T(8,128)(2,1)} %bitcast.79), calls=%async_computation | async-start | bytes 2097152 | tf_op jit(solution)/shard_map/all_to_all | solution.py:29
  178.7 312.4 %all-reduce.3.cloned.1.call-start = ((), (), s32[]{:S(2)}) async-start(), calls=%async_computation.5 | async-start | bytes 14680064 | tf_op jit(solution)/shard_map/psum | solution.py:119
  298.1 7.7 %copy-start.4 = (bf16[8,64,512]{2,1,0:T(8,128)(2,1)S(1)}, bf16[8,64,512]{2,1,0:T(8,128)(2,1)}, u32[]{:S(2)}) copy-start(bf16[8,64,512]{2,1,0:T(8,128)(2,1)} %get-tuple-element.31) | copy-start | bytes 1572868
  321.3 1.0 copy-start.10
  331.0 1.7 copy-start.12
  333.8 25.3 %all-to-all-start.1 = ((bf16[32,32,512]{2,1,0:T(8,128)(2,1)}), bf16[32,32,512]{2,1,0:T(8,128)(2,1)}, u32[]{:S(2)}, u32[]{:S(2)}) async-start(bf16[32,32,512]{2,1,0:T(8,128)(2,1)} %bitcast.80), calls=%async_computation.2 | async-start | bytes 2097152 | tf_op jit(solution)/shard_map/all_to_all | solution.py:105
  338.8 5.7 %copy-start.7 = (bf16[512,512]{1,0:T(8,128)(2,1)S(1)}, bf16[512,512]{1,0:T(8,128)(2,1)}, u32[]{:S(2)}) copy-start(bf16[512,512]{1,0:T(8,128)(2,1)} %param.13) | copy-start | bytes 1572868
  491.0 9.3 %copy-start.11 = (f32[512,512]{1,0:T(8,128)S(1)}, f32[512,512]{1,0:T(8,128)}, u32[]{:S(2)}) copy-start(f32[512,512]{1,0:T(8,128)} %get-tuple-element.37) | copy-start | bytes 3145732
Sparse Core Ops, SparseCore 0:
  13.0 50.1 all-gather.1
  163.4 90.9 reduce-scatter.1
  326.2 164.8 all-reduce.2
where the time goes:
time: 515 us; the launch traced here: 508 us
  waiting for transfers between devices  207 us (40%)
  matrix products  108 us (21%)
  other arithmetic  98.5 us (19%)
  local copies, waits for them, and re-layouts  65.8 us (13%)
  starting transfers between devices  14.4 us (3%)
  between operations  14.2 us (3%)
    psum x1, waiting for transfers between devices, body(): lax.psum((grad_gate_w, grad_source_w, grad_qkv_w, grad_out_w), ('blk', 'd...  120 us
    all_gather x1, waiting for transfers between devices, body(): keys_vals = lax.all_gather(qkv[:, feat_width:], 'blk', axis=0, tiled=True)  47.7 us
    scatter-add x1, other arithmetic, body(): jax.ops.segment_sum(edge_terms, neighbour_slots.reshape(-1), num_segments...  38.4 us
    all_to_all x1, waiting for transfers between devices, body(): lax.all_to_all(outgoing, 'dom', split_axis=0, concat_axis=0, tiled=True)  25.8 us
    gather x1, local copies, waits for them, and re-layouts, body(): edge_source = source_terms[neighbour_slots]  25.1 us
    convert_element_type x1, other arithmetic, body(): prob_half = prob_weights.astype(jnp.bfloat16)  19 us
    reduce_sum x1, other arithmetic, body(): d_gate = jnp.sum(d_edge_logit, axis=1).astype(jnp.bfloat16)  18.9 us
    unnamed x37, local copies, waits for them, and re-layouts  17.2 us
  transfers between devices with their start and end apart: 5, of which 4 were waited for; matrix products, arithmetic and copies ran while one was open for 29% of the time, Pallas kernels for 0%

commit v1 on v0

v1 whole, which is shorter than its diff:
```python
import functools

import jax
import jax.numpy as jnp
from jax import lax
from jax.experimental import pallas as pl
from jax.experimental.pallas import tpu as pltpu
from jax.sharding import Mesh, PartitionSpec as P

BF = jnp.bfloat16
F32 = jnp.float32
NT = (((1,), (1,)), ((), ()))
NN = (((1,), (0,)), ((), ()))
TN = (((0,), (0,)), ((), ()))
LOG2E = 1.4426950408889634
NACC = 2
UN = 2
ALL = ("xl", "c", "z", "y", "xh")
CHIPS = ("xl", "z", "y", "xh")
DOM = ("z", "y", "xh")
SWAP = [(0, 1), (1, 0)]


def attn_kernel(xa, cot, w, mixed_o, dq_o, dk_o, dv_o, k_s, v_s, kt_s, vt_s, qt_s, dmt_s, s_s, e_s, d_s, dka, dva, mt_s, dqt_s):
    seq=xa.shape[0]; nq=cot.shape[0]; hw=w.shape[1]
    CK=256; QB=256
    scale=0.125; c2=scale*LOG2E
    dg=functools.partial(lax.dot_general, preferred_element_type=F32)
    qt_s[...]=dg(w[0],xa[0:nq,:],NT).astype(BF)
    kt_s[...]=dg(w[1],xa[...],NT).astype(BF)
    vt_s[...]=dg(w[2],xa[...],NT).astype(BF)
    k_s[...]=dg(xa[...],w[1],NT).astype(BF)
    v_s[...]=dg(xa[...],w[2],NT).astype(BF)
    dmt_s[...]=dg(w[3],cot[...],NT).astype(BF)
    row=lax.broadcasted_iota(jnp.int32,(128,QB),0)
    def bd(x):
        z=jnp.zeros_like(x)
        return jnp.concatenate([jnp.where(row<64,x,z),jnp.where(row>=64,x,z)],axis=1)
    for p in range(2):
        ps=slice(p*128,p*128+128)
        dka[...]=jnp.zeros_like(dka)
        dva[...]=jnp.zeros_like(dva)
        def qblock(b,_):
            qc=pl.ds(pl.multiple_of(b*QB,QB),QB)
            qt=qt_s[ps,qc]; dmt=dmt_s[ps,qc]
            qbd=bd(qt)
            mx=jnp.full((8,2*QB),-jnp.inf,F32)
            for c in range(seq//CK):
                cs=slice(c*CK,c*CK+CK)
                s=dg(k_s[cs,ps],qbd,NN)
                s_s[cs,:]=s
                mx=jnp.maximum(mx,jnp.max(s.reshape(CK//8,8,2*QB),axis=0))
            m=jnp.max(mx,axis=0,keepdims=True)*c2
            ls=jnp.zeros((8,2*QB),F32)
            acc=[jnp.zeros((64,QB),F32),jnp.zeros((64,QB),F32)]
            for c in range(seq//CK):
                cs=slice(c*CK,c*CK+CK)
                e=jnp.exp2(s_s[cs,:]*c2-m)
                ls=ls+jnp.sum(e.reshape(CK//8,8,2*QB),axis=0)
                s_s[cs,:]=e
            inv=1.0/jnp.sum(ls,axis=0,keepdims=True)
            for c in range(seq//CK):
                cs=slice(c*CK,c*CK+CK)
                eb=(s_s[cs,:]*inv).astype(BF)
                e_s[cs,:]=eb
                for h in range(2):
                    acc[h]=acc[h]+dg(vt_s[p*128+h*64:p*128+h*64+64,cs],eb[:,h*QB:h*QB+QB],NN)
            dl=[];dn=[]
            for h in range(2):
                hs=slice(p*128+h*64,p*128+h*64+64)
                ih=inv[:,h*QB:h*QB+QB]
                mt=acc[h].astype(BF)
                mt_s[hs,qc]=mt
                dmh=dmt[h*64:h*64+64,:].astype(F32)
                dl.append(jnp.sum(dmh*mt.astype(F32),axis=0,keepdims=True))
                dn.append(dmh.astype(BF))
            delta=jnp.concatenate(dl,axis=1)
            cs_row=inv*scale
            dmbd=bd(dmt)
            dnbd=bd(jnp.concatenate(dn,axis=0))
            dqa=[jnp.zeros((64,QB),F32),jnp.zeros((64,QB),F32)]
            for c in range(seq//CK):
                cs=slice(c*CK,c*CK+CK)
                eb=e_s[cs,:]
                dva[cs,:]+=dg(eb,dnbd,NT)
                dp=dg(v_s[cs,ps],dmbd,NN)
                ds=((dp-delta)*(s_s[cs,:]*cs_row)).astype(BF)
                dka[cs,:]+=dg(ds,qbd,NT)
                for h in range(2):
                    dqa[h]=dqa[h]+dg(kt_s[p*128+h*64:p*128+h*64+64,cs],ds[:,h*QB:h*QB+QB],NN)
            for h in range(2):
                dqt_s[p*128+h*64:p*128+h*64+64,qc]=dqa[h]
            return 0
        lax.fori_loop(0,nq//QB,qblock,0)
        dk_o[:,ps]=dka[...].astype(BF)
        dv_o[:,ps]=dva[...].astype(BF)
    mixed_o[...]=mt_s[...].T
    dq_o[...]=dqt_s[...].T.astype(BF)

def attention(xa,cot,w):
    seq=xa.shape[0]; nq=cot.shape[0]; hw=w.shape[1]
    sd=jax.ShapeDtypeStruct
    V=pltpu.VMEM
    vm=pl.BlockSpec(memory_space=pltpu.VMEM)
    return pl.pallas_call(attn_kernel,
        out_shape=(sd((nq,hw),BF),sd((nq,hw),BF),sd((seq,hw),BF),sd((seq,hw),BF)),
        in_specs=[vm]*3, out_specs=(vm,)*4,
        scratch_shapes=[V((seq,hw),BF),V((seq,hw),BF),V((hw,seq),BF),V((hw,seq),BF),V((hw,nq),BF),V((hw,nq),BF),
            V((seq,512),F32),V((seq,512),BF),V((8,128),BF),V((seq,128),F32),V((seq,128),F32),V((hw,nq),BF),V((hw,nq),F32)],
        compiler_params=pltpu.CompilerParams(vmem_limit_bytes=56*2**20),
        cost_estimate=pl.CostEstimate(flops=26*10**9,bytes_accessed=8*2**20,transcendentals=8*2**20),
        name="attention")(xa,cot,w)


def gnn_kernel(idx, tab, cot, inv, wg, ws, msg_o, dsrc_o, dgate_o, a_s, b_s, gt_s, up_s, *accs):
    rows=tab.shape[0]; n=cot.shape[0]
    dg=functools.partial(lax.dot_general, preferred_element_type=F32)
    R=128
    def fill(i,_):
        base=pl.multiple_of(i*R,R)
        t=dg(tab[pl.ds(base,R),:],ws[...],NN)
        for c in range(4):
            g=t[:,c*128:c*128+128]*0.5
            v=t[:,512+c*128:512+c*128+128]
            a_s[pl.ds(base*8+c,R,stride=8),:]=g
            a_s[pl.ds(base*8+4+c,R,stride=8),:]=g
            b_s[pl.ds(base*8+c,R,stride=8),:]=v
            b_s[pl.ds(base*8+4+c,R,stride=8),:]=jnp.full_like(v,2.0)
        for acc in accs:
            acc[pl.ds(pl.multiple_of(base*8,8),R*8),:]=jnp.zeros((R*8,128),F32)
        return 0
    lax.fori_loop(0,rows//R,fill,0)
    a_s[pl.ds(rows*8,8),:]=jnp.zeros((8,128),F32)
    b_s[pl.ds(rows*8,8),:]=jnp.zeros((8,128),F32)
    for acc in accs: acc[pl.ds(rows*8,8),:]=jnp.zeros((8,128),F32)
    def filln(i,_):
        base=pl.multiple_of(i*R,R)
        t=dg(tab[pl.ds(base,R),:],wg[...],NN)*0.5
        u=cot[pl.ds(base,R),:].astype(F32)*(inv[pl.ds(base,R),:]*0.25)
        for c in range(4):
            g=t[:,c*128:c*128+128]; uu=u[:,c*128:c*128+128]
            for h in (0,4):
                gt_s[pl.ds(base*8+h+c,R,stride=8),:]=g
                up_s[pl.ds(base*8+h+c,R,stride=8),:]=uu
        return 0
    lax.fori_loop(0,n//R,filln,0)
    hm=jnp.where(lax.broadcasted_iota(jnp.int32,(8,128),0)<4,1.0,0.0).astype(F32)
    def node(i):
        nb=pl.multiple_of(i*8,8)
        gt=gt_s[pl.ds(nb,8),:]; up=up_s[pl.ds(nb,8),:]
        ms=None; dgs=None
        for k in range(8):
            j=pl.multiple_of(idx[i*8+k],8)
            t=jnp.tanh(a_s[pl.ds(j,8),:]+gt)
            p=(1.0+t)*b_s[pl.ds(j,8),:]
            d=p*(1.0-t*hm)*up
            ms=p if ms is None else ms+p
            dgs=d if dgs is None else dgs+d
            acc=accs[k%NACC]
            acc[pl.ds(j,8),:]=acc[pl.ds(j,8),:]+d
        gt_s[pl.ds(nb,8),:]=ms
        up_s[pl.ds(nb,8),:]=dgs
    def loop(i,_):
        for u in range(UN): node(i*UN+u)
        return 0
    lax.fori_loop(0,n//UN,loop,0)
    def out(i,_):
        base=pl.multiple_of(i*R,R)
        for c in range(8):
            v=accs[0][pl.ds(base*8+c,R,stride=8),:]
            for acc in accs[1:]: v=v+acc[pl.ds(base*8+c,R,stride=8),:]
            dsrc_o[pl.ds(base,R),c*128:c*128+128]=v.astype(BF)
        return 0
    lax.fori_loop(0,rows//R,out,0)
    def outn(i,_):
        base=pl.multiple_of(i*R,R)
        iv=inv[pl.ds(base,R),:]*0.5
        for c in range(4):
            msg_o[pl.ds(base,R),c*128:c*128+128]=gt_s[pl.ds(base*8+c,R,stride=8),:]*iv
            dgate_o[pl.ds(base,R),c*128:c*128+128]=up_s[pl.ds(base*8+c,R,stride=8),:].astype(BF)
        return 0
    lax.fori_loop(0,n//R,outn,0)

def gnn(idx,tab,cot,inv,wg,ws):
    rows=tab.shape[0]; n=cot.shape[0]
    sd=jax.ShapeDtypeStruct
    V=pltpu.VMEM
    vm=pl.BlockSpec(memory_space=pltpu.VMEM)
    sm=pl.BlockSpec(memory_space=pltpu.SMEM)
    big=V(((rows+1)*8,128),F32); nd=V((n*8,128),F32)
    return pl.pallas_call(gnn_kernel,
        out_shape=(sd((n,512),F32),sd((rows,1024),BF),sd((n,512),BF)),
        in_specs=[sm]+[vm]*5, out_specs=(vm,)*3,
        scratch_shapes=[big,big,nd,nd]+[big]*NACC,
        compiler_params=pltpu.CompilerParams(vmem_limit_bytes=56*2**20),
        cost_estimate=pl.CostEstimate(flops=10*10**9,bytes_accessed=8*2**20,transcendentals=4*2**20),
        name="edges")(idx,tab,cot,inv,wg,ws)


def dot(a, b, dims):
    return lax.dot_general(a, b, dims, preferred_element_type=F32)


def chip_sum(part):
    w = part.shape[1]
    got = lax.all_to_all(part.astype(BF).reshape(64, 8, w), CHIPS, 0, 0, tiled=True)
    mine = jnp.sum(got.astype(F32), axis=0).astype(BF)
    spread = jnp.broadcast_to(mine[None], (64, 8, w))
    return lax.all_to_all(spread, CHIPS, 0, 0, tiled=True).reshape(512, w)


def body(x, send_rows, slots, mask, wg, ws, wqkv, wo, cot):
    core = lax.axis_index("c")
    n, d = x.shape
    rows = send_rows.reshape(-1)
    pick = (rows[:, None] == lax.broadcasted_iota(jnp.int32, (rows.shape[0], n), 1)).astype(BF)
    outgoing = dot(pick, x, NN).astype(BF)
    incoming = lax.all_to_all(outgoing.reshape(32, 32, d), DOM, 0, 0, tiled=True).reshape(-1, d)
    x_sib = lax.ppermute(x, "c", SWAP)
    cot_sib = lax.ppermute(cot, "c", SWAP)
    x_far = lax.ppermute(x, "xl", SWAP)
    x_far_sib = lax.ppermute(x_far, "c", SWAP)
    xa = jnp.concatenate([x, x_sib, x_far, x_far_sib], axis=0)
    ca = jnp.concatenate([cot, cot_sib], axis=0)
    w3 = lax.dynamic_index_in_dim(wqkv.reshape(d, 3, 2, 256), core, 2, keepdims=False)
    wo2 = wo.reshape(2, 256, d)
    wo_own = lax.dynamic_index_in_dim(wo2, core, 0, keepdims=False)
    wo_sib = lax.dynamic_index_in_dim(wo2, 1 - core, 0, keepdims=False)
    slab = jnp.concatenate([w3.transpose(1, 2, 0), wo_own[None]], axis=0)
    mixed, dq, dk, dv = attention(xa, ca, slab)
    mixed_sib = lax.ppermute(mixed[n:], "c", SWAP)
    attended = dot(mixed[:n], wo_own, NN) + dot(mixed_sib, wo_sib, NN)
    wq, wk, wv = w3[:, 0], w3[:, 1], w3[:, 2]
    dkv = jnp.concatenate([dk, dv], axis=1)
    wkv = jnp.concatenate([wk, wv], axis=1)
    d_near = dot(jnp.concatenate([dq, dkv[: 2 * n]], axis=1), w3.reshape(d, -1), NT)
    d_far = dot(dkv[2 * n :], wkv, NT)
    from_sib = lax.ppermute(jnp.concatenate([d_near[n:], d_far[n:]], axis=0).astype(BF), "c", SWAP)
    to_far = (d_far[:n] + from_sib[n:].astype(F32)).astype(BF)
    from_far = lax.ppermute(to_far, "xl", SWAP)
    attn_grad = jnp.concatenate(
        [dot(xa[: 2 * n], dq, TN), dot(xa, dkv, TN), dot(ca, mixed, TN)], axis=1
    )
    attn_sum = chip_sum(attn_grad)
    table = jnp.concatenate([x, incoming], axis=0)
    on = mask > 0
    idx = (jnp.where(on, slots, table.shape[0]) * 8).reshape(-1)
    inv = 1.0 / jnp.maximum(jnp.sum(mask.astype(F32), axis=1, keepdims=True), 1.0)
    message, d_source, d_gate = gnn(idx, table, cot, inv, wg, ws)
    layer_out = (x.astype(F32) + message + attended).astype(BF)
    d_remote = dot(d_source[n:], ws, NT).astype(BF)
    returned = lax.all_to_all(d_remote.reshape(32, 32, d), DOM, 0, 0, tiled=True).reshape(-1, d)
    edge_grad = jnp.concatenate([dot(table, d_source, TN), dot(x, d_gate, TN)], axis=1)
    half = edge_grad.shape[1] // 2
    keep = lax.dynamic_slice_in_dim(edge_grad, core * half, half, 1)
    give = lax.dynamic_slice_in_dim(edge_grad, (1 - core) * half, half, 1).astype(BF)
    edge_sum = chip_sum(keep + lax.ppermute(give, "c", SWAP).astype(F32))
    feats_grad = (
        cot.astype(F32)
        + d_near[:n]
        + from_sib[:n].astype(F32)
        + from_far.astype(F32)
        + dot(d_source[:n], ws, NT)
        + dot(d_gate, wg, NT)
        + dot(pick, returned, TN)
    ).astype(BF)

    def both(own):
        other = lax.ppermute(own, "c", SWAP)
        first = jnp.where(core == 0, own, other).astype(F32)
        second = jnp.where(core == 0, other, own).astype(F32)
        return first, second

    a0, a1 = both(attn_sum)
    qkv_grad = jnp.concatenate(
        [t for i in range(3) for t in (a0[:, i * 256 : i * 256 + 256], a1[:, i * 256 : i * 256 + 256])], axis=1
    )
    out_grad = jnp.concatenate([a0[:, 768:], a1[:, 768:]], axis=1).T
    e0, e1 = both(edge_sum)
    edges = jnp.concatenate([e0, e1], axis=1)
    return layer_out, feats_grad, edges[:, 1024:], edges[:, :1024], qkv_grad, out_grad


def solution(mesh):
    fine = Mesh(mesh.devices.reshape(2, 2, 4, 4, 2), ALL)
    return jax.shard_map(
        body,
        mesh=fine,
        in_specs=(P(ALL), P(ALL), P(ALL), P(ALL), P(), P(), P(), P(), P(ALL)),
        out_specs=(P(ALL), P(ALL), P(), P(), P(), P()),
        check_vma=False,
    )
```

time: 515 us -> 257 us (0.50)
  waiting for transfers between devices: 207 us -> 49.8 us
  matrix products: 108 us -> 26.6 us
  other arithmetic: 98.5 us -> 23.8 us
  Pallas kernels: 0 us -> 70.3 us
  starting transfers between devices: 14.4 us -> 54.5 us
  local copies, waits for them, and re-layouts: 65.8 us -> 28.5 us
  between operations: 14.2 us -> 1.23 us
    psum x1 -> x0, waiting for transfers between devices: 120 us -> none  [body(): lax.psum((grad_gate_w, grad_source_w, grad_qkv_w, grad_out_w), ('blk', 'd...]
    pallas_call x0 -> x2, Pallas kernels: none -> 70.3 us  [the longest x1 43.4 us: attention(): pl.pallas_call(attn_kernel, out_shape=(sd((nq, hw), BF), sd((nq, hw), BF)...]
    dot_general x17 -> x14, matrix products: 91.5 us -> 26.6 us  [dot(): return lax.dot_general(a, b, dims, preferred_element_type=F32)]
    scatter-add x2 -> x0, other arithmetic: 47.8 us -> none  [the longest x1 38.4 us: body(): jax.ops.segment_sum(edge_terms, neighbour_slots.reshape(-1), num_segments...]
    all_gather x1 -> x0, waiting for transfers between devices: 47.7 us -> none  [body(): keys_vals = lax.all_gather(qkv[:, feat_width:], 'blk', axis=0, tiled=True)]
    gather x2 -> x0, local copies, waits for them, and re-layouts: 30.2 us -> none  [the longest x1 25.1 us: body(): edge_source = source_terms[neighbour_slots]]
    all_to_all x2 -> x6, starting transfers between devices: 14.2 us -> 42.6 us  [the longest x2 13.7 us: chip_sum(): lax.all_to_all(part.astype(BF).reshape(64, 8, w), CHIPS, 0, 0, tiled=True)]
    sub x1 -> x0, matrix products: 16.6 us -> none  [body(): raw_weights = jnp.exp(scores - row_top)]
  transfers between devices with their start and end apart: 5 -> 16, of which waited for: 4 -> 7; matrix products, arithmetic and copies ran while one was open for 29% -> 26% of each run, Pallas kernels for 0% -> 28%
where the time goes in v1:
time: 257 us; the launch traced here: 255 us
  Pallas kernels  70.3 us (27%)
  starting transfers between devices  54.5 us (21%)
  waiting for transfers between devices  49.8 us (19%)
  local copies, waits for them, and re-layouts  28.5 us (11%)
  matrix products  26.6 us (10%)
  other arithmetic  23.8 us (9%)
    pallas_call x1, Pallas kernels, attention(): pl.pallas_call(attn_kernel, out_shape=(sd((nq, hw), BF), sd((nq, hw), BF)...  43.4 us
    pallas_call x1, Pallas kernels, gnn(): pl.pallas_call(gnn_kernel, out_shape=(sd((n, 512), F32), sd((rows, 1024),...  26.9 us
    all_to_all x2, waiting for transfers between devices, chip_sum(): lax.all_to_all(part.astype(BF).reshape(64, 8, w), CHIPS, 0, 0, tiled=True)  26.8 us
    dot_general x14, matrix products, dot(): return lax.dot_general(a, b, dims, preferred_element_type=F32)  26.6 us
    all_to_all x2, starting transfers between devices, chip_sum(): lax.all_to_all(part.astype(BF).reshape(64, 8, w), CHIPS, 0, 0, tiled=True)  13.7 us
    unnamed x77, local copies, waits for them, and re-layouts  12.5 us
    all_to_all x2, starting transfers between devices, chip_sum(): return lax.all_to_all(spread, CHIPS, 0, 0, tiled=True).reshape(512, w)  11.9 us
    all_to_all x2, waiting for transfers between devices, chip_sum(): return lax.all_to_all(spread, CHIPS, 0, 0, tiled=True).reshape(512, w)  11.2 us
  transfers between devices with their start and end apart: 16, of which 7 were waited for; matrix products, arithmetic and copies ran while one was open for 26% of the time, Pallas kernels for 28%

profile of v1, /device:TPU:1, one launch (start us, length us, event | category | flops | bytes accessed | tf_op | source)
XLA Modules:
  0.0 254.7 jit_solution(16205265790247134758)
XLA Ops:
  0.6 2.1 collective-permute-start.1
  2.8 1.0 collective-permute-start
  4.5 2.9 %fusion.13 = bf16[1024,512]{1,0:T(8,128)(2,1)} fusion(bf16[512,512]{1,0:T(8,128)(2,1)} %param.9, s32[1024]{0:T(1024)S(1)} %eq.16), kind=kOutput, calls=%fused_computation.20 | convolution fusion | flops 537919488 | bytes 1576960 | tf_op jit(solution)/shard_map/dot_general | solution.py:201
  7.4 10.3 %all-to-all-start = ((bf16[32,32,512]{2,1,0:T(8,128)(2,1)}), bf16[32,32,512]{2,1,0:T(8,128)(2,1)}, u32[]{:S(2)}, u32[]{:S(2)}) async-start(bf16[32,32,512]{2,1,0:T(8,128)(2,1)} %bitcast.60), calls=%async_computation | async-start | bytes 2097152 | tf_op jit(solution)/shard_map/all_to_all | solution.py:218
  17.9 1.3 reshape.75
  19.2 0.8 constant_dynamic-update-slice_fusion.5
  20.0 3.0 %constant_dynamic-slice_fusion.1 = bf16[512,3,1,256]{3,2,1,0:T(2,128)(2,1)S(1)} fusion(bf16[512,3,2,256]{3,2,1,0:T(2,128)(2,1)} %reshape.75, s32[]{:T(128)S(6)} %select_n.44), kind=kLoop, calls=%fused_computation.90 | loop fusion | bytes 1572868 | tf_op jit(solution)/shard_map/jit(dynamic_index_in_dim)/dynamic_slice | solution.py:225
  24.7 0.9 copy.19.inv
  25.5 2.0 copy.24
  27.6 2.3 pad_maximum_fusion.2.w
  30.6 1.1 constant_dynamic-update-slice_fusion.2
  31.7 1.1 constant_dynamic-update-slice_fusion.1
  32.8 1.3 copy-done.8
  34.1 1.1 constant_dynamic-update-slice_fusion.4.cot
  36.1 2.5 pad_maximum_fusion.1.tab
  38.6 26.9 %edges.1 = (f32[512,512]{1,0:T(8,128)}, bf16[1536,1024]{1,0:T(8,128)(2,1)}, bf16[512,512]{1,0:T(8,128)(2,1)}) custom-call(s32[4096]{0:T(1024)} %reshape.72.idx, bf16[1536,512]{1,0:T(8,128)(2,1)} %pad_maximum_fusion.1.tab, bf16[512,512]{1,0:T(8,128)(2,1)} %cot.1, f32[512,1]{1,0:T(8,128)} %copy.19.inv, bf16[512,512]{1,0:T(8,128)(2,1)} %wg.1, bf16[512,1024]{1,0:T(8,128)(2,1)} %ws.1), custom_call_target="tpu_custom_call" | custom-call | flops 10000000000 | bytes 8388608 | tf_op jit(solution)/shard_map/edges/pallas_call | solution.py:191
  65.5 1.5 convolution_bitcast_fusion
  67.0 4.4 %fusion.51 = f32[512,1024]{1,0:T(8,128)S(1)} fusion(bf16[1536,1024]{1,0:T(8,128)(2,1)} %get-tuple-element.18, bf16[1024,512]{1,0:T(8,128)(2,1)} %bitcast.1, bf16[512,512]{1,0:T(8,128)(2,1)S(1)} %copy-done.3), kind=kOutput, calls=%fused_computation.94 | convolution fusion | flops 1613758464 | bytes 6815744 | tf_op jit(solution)/shard_map/dot_general | solution.py:201
  71.4 1.6 fusion.5
  73.0 2.0 collective-permute-start.7
  75.0 0.8 constant_dynamic-update-slice_fusion.xa
  75.8 43.4 %attention.1 = (bf16[1024,256]{1,0:T(8,128)(2,1)}, bf16[1024,256]{1,0:T(8,128)(2,1)}, bf16[2048,256]{1,0:T(8,128)(2,1)}, bf16[2048,256]{1,0:T(8,128)(2,1)}) custom-call(bf16[2048,512]{1,0:T(8,128)(2,1)} %constant_dynamic-update-slice_fusion.xa, bf16[1024,512]{1,0:T(8,128)(2,1)} %copy-done.24, bf16[4,256,512]{2,1,0:T(8,128)(2,1)} %pad_maximum_fusion.2.w), custom_call_target="tpu_custom_call" | custom-call | flops 25999998976 | bytes 8388608 | tf_op jit(solution)/shard_map/attention/pallas_call | solution.py:105
  119.2 1.7 fusion.21
  121.1 1.4 copy-done.9
  122.5 1.3 fusion.19
  123.8 1.5 fusion.20
  125.3 1.1 pad_maximum_fusion.4
  126.5 8.1 %all-to-all-start.4 = ((bf16[64,8,1024]{2,1,0:T(8,128)(2,1)}), bf16[64,8,1024]{2,1,0:T(8,128)(2,1)}, u32[]{:S(2)}, u32[]{:S(2)}) async-start(bf16[64,8,1024]{2,1,0:T(8,128)(2,1)} %pad_maximum_fusion.4), calls=%async_computation.4 | async-start | bytes 2097152 | tf_op jit(solution)/shard_map/all_to_all | solution.py:206
  134.5 2.8 %fusion.38 = bf16[64,8,768]{2,1,0:T(8,128)(2,1)} fusion(bf16[512,768]{1,0:T(8,128)(2,1)} %collective-permute-done.7, s32[]{:T(128)S(6)} %select_n.47, f32[512,512]{1,0:T(8,128)} %copy-done.1, f32[512,1024]{1,0:T(8,128)} %copy-done.2), kind=kLoop, calls=%fused_computation.58 | loop fusion | flops 1572864 | bytes 4718596 | tf_op jit(solution)/shard_map/reshape | solution.py:206
  137.3 14.4 %all-to-all-done.4 = bf16[64,8,1024]{2,1,0:T(8,128)(2,1)} async-done(((bf16[64,8,1024]{2,1,0:T(8,128)(2,1)}), bf16[64,8,1024]{2,1,0:T(8,128)(2,1)}, u32[]{:S(2)}, u32[]{:S(2)}) %all-to-all-start.4) | async-done | bytes 1048608 | tf_op jit(solution)/shard_map/all_to_all | solution.py:206
  151.7 5.7 %all-to-all-start.2 = ((bf16[64,8,768]{2,1,0:T(8,128)(2,1)}), bf16[64,8,768]{2,1,0:T(8,128)(2,1)}, u32[]{:S(2)}, u32[]{:S(2)}) async-start(bf16[64,8,768]{2,1,0:T(8,128)(2,1)} %fusion.38), calls=%async_computation.2 | async-start | bytes 1572864 | tf_op jit(solution)/shard_map/all_to_all | solution.py:206
  157.4 1.4 reduce_sum.35
  158.8 12.4 %all-to-all-done.2 = bf16[64,8,768]{2,1,0:T(8,128)(2,1)} async-done(((bf16[64,8,768]{2,1,0:T(8,128)(2,1)}), bf16[64,8,768]{2,1,0:T(8,128)(2,1)}, u32[]{:S(2)}, u32[]{:S(2)}) %all-to-all-start.2) | async-done | bytes 786464 | tf_op jit(solution)/shard_map/all_to_all | solution.py:206
  171.2 1.1 broadcast_in_dim.10
  172.3 5.5 %all-to-all-start.5 = ((bf16[64,8,1024]{2,1,0:T(8,128)(2,1)}), bf16[64,8,1024]{2,1,0:T(8,128)(2,1)}, u32[]{:S(2)}, u32[]{:S(2)}) async-start(bf16[64,8,1024]{2,1,0:T(8,128)(2,1)} %broadcast_in_dim.10), calls=%async_computation.5 | async-start | bytes 2097152 | tf_op jit(solution)/shard_map/all_to_all | solution.py:209
  177.9 1.2 slice_bitcast_fusion.1
  179.3 1.0 fusion.9
  180.3 0.9 slice.158
  181.9 1.3 copy-done.4
  183.3 1.3 reduce_sum.34
  184.6 8.4 %all-to-all-done.5 = bf16[64,8,1024]{2,1,0:T(8,128)(2,1)} async-done(((bf16[64,8,1024]{2,1,0:T(8,128)(2,1)}), bf16[64,8,1024]{2,1,0:T(8,128)(2,1)}, u32[]{:S(2)}, u32[]{:S(2)}) %all-to-all-start.5) | async-done | bytes 1048608 | tf_op jit(solution)/shard_map/all_to_all | solution.py:209
  193.1 0.9 broadcast_in_dim.9
  194.0 6.3 %all-to-all-start.3 = ((bf16[64,8,768]{2,1,0:T(8,128)(2,1)}), bf16[64,8,768]{2,1,0:T(8,128)(2,1)S(1)}, u32[]{:S(2)}, u32[]{:S(2)}) async-start(bf16[64,8,768]{2,1,0:T(8,128)(2,1)} %broadcast_in_dim.9), calls=%async_computation.3 | async-start | bytes 1572864 | tf_op jit(solution)/shard_map/all_to_all | solution.py:209
  200.4 1.0 pad_maximum_fusion.3
  201.4 2.6 %collective-permute-start.5 = (bf16[1024,512]{1,0:T(8,128)(2,1)}, bf16[1024,512]{1,0:T(8,128)(2,1)}, u32[]{:S(2)}, u32[]{:S(2)}) collective-permute-start(bf16[1024,512]{1,0:T(8,128)(2,1)} %pad_maximum_fusion.3), channel_id=1, source_target_pairs={{0,32},{32,0},{1,33},{33,1},{2,34},{34,2},{3,35},{35,3},{4,36},{36... | collective-permute-start | bytes 3145736 | tf_op jit(solution)/shard_map/ppermute | solution.py:238
  204.0 2.9 %fusion.34 = f32[512,512]{1,0:T(8,128)} fusion(bf16[512,1024]{1,0:T(8,128)(2,1)S(1)} %copy-done.29, bf16[1536,1024]{1,0:T(8,128)(2,1)} %get-tuple-element.18), kind=kOutput, calls=%fused_computation.54 | convolution fusion | flops 536870912 | bytes 3145728 | tf_op jit(solution)/shard_map/dot_general | solution.py:201
  207.0 2.3 fusion.14
  210.8 2.8 %all-to-all-done.3 = bf16[64,8,768]{2,1,0:T(8,128)(2,1)S(1)} async-done(((bf16[64,8,768]{2,1,0:T(8,128)(2,1)}), bf16[64,8,768]{2,1,0:T(8,128)(2,1)S(1)}, u32[]{:S(2)}, u32[]{:S(2)}) %all-to-all-start.3) | async-done | bytes 786464 | tf_op jit(solution)/shard_map/all_to_all | solution.py:209
  213.5 6.7 %all-to-all-start.1 = ((bf16[32,32,512]{2,1,0:T(8,128)(2,1)}), bf16[32,32,512]{2,1,0:T(8,128)(2,1)}, u32[]{:S(2)}, u32[]{:S(2)}) async-start(bf16[32,32,512]{2,1,0:T(8,128)(2,1)} %bitcast.11), calls=%async_computation.1 | async-start | bytes 2097152 | tf_op jit(solution)/shard_map/all_to_all | solution.py:252
  220.2 1.7 fusion.54
  221.9 1.4 fusion.42
  223.3 2.0 fusion.22
  225.8 2.1 collective-permute-start.8
  227.9 1.1 fusion.18
  229.0 8.4 %all-to-all-done.1 = bf16[32,32,512]{2,1,0:T(8,128)(2,1)} async-done(((bf16[32,32,512]{2,1,0:T(8,128)(2,1)}), bf16[32,32,512]{2,1,0:T(8,128)(2,1)}, u32[]{:S(2)}, u32[]{:S(2)}) %all-to-all-start.1) | async-done | bytes 1048608 | tf_op jit(solution)/shard_map/all_to_all | solution.py:252
  237.4 2.4 fusion.2
  239.8 2.5 collective-permute-done.6
  242.3 2.8 %fusion.30 = bf16[512,512]{1,0:T(8,128)(2,1)} fusion(f32[512,512]{1,0:T(8,128)S(1)} %fusion.2, f32[512,512]{1,0:T(8,128)S(1)} %fusion.54, f32[512,512]{1,0:T(8,128)} %fusion.34, f32[1024,512]{1,0:T(8,128)S(1)} %copy-done.17, bf16[512,512]{1,0:T(8,128)(2,1)S(1)} %collective-permute-done.6, bf16[512,512]{1,0:T(8,128)(2,1)S(1)} %copy-done.12, ...), kind=kLoop, calls=%fused_computation.44 | loop fusion | flops 2621440 | bytes 6291456 | tf_op jit(solution)/shard_map/convert_element_type | solution.py:266
  245.2 1.3 select_convert_fusion.2
  246.5 1.1 slice.110
  247.6 1.6 pad_maximum_fusion
  249.3 1.8 select_convert_fusion
  251.5 1.7 copy-done.26
  253.3 1.3 copy.22
  (98 shorter events, 8.0 us)
Async XLA Ops:
  0.6 22.4 %copy-start = (bf16[512,512]{1,0:T(8,128)(2,1)S(1)}, bf16[512,512]{1,0:T(8,128)(2,1)}, u32[]{:S(2)}) copy-start(bf16[512,512]{1,0:T(8,128)(2,1)} %param.16) | copy-start | bytes 1572868
  0.6 29.2 %collective-permute-start.1 = (bf16[512,512]{1,0:T(8,128)(2,1)}, bf16[512,512]{1,0:T(8,128)(2,1)}, u32[]{:S(2)}, u32[]{:S(2)}) collective-permute-start(bf16[512,512]{1,0:T(8,128)(2,1)} %param.9), channel_id=1, source_target_pairs={{0,64},{64,0},{1,65},{65,1},{2,66},{66,2},{3,67},{67,3},{4,68},{68... | collective-permute-start | bytes 1572872 | tf_op jit(solution)/shard_map/ppermute | solution.py:221
  2.8 27.9 %collective-permute-start = (bf16[512,512]{1,0:T(8,128)(2,1)}, bf16[512,512]{1,0:T(8,128)(2,1)}, u32[]{:S(2)}, u32[]{:S(2)}) collective-permute-start(bf16[512,512]{1,0:T(8,128)(2,1)} %param.9), channel_id=1, source_target_pairs={{0,32},{32,0},{1,33},{33,1},{2,34},{34,2},{3,35},{35,3},{4,36},{36... | collective-permute-start | bytes 1572872 | tf_op jit(solution)/shard_map/ppermute | solution.py:219
  3.7 30.4 %collective-permute-start.3 = (bf16[512,512]{1,0:T(8,128)(2,1)}, bf16[512,512]{1,0:T(8,128)(2,1)}, u32[]{:S(2)}, u32[]{:S(2)}) collective-permute-start(bf16[512,512]{1,0:T(8,128)(2,1)} %cot.1), channel_id=1, source_target_pairs={{0,32},{32,0},{1,33},{33,1},{2,34},{34,2},{3,35},{35,3},{4,36},{36... | collective-permute-start | bytes 1572872 | tf_op jit(solution)/shard_map/ppermute | solution.py:220
  4.5 13.3 %copy-start.27 = (s32[512,8]{0,1:T(8,128)S(1)}, s32[512,8]{0,1:T(8,128)}, u32[]{:S(2)}) copy-start(s32[512,8]{0,1:T(8,128)} %param.12) | copy-start | bytes 49156
  4.5 13.3 %copy-start.28 = (s32[512,8]{0,1:T(8,128)S(1)}, s32[512,8]{0,1:T(8,128)}, u32[]{:S(2)}) copy-start(s32[512,8]{0,1:T(8,128)} %param.11) | copy-start | bytes 49156
  4.5 13.3 %copy-start.15 = (bf16[512,1536]{1,0:T(8,128)(2,1)S(1)}, bf16[512,1536]{1,0:T(8,128)(2,1)}, u32[]{:S(2)}) copy-start(bf16[512,1536]{1,0:T(8,128)(2,1)} %param.15) | copy-start | bytes 4718596
  7.4 28.7 %all-to-all-start = ((bf16[32,32,512]{2,1,0:T(8,128)(2,1)}), bf16[32,32,512]{2,1,0:T(8,128)(2,1)}, u32[]{:S(2)}, u32[]{:S(2)}) async-start(bf16[32,32,512]{2,1,0:T(8,128)(2,1)} %bitcast.60), calls=%async_computation | async-start | bytes 2097152 | tf_op jit(solution)/shard_map/all_to_all | solution.py:218
  17.8 1.4 copy-start.11
  23.1 4.5 %copy-start.3 = (bf16[512,512]{1,0:T(8,128)(2,1)S(1)}, bf16[512,512]{1,0:T(8,128)(2,1)}, u32[]{:S(2)}) copy-start(bf16[512,512]{1,0:T(8,128)(2,1)} %param.9) | copy-start | bytes 1572868
  27.5 4.2 %copy-start.6 = (bf16[512,3,1,256]{0,3,1,2:T(8,128)(2,1)}, bf16[512,3,1,256]{0,3,1,2:T(8,128)(2,1)S(1)}, u32[]{:S(2)}) copy-start(bf16[512,3,1,256]{0,3,1,2:T(8,128)(2,1)S(1)} %copy.24) | copy-start | bytes 2359300
  27.6 6.6 %copy-start.23 = (bf16[1024,512]{1,0:T(8,128)(2,1)S(1)}, bf16[1024,512]{1,0:T(8,128)(2,1)}, u32[]{:S(2)}) copy-start(bf16[1024,512]{1,0:T(8,128)(2,1)} %constant_dynamic-update-slice_fusion.5) | copy-start | bytes 3145732
  29.9 45.1 %collective-permute-start.2 = (bf16[512,512]{1,0:T(8,128)(2,1)}, bf16[512,512]{1,0:T(8,128)(2,1)S(1)}, u32[]{:S(2)}, u32[]{:S(2)}) collective-permute-start(bf16[512,512]{1,0:T(8,128)(2,1)} %collective-permute-done.1), channel_id=1, source_target_pairs={{0,32},{32,0},{1,33},{33,1},{2,34},{34,2},{3,35},{35,3},{4,36},{36... | collective-permute-start | bytes 1572872 | tf_op jit(solution)/shard_map/ppermute | solution.py:222
  32.8 1.3 copy-start.8
  35.2 30.2 %copy-start.24 = (bf16[1024,512]{1,0:T(8,128)(2,1)}, bf16[1024,512]{1,0:T(8,128)(2,1)S(1)}, u32[]{:S(2)}) copy-start(bf16[1024,512]{1,0:T(8,128)(2,1)S(1)} %constant_dynamic-update-slice_fusion.4.cot) | copy-start | bytes 3145732
  67.0 4.4 %copy-start.1 = (f32[512,512]{1,0:T(8,128)}, f32[512,512]{1,0:T(8,128)S(1)}, u32[]{:S(2)}) copy-start(f32[512,512]{1,0:T(8,128)S(1)} %convolution_bitcast_fusion) | copy-start | bytes 3145732
  71.4 1.6 copy-start.2
  73.0 61.5 %collective-permute-start.7 = (bf16[512,768]{1,0:T(8,128)(2,1)}, bf16[512,768]{1,0:T(8,128)(2,1)}, u32[]{:S(2)}, u32[]{:S(2)}) collective-permute-start(bf16[512,768]{1,0:T(8,128)(2,1)} %fusion.5), channel_id=1, source_target_pairs={{0,32},{32,0},{1,33},{33,1},{2,34},{34,2},{3,35},{35,3},{4,36},{36... | collective-permute-start | bytes 2359304 | tf_op jit(solution)/shard_map/ppermute | solution.py:257
  75.8 43.4 %copy-start.25 = (bf16[1024,512]{1,0:T(8,128)(2,1)S(1)}, bf16[1024,512]{1,0:T(8,128)(2,1)}, u32[]{:S(2)}) copy-start(bf16[1024,512]{1,0:T(8,128)(2,1)} %copy-done.24) | copy-start | bytes 3145732
  119.2 1.7 copy-start.20
  119.2 1.8 copy-start.19
  120.9 1.6 copy-start.9
  122.5 1.3 copy-start.31
  126.5 25.3 %all-to-all-start.4 = ((bf16[64,8,1024]{2,1,0:T(8,128)(2,1)}), bf16[64,8,1024]{2,1,0:T(8,128)(2,1)}, u32[]{:S(2)}, u32[]{:S(2)}) async-start(bf16[64,8,1024]{2,1,0:T(8,128)(2,1)} %pad_maximum_fusion.4), calls=%async_computation.4 | async-start | bytes 2097152 | tf_op jit(solution)/shard_map/all_to_all | solution.py:206
  151.7 19.5 %all-to-all-start.2 = ((bf16[64,8,768]{2,1,0:T(8,128)(2,1)}), bf16[64,8,768]{2,1,0:T(8,128)(2,1)}, u32[]{:S(2)}, u32[]{:S(2)}) async-start(bf16[64,8,768]{2,1,0:T(8,128)(2,1)} %fusion.38), calls=%async_computation.2 | async-start | bytes 1572864 | tf_op jit(solution)/shard_map/all_to_all | solution.py:206
  172.3 20.8 %all-to-all-start.5 = ((bf16[64,8,1024]{2,1,0:T(8,128)(2,1)}), bf16[64,8,1024]{2,1,0:T(8,128)(2,1)}, u32[]{:S(2)}, u32[]{:S(2)}) async-start(bf16[64,8,1024]{2,1,0:T(8,128)(2,1)} %broadcast_in_dim.10), calls=%async_computation.5 | async-start | bytes 2097152 | tf_op jit(solution)/shard_map/all_to_all | solution.py:209
  177.8 1.3 copy-start.7
  177.8 1.4 copy-start.32
  180.2 1.7 copy-start.16
  181.9 1.3 copy-start.4
  183.2 17.1 %copy-start.13 = (bf16[512,512]{1,0:T(8,128)(2,1)S(1)}, bf16[512,512]{1,0:T(8,128)(2,1)}, u32[]{:S(2)}) copy-start(bf16[512,512]{1,0:T(8,128)(2,1)} %slice.158) | copy-start | bytes 1572868
  194.0 19.5 %all-to-all-start.3 = ((bf16[64,8,768]{2,1,0:T(8,128)(2,1)}), bf16[64,8,768]{2,1,0:T(8,128)(2,1)S(1)}, u32[]{:S(2)}, u32[]{:S(2)}) async-start(bf16[64,8,768]{2,1,0:T(8,128)(2,1)} %broadcast_in_dim.9), calls=%async_computation.3 | async-start | bytes 1572864 | tf_op jit(solution)/shard_map/all_to_all | solution.py:209
  200.4 3.6 %copy-start.29 = (bf16[512,1024]{1,0:T(8,128)(2,1)S(1)}, bf16[512,1024]{1,0:T(8,128)(2,1)}, u32[]{:S(2)}) copy-start(bf16[512,1024]{1,0:T(8,128)(2,1)} %ws.1) | copy-start | bytes 3145732
  201.4 5.5 %copy-start.30 = (bf16[1536,1024]{1,0:T(8,128)(2,1)S(1)}, bf16[1536,1024]{1,0:T(8,128)(2,1)}, u32[]{:S(2)}) copy-start(bf16[1536,1024]{1,0:T(8,128)(2,1)} %get-tuple-element.18) | copy-start | bytes 9437188
  201.4 21.9 %collective-permute-start.5 = (bf16[1024,512]{1,0:T(8,128)(2,1)}, bf16[1024,512]{1,0:T(8,128)(2,1)}, u32[]{:S(2)}, u32[]{:S(2)}) collective-permute-start(bf16[1024,512]{1,0:T(8,128)(2,1)} %pad_maximum_fusion.3), channel_id=1, source_target_pairs={{0,32},{32,0},{1,33},{33,1},{2,34},{34,2},{3,35},{35,3},{4,36},{36... | collective-permute-start | bytes 3145736 | tf_op jit(solution)/shard_map/ppermute | solution.py:238
  207.0 2.3 copy-start.21
  209.2 11.0 %copy-start.14 = (bf16[512,512]{1,0:T(8,128)(2,1)S(1)}, bf16[512,512]{1,0:T(8,128)(2,1)}, u32[]{:S(2)}) copy-start(bf16[512,512]{1,0:T(8,128)(2,1)} %get-tuple-element.19) | copy-start | bytes 1572868
  209.9 12.0 %collective-permute-start.4 = (bf16[512,256]{1,0:T(8,128)(2,1)}, bf16[512,256]{1,0:T(8,128)(2,1)}, u32[]{:S(2)}, u32[]{:S(2)}) collective-permute-start(bf16[512,256]{1,0:T(8,128)(2,1)} %slice.77), channel_id=1, source_target_pairs={{0,32},{32,0},{1,33},{33,1},{2,34},{34,2},{3,35},{35,3},{4,36},{36... | collective-permute-start | bytes 786440 | tf_op jit(solution)/shard_map/ppermute | solution.py:231
  213.5 23.9 %all-to-all-start.1 = ((bf16[32,32,512]{2,1,0:T(8,128)(2,1)}), bf16[32,32,512]{2,1,0:T(8,128)(2,1)}, u32[]{:S(2)}, u32[]{:S(2)}) async-start(bf16[32,32,512]{2,1,0:T(8,128)(2,1)} %bitcast.11), calls=%async_computation.1 | async-start | bytes 2097152 | tf_op jit(solution)/shard_map/all_to_all | solution.py:252
  220.2 3.1 %copy-start.5 = (f32[1024,512]{1,0:T(8,128)S(1)}, f32[1024,512]{1,0:T(8,128)}, u32[]{:S(2)}) copy-start(f32[1024,512]{1,0:T(8,128)} %copy-done.4) | copy-start | bytes 6291460
  221.9 6.0 %copy-start.10 = (bf16[1,256,512]{2,1,0:T(8,128)(2,1)S(1)}, bf16[1,256,512]{2,1,0:T(8,128)(2,1)}, u32[]{:S(2)}) copy-start(bf16[1,256,512]{2,1,0:T(8,128)(2,1)} %constant_dynamic-slice_fusion) | copy-start | bytes 786436
  221.9 6.0 %copy-start.18 = (f32[512,512]{1,0:T(8,128)S(1)}, f32[512,512]{1,0:T(8,128)}, u32[]{:S(2)}) copy-start(f32[512,512]{1,0:T(8,128)} %get-tuple-element.13) | copy-start | bytes 3145732
  221.9 6.0 %copy-start.22 = (bf16[1024,256]{1,0:T(8,128)(2,1)S(1)}, bf16[1024,256]{1,0:T(8,128)(2,1)}, u32[]{:S(2)}) copy-start(bf16[1024,256]{1,0:T(8,128)(2,1)} %get-tuple-element.14) | copy-start | bytes 1572868
  225.3 17.0 %collective-permute-start.6 = (bf16[512,512]{1,0:T(8,128)(2,1)}, bf16[512,512]{1,0:T(8,128)(2,1)S(1)}, u32[]{:S(2)}, u32[]{:S(2)}) collective-permute-start(bf16[512,512]{1,0:T(8,128)(2,1)} %fusion.22), channel_id=1, source_target_pairs={{0,64},{64,0},{1,65},{65,1},{2,66},{66,2},{3,67},{67,3},{4,68},{68... | collective-permute-start | bytes 1572872 | tf_op jit(solution)/shard_map/ppermute | solution.py:240
  225.8 19.3 %collective-permute-start.8 = (bf16[512,768]{1,0:T(8,128)(2,1)S(1)}, bf16[512,768]{1,0:T(8,128)(2,1)}, u32[]{:S(2)}, u32[]{:S(2)}) collective-permute-start(bf16[512,768]{1,0:T(8,128)(2,1)S(1)} %bitcast.59), channel_id=1, source_target_pairs={{0,32},{32,0},{1,33},{33,1},{2,34},{34,2},{3,35},{35,3},{4,36},{36... | collective-permute-start | bytes 2359304 | tf_op jit(solution)/shard_map/ppermute | solution.py:269
  229.0 13.3 %copy-start.12 = (bf16[512,512]{1,0:T(8,128)(2,1)S(1)}, bf16[512,512]{1,0:T(8,128)(2,1)}, u32[]{:S(2)}) copy-start(bf16[512,512]{1,0:T(8,128)(2,1)} %cot.1) | copy-start | bytes 1572868
  229.0 20.2 %collective-permute-start.9 = (bf16[512,1024]{1,0:T(8,128)(2,1)}, bf16[512,1024]{1,0:T(8,128)(2,1)}, u32[]{:S(2)}, u32[]{:S(2)}) collective-permute-start(bf16[512,1024]{1,0:T(8,128)(2,1)} %bitcast.19), channel_id=1, source_target_pairs={{0,32},{32,0},{1,33},{33,1},{2,34},{34,2},{3,35},{35,3},{4,36},{36... | collective-permute-start | bytes 3145736 | tf_op jit(solution)/shard_map/ppermute | solution.py:269
  237.4 4.9 %copy-start.17 = (f32[1024,512]{1,0:T(8,128)S(1)}, f32[1024,512]{1,0:T(8,128)}, u32[]{:S(2)}) copy-start(f32[1024,512]{1,0:T(8,128)} %copy-done.16) | copy-start | bytes 6291460
  251.5 1.7 copy-start.26

commit v2 on v0

v2 whole, which is shorter than its diff:
```python
import functools

import jax
import jax.numpy as jnp
from jax import lax
from jax.experimental import pallas as pl
from jax.experimental.pallas import tpu as pltpu
from jax.sharding import Mesh, PartitionSpec as P

BF = jnp.bfloat16
F32 = jnp.float32
NT = (((1,), (1,)), ((), ()))
NN = (((1,), (0,)), ((), ()))
TN = (((0,), (0,)), ((), ()))
LOG2E = 1.4426950408889634
CK = 256
QB = 256
NACC = 2
UN = 4
ALL = ("xl", "c", "z", "y", "xh")
CHIPS = ("xl", "z", "y", "xh")
DOM = ("z", "y", "xh")
SWAP = [(0, 1), (1, 0)]
MIB = 2**20


def dot(a, b, dims):
    return lax.dot_general(a, b, dims, preferred_element_type=F32)


def attn_kernel(pair, core, xa, cot, wqkv, wo, *rest):
    if pair:
        g_first, keep, got, d_first, joint_o, mixed_o, part_o = rest[:7]
        rest = rest[7:]
    else:
        grad_o, mixed_o, part_o = rest[:3]
        rest = rest[3:]
    k_s, v_s, kt_s, vt_s, qt_s, dmt_s, s_s, e_s, dka, dva, mt_s, dqt_s = rest
    seq = xa.shape[0]
    nq = cot.shape[0]
    chunks = [slice(c * CK, c * CK + CK) for c in range(seq // CK)]
    scale = 0.125
    c2 = scale * LOG2E
    off = pl.multiple_of(core[0] * 256 + pair * 128, 128)
    wq = wqkv[:, pl.ds(off, 128)]
    wk = wqkv[:, pl.ds(pl.multiple_of(off + 512, 128), 128)]
    wv = wqkv[:, pl.ds(pl.multiple_of(off + 1024, 128), 128)]
    wo_own = wo[pl.ds(off, 128), :]
    wkv = jnp.concatenate([wk, wv], axis=1)
    for r in chunks:
        kv = dot(xa[r, :], wkv, NN)
        k_s[r, :] = kv[:, :128].astype(BF)
        v_s[r, :] = kv[:, 128:].astype(BF)
        kvt = kv.T
        kt_s[:, r] = kvt[:128].astype(BF)
        vt_s[:, r] = kvt[128:].astype(BF)
    for r in chunks[: nq // CK]:
        qt_s[:, r] = dot(xa[r, :], wq, NN).T.astype(BF)
        dmt_s[:, r] = dot(cot[r, :], wo_own, NT).T.astype(BF)
    row = lax.broadcasted_iota(jnp.int32, (128, QB), 0)
    heads = [slice(h * 64, h * 64 + 64) for h in range(2)]
    lanes = [slice(h * QB, h * QB + QB) for h in range(2)]

    def split_heads(x):
        zero = jnp.zeros_like(x)
        return jnp.concatenate([jnp.where(row < 64, x, zero), jnp.where(row >= 64, x, zero)], axis=1)

    kept = {}

    def forward(b):
        qc = slice(b * QB, b * QB + QB)
        u = b % 2
        queries = split_heads(qt_s[:, qc])
        top = jnp.full((8, 2 * QB), -jnp.inf, F32)
        for r in chunks:
            s = dot(k_s[r, :], queries, NN)
            s_s[u, r, :] = s
            top = jnp.maximum(top, jnp.max(s.reshape(CK // 8, 8, 2 * QB), axis=0))
            yield
        top = jnp.max(top, axis=0, keepdims=True) * c2
        total = jnp.zeros((8, 2 * QB), F32)
        for r in chunks:
            e = jnp.exp2(s_s[u, r, :] * c2 - top)
            total = total + jnp.sum(e.reshape(CK // 8, 8, 2 * QB), axis=0)
            s_s[u, r, :] = e
            yield
        inv = 1.0 / jnp.sum(total, axis=0, keepdims=True)
        acc = [jnp.zeros((64, QB), F32) for _ in heads]
        for r in chunks:
            half = (s_s[u, r, :] * inv).astype(BF)
            e_s[u, r, :] = half
            for h in range(2):
                acc[h] = acc[h] + dot(vt_s[heads[h], r], half[:, lanes[h]], NN)
            if r != chunks[-1]:
                yield
        delta = []
        for h in range(2):
            mixed = acc[h].astype(BF)
            mt_s[heads[h], qc] = mixed
            delta.append(jnp.sum(dmt_s[heads[h], qc].astype(F32) * mixed.astype(F32), axis=0, keepdims=True))
        kept[b] = (jnp.concatenate(delta, axis=1), inv * scale)
        yield

    def backward(b):
        qc = slice(b * QB, b * QB + QB)
        u = b % 2
        delta, weight = kept[b]
        d_mixed = split_heads(dmt_s[:, qc])
        acc = [jnp.zeros((64, QB), F32) for _ in heads]
        for r in chunks:
            dp = dot(v_s[r, :], d_mixed, NN)
            for h in range(2):
                t = dot(dmt_s[heads[h], qc], e_s[u, r, lanes[h]], NT)
                dva[heads[h], r] = t if b == 0 else dva[heads[h], r] + t
            yield
            ds = ((dp - delta) * (s_s[u, r, :] * weight)).astype(BF)
            yield
            for h in range(2):
                t = dot(qt_s[heads[h], qc], ds[:, lanes[h]], NT)
                dka[heads[h], r] = t if b == 0 else dka[heads[h], r] + t
                acc[h] = acc[h] + dot(kt_s[heads[h], r], ds[:, lanes[h]], NN)
            yield
        for h in range(2):
            dqt_s[heads[h], qc] = acc[h]

    for _ in forward(0):
        pass
    blocks = nq // QB
    for b in range(blocks):
        coming = forward(b + 1) if b + 1 < blocks else iter(())
        for _ in backward(b):
            next(coming, None)
        for _ in coming:
            pass
    dqt = dqt_s[...].astype(BF)
    dkt = dka[...].astype(BF)
    dvt = dva[...].astype(BF)
    grads = (
        dot(dqt, xa[:nq, :], NN),
        dot(dkt, xa[...], NN),
        dot(dvt, xa[...], NN),
        dot(mt_s[...], cot[...], NN),
    )
    for i, g in enumerate(grads):
        if pair:
            joint_o[i * 128 : i * 128 + 128, 512:1024] = g.astype(BF)
        else:
            grad_o[i * 128 : i * 128 + 128, :] = g.astype(BF)
    if pair:
        joint_o[:, :512] = g_first[...]
        joint_o[:, 1024:] = (keep[...].astype(F32) + got[...].astype(F32)).astype(BF)
    mixed_o[...] = mt_s[...].T
    dkv = jnp.concatenate([dka[...], dva[...]], axis=0).T.astype(BF)
    dq = dqt_s[...].T.astype(BF)
    for r in chunks:
        part = dot(dkv[r, :], wkv, NT)
        if r.start < nq:
            part = part + dot(dq[r, :], wq, NT)
        if pair:
            part = part + d_first[r, :].astype(F32)
        part_o[r, :] = part.astype(BF)


def attention(pair, core, xa, cot, wqkv, wo, *first):
    seq, d = xa.shape
    nq = cot.shape[0]
    hw = 128
    sd = jax.ShapeDtypeStruct
    V = pltpu.VMEM
    vm = pl.BlockSpec(memory_space=pltpu.VMEM)
    return pl.pallas_call(
        functools.partial(attn_kernel, pair),
        out_shape=(sd((512, 1792 if pair else 512), BF), sd((nq, hw), BF), sd((seq, d), BF)),
        in_specs=[pl.BlockSpec(memory_space=pltpu.SMEM)] + [vm] * (4 + len(first)),
        out_specs=(vm,) * 3,
        scratch_shapes=[V((seq, hw), BF)] * 2
        + [V((hw, seq), BF)] * 2
        + [V((hw, nq), BF)] * 2
        + [V((2, seq, 2 * QB), F32), V((2, seq, 2 * QB), BF)]
        + [V((hw, seq), F32)] * 2
        + [V((hw, nq), BF), V((hw, nq), F32)],
        compiler_params=pltpu.CompilerParams(vmem_limit_bytes=40 * MIB),
        cost_estimate=pl.CostEstimate(flops=16 * 10**9, bytes_accessed=8 * MIB, transcendentals=4 * MIB),
        name="attention",
    )(core, xa, cot, wqkv, wo, *first)


def edges_kernel(core, idx, x, inc, cot, mask, wg, ws, base_o, local_o, remote_o, keep_o, give_o, a_s, b_s, gt_s, up_s, dsrc, dgate, e_s, *accs):
    n, d = x.shape
    rows = n + inc.shape[0]
    R = 128

    def fill(src, first):
        def step(i, _):
            base = pl.multiple_of(i * R, R)
            at = (base + first) * 8
            t = dot(src[pl.ds(base, R), :], ws[...], NN)
            for c in range(4):
                g = t[:, c * 128 : c * 128 + 128] * 0.5
                v = t[:, 512 + c * 128 : 512 + c * 128 + 128]
                a_s[pl.ds(at + c, R, stride=8), :] = g
                a_s[pl.ds(at + 4 + c, R, stride=8), :] = g
                b_s[pl.ds(at + c, R, stride=8), :] = v
                b_s[pl.ds(at + 4 + c, R, stride=8), :] = jnp.full_like(v, 2.0)
            for acc in accs:
                acc[pl.ds(pl.multiple_of(at, 8), R * 8), :] = jnp.zeros((R * 8, 128), F32)
            return 0

        lax.fori_loop(0, src.shape[0] // R, step, 0)

    fill(x, 0)
    fill(inc, n)
    for ref in (a_s, b_s, *accs):
        ref[pl.ds(rows * 8, 8), :] = jnp.zeros((8, 128), F32)

    def inverse(base):
        count = jnp.sum(mask[pl.ds(base, R), :].astype(F32), axis=1, keepdims=True)
        return 1.0 / jnp.maximum(count, 1.0)

    def fill_nodes(i, _):
        base = pl.multiple_of(i * R, R)
        t = dot(x[pl.ds(base, R), :], wg[...], NN) * 0.5
        u = cot[pl.ds(base, R), :].astype(F32) * (inverse(base) * 0.25)
        for c in range(4):
            cs = slice(c * 128, c * 128 + 128)
            for h in (0, 4):
                gt_s[pl.ds(base * 8 + h + c, R, stride=8), :] = t[:, cs]
                up_s[pl.ds(base * 8 + h + c, R, stride=8), :] = u[:, cs]
        return 0

    lax.fori_loop(0, n // R, fill_nodes, 0)
    gate_half = jnp.where(lax.broadcasted_iota(jnp.int32, (8, 128), 0) < 4, 1.0, 0.0).astype(F32)

    def node(i):
        at = pl.multiple_of(i * 8, 8)
        gt = gt_s[pl.ds(at, 8), :]
        up = up_s[pl.ds(at, 8), :]
        ps = []
        ds = []
        for k in range(8):
            j = pl.multiple_of(idx[i * 8 + k], 8)
            t = jnp.tanh(a_s[pl.ds(j, 8), :] + gt)
            p = (1.0 + t) * b_s[pl.ds(j, 8), :]
            g = p * (1.0 - t * gate_half) * up
            ps.append(p)
            ds.append(g)
            acc = accs[k % NACC]
            acc[pl.ds(j, 8), :] = acc[pl.ds(j, 8), :] + g
        while len(ps) > 1:
            ps = [a + b for a, b in zip(ps[::2], ps[1::2])]
            ds = [a + b for a, b in zip(ds[::2], ds[1::2])]
        gt_s[pl.ds(at, 8), :] = ps[0]
        up_s[pl.ds(at, 8), :] = ds[0]

    def nodes(i, _):
        for u in range(UN):
            node(i * UN + u)
        return 0

    lax.fori_loop(0, n // UN, nodes, 0)

    def read(base):
        for c in range(8):
            v = accs[0][pl.ds(base * 8 + c, R, stride=8), :]
            for acc in accs[1:]:
                v = v + acc[pl.ds(base * 8 + c, R, stride=8), :]
            dsrc[pl.ds(base, R), c * 128 : c * 128 + 128] = v.astype(BF)

    def read_local(i, _):
        base = pl.multiple_of(i * R, R)
        read(base)
        inv = inverse(base) * 0.5
        for c in range(4):
            cs = slice(c * 128, c * 128 + 128)
            base_o[pl.ds(base, R), cs] = x[pl.ds(base, R), cs].astype(F32) + gt_s[pl.ds(base * 8 + c, R, stride=8), :] * inv
            dgate[pl.ds(base, R), cs] = up_s[pl.ds(base * 8 + c, R, stride=8), :].astype(BF)
        local_o[pl.ds(base, R), :] = (
            cot[pl.ds(base, R), :].astype(F32)
            + dot(dsrc[pl.ds(base, R), :], ws[...], NT)
            + dot(dgate[pl.ds(base, R), :], wg[...], NT)
        )
        return 0

    lax.fori_loop(0, n // R, read_local, 0)

    def read_remote(i, _):
        base = pl.multiple_of(i * R, R)
        read(base + n)
        remote_o[pl.ds(base, R), :] = dot(dsrc[pl.ds(base + n, R), :], ws[...], NT).astype(BF)
        return 0

    lax.fori_loop(0, inc.shape[0] // R, read_remote, 0)
    xt = x[...].T
    it = inc[...].T
    for c in range(4):
        cs = slice(c * 256, c * 256 + 256)
        e_s[:, cs] = dot(xt, dsrc[:n, cs], NN) + dot(it, dsrc[n:, cs], NN)
    e_s[:, 1024:] = dot(xt, dgate[...], NN)
    half = e_s.shape[1] // 2
    keep_o[...] = e_s[:, pl.ds(pl.multiple_of(core[0] * half, 128), half)]
    give_o[...] = e_s[:, pl.ds(pl.multiple_of((1 - core[0]) * half, 128), half)].astype(BF)


def edges(core, idx, x, inc, cot, mask, wg, ws):
    n, d = x.shape
    rows = n + inc.shape[0]
    sd = jax.ShapeDtypeStruct
    V = pltpu.VMEM
    vm = pl.BlockSpec(memory_space=pltpu.VMEM)
    sm = pl.BlockSpec(memory_space=pltpu.SMEM)
    table = V(((rows + 1) * 8, 128), F32)
    per_node = V((n * 8, 128), F32)
    return pl.pallas_call(
        edges_kernel,
        out_shape=(sd((n, d), F32), sd((n, d), F32), sd(inc.shape, BF), sd((d, 768), F32), sd((d, 768), BF)),
        in_specs=[sm, sm] + [vm] * 6,
        out_specs=(vm,) * 5,
        scratch_shapes=[table, table, per_node, per_node, V((rows, 2 * d), BF), V((n, d), BF), V((d, 3 * d), F32)] + [table] * NACC,
        compiler_params=pltpu.CompilerParams(vmem_limit_bytes=52 * MIB),
        cost_estimate=pl.CostEstimate(flops=20 * 10**9, bytes_accessed=8 * MIB, transcendentals=4 * MIB),
        name="edges",
    )(core, idx, x, inc, cot, mask, wg, ws)


def spread_kernel(got, out):
    total = jnp.sum(got[...].astype(F32), axis=0).astype(BF)
    out[...] = jnp.broadcast_to(total[None], out.shape)


def sum_spread(got):
    vm = pl.BlockSpec(memory_space=pltpu.VMEM)
    return pl.pallas_call(
        spread_kernel,
        out_shape=jax.ShapeDtypeStruct(got.shape, BF),
        in_specs=[vm],
        out_specs=vm,
        cost_estimate=pl.CostEstimate(flops=got.size, bytes_accessed=got.size * 4, transcendentals=0),
        name="sum_spread",
    )(got)


def place_kernel(core, own, other, gate, source, qkv, out):
    for c in range(2):

        @pl.when(core[0] == c)
        def _():
            for mine, src in ((c, own), (1 - c, other)):
                for p in range(2):
                    cols = slice(p * 512, p * 512 + 512)
                    at = mine * 256 + p * 128
                    for i in range(3):
                        qkv[:, i * 512 + at : i * 512 + at + 128] = src[i * 128 : i * 128 + 128, cols].astype(F32).T
                    out[at : at + 128, :] = src[384:, cols].astype(F32)
                if mine == 0:
                    source[:, :768] = src[:, 1024:].astype(F32)
                else:
                    source[:, 768:] = src[:, 1024:1280].astype(F32)
                    gate[...] = src[:, 1280:].astype(F32)


def place(core, own, other):
    vm = pl.BlockSpec(memory_space=pltpu.VMEM)
    sd = jax.ShapeDtypeStruct
    return pl.pallas_call(
        place_kernel,
        out_shape=(sd((512, 512), F32), sd((512, 1024), F32), sd((512, 1536), F32), sd((512, 512), F32)),
        in_specs=[pl.BlockSpec(memory_space=pltpu.SMEM), vm, vm],
        out_specs=(vm,) * 4,
        name="place",
    )(core, own, other)


def swap(a, axis):
    return lax.ppermute(a, axis, SWAP)


def chips(a):
    return lax.all_to_all(a, CHIPS, 0, 0, tiled=True)


def domains(a):
    return lax.all_to_all(a.reshape(32, 32, -1), DOM, 0, 0, tiled=True).reshape(1024, -1)


def body(x, send_rows, slots, mask, wg, ws, wqkv, wo, cot):
    core = lax.axis_index("c").reshape(1)
    n, d = x.shape
    x_far = swap(x, "xl")
    x_sib = swap(x, "c")
    cot_sib = swap(cot, "c")
    rows = send_rows.reshape(-1)
    pick = (rows[:, None] == lax.broadcasted_iota(jnp.int32, (rows.shape[0], n), 1)).astype(BF)
    incoming = domains(dot(pick, x, NN).astype(BF))
    x_far_sib = swap(x_far, "c")
    xa = jnp.concatenate([x, x_sib, x_far, x_far_sib], axis=0)
    ca = jnp.concatenate([cot, cot_sib], axis=0)
    grad_first, mixed_first, part_first = attention(0, core, xa, ca, wqkv, wo)
    idx = (jnp.where(mask > 0, slots, 3 * n) * 8).reshape(-1)
    incoming, grad_first = lax.optimization_barrier((incoming, grad_first))
    base, local, remote, keep, give = edges(core, idx, x, incoming, cot, mask, wg, ws)
    returned = domains(remote)
    got = swap(give, "c")
    joint, mixed_second, part = attention(1, core, xa, ca, wqkv, wo, grad_first, keep, got, part_first)
    joint, returned = lax.optimization_barrier((joint, returned))
    parts = chips(joint.reshape(64, 8, -1))
    mixed = jnp.concatenate([mixed_first, mixed_second], axis=1)
    mixed_sib = swap(mixed[n:], "c")
    wo2 = wo.reshape(2, 256, d)
    wo_own = lax.dynamic_index_in_dim(wo2, core[0], 0, keepdims=False)
    wo_sib = lax.dynamic_index_in_dim(wo2, 1 - core[0], 0, keepdims=False)
    attended = dot(mixed[:n], wo_own, NN) + dot(mixed_sib, wo_sib, NN)
    layer_out = (base + attended).astype(BF)
    part4 = part.reshape(2, 2, n, d)
    from_sib = swap(part4[:, 1], "c").astype(F32)
    from_far = swap((part4[1, 0].astype(F32) + from_sib[1]).astype(BF), "xl")
    feats_grad = (
        local + part4[0, 0].astype(F32) + from_sib[0] + from_far.astype(F32) + dot(pick, returned, TN)
    ).astype(BF)
    own = chips(sum_spread(parts)).reshape(512, -1)
    own, layer_out, feats_grad = lax.optimization_barrier((own, layer_out, feats_grad))
    gate_grad, source_grad, qkv_grad, out_grad = place(core, own, swap(own, "c"))
    return layer_out, feats_grad, gate_grad, source_grad, qkv_grad, out_grad


def solution(mesh):
    fine = Mesh(mesh.devices.reshape(2, 2, 4, 4, 2), ALL)
    return jax.shard_map(
        body,
        mesh=fine,
        in_specs=(P(ALL), P(ALL), P(ALL), P(ALL), P(), P(), P(), P(), P(ALL)),
        out_specs=(P(ALL), P(ALL), P(), P(), P(), P()),
        check_vma=False,
    )
```

time: 515 us -> 210 us (0.41)
  waiting for transfers between devices: 207 us -> 45.9 us
  matrix products: 108 us -> 6.46 us
  other arithmetic: 98.5 us -> 2.94 us
  Pallas kernels: 0 us -> 72.2 us
  local copies, waits for them, and re-layouts: 65.8 us -> 28 us
  starting transfers between devices: 14.4 us -> 49.3 us
  between operations: 14.2 us -> 1.11 us
    psum x1 -> x0, waiting for transfers between devices: 120 us -> none  [body(): lax.psum((grad_gate_w, grad_source_w, grad_qkv_w, grad_out_w), ('blk', 'd...]
    dot_general x17 -> x4, matrix products: 91.5 us -> 6.46 us  [dot(): return lax.dot_general(a, b, dims, preferred_element_type=F32)]
    pallas_call x0 -> x5, Pallas kernels: none -> 72.2 us  [the longest x2 32.4 us: attention(): pl.pallas_call(functools.partial(attn_kernel, pair), out_shape=(sd((512,...]
    scatter-add x2 -> x0, other arithmetic: 47.8 us -> none  [the longest x1 38.4 us: body(): jax.ops.segment_sum(edge_terms, neighbour_slots.reshape(-1), num_segments...]
    all_gather x1 -> x0, waiting for transfers between devices: 47.7 us -> none  [body(): keys_vals = lax.all_gather(qkv[:, feat_width:], 'blk', axis=0, tiled=True)]
    gather x2 -> x0, local copies, waits for them, and re-layouts: 30.2 us -> none  [the longest x1 25.1 us: body(): edge_source = source_terms[neighbour_slots]]
    ppermute x0 -> x9, waiting for transfers between devices: none -> 23.4 us  [swap(): return lax.ppermute(a, axis, SWAP)]
    all_to_all x2 -> x4, starting transfers between devices: 14.2 us -> 35.9 us  [the longest x2 20.4 us: domains(): lax.all_to_all(a.reshape(32, 32, -1), DOM, 0, 0, tiled=True)]
  transfers between devices with their start and end apart: 5 -> 13, of which waited for: 4 -> 3; matrix products, arithmetic and copies ran while one was open for 29% -> 10% of each run, Pallas kernels for 0% -> 17%
where the time goes in v2:
time: 210 us; the launch traced here: 206 us
  Pallas kernels  72.2 us (34%)
  starting transfers between devices  49.3 us (23%)
  waiting for transfers between devices  45.9 us (22%)
  local copies, waits for them, and re-layouts  28 us (13%)
  matrix products  6.46 us (3%)
  other arithmetic  2.94 us (1%)
    pallas_call x2, Pallas kernels, attention(): pl.pallas_call(functools.partial(attn_kernel, pair), out_shape=(sd((512,...  32.4 us
    pallas_call x1, Pallas kernels, edges(): pl.pallas_call(edges_kernel, out_shape=(sd((n, d), F32), sd((n, d), F32),...  31 us
    ppermute x9, waiting for transfers between devices, swap(): return lax.ppermute(a, axis, SWAP)  23.4 us
    unnamed x52, local copies, waits for them, and re-layouts  22.5 us
    all_to_all x2, waiting for transfers between devices, chips(): return lax.all_to_all(a, CHIPS, 0, 0, tiled=True)  22.4 us
    all_to_all x2, starting transfers between devices, domains(): lax.all_to_all(a.reshape(32, 32, -1), DOM, 0, 0, tiled=True)  20.4 us
    all_to_all x2, starting transfers between devices, chips(): return lax.all_to_all(a, CHIPS, 0, 0, tiled=True)  15.5 us
    ppermute x9, starting transfers between devices, swap(): return lax.ppermute(a, axis, SWAP)  13.3 us
  transfers between devices with their start and end apart: 13, of which 3 were waited for; matrix products, arithmetic and copies ran while one was open for 10% of the time, Pallas kernels for 17%

profile of v2, /device:TPU:1, one launch (start us, length us, event | category | flops | bytes accessed | tf_op | source)
XLA Modules:
  0.0 205.9 jit_solution(18064687634232057020)
XLA Ops:
  0.6 2.1 %collective-permute-start.1 = (bf16[512,512]{1,0:T(8,128)(2,1)}, bf16[512,512]{1,0:T(8,128)(2,1)}, u32[]{:S(2)}, u32[]{:S(2)}) collective-permute-start(bf16[512,512]{1,0:T(8,128)(2,1)} %x.1), channel_id=1, source_target_pairs={{0,64},{64,0},{1,65},{65,1},{2,66},{66,2},{3,67},{67,3},{4,68},{68... | collective-permute-start | bytes 1572872 | tf_op jit(solution)/shard_map/ppermute | solution.py:374
  2.8 1.0 collective-permute-start
  3.7 0.0 collective-permute-start.3
  3.7 0.8 eq.10
  4.5 2.8 %fusion.2 = bf16[1024,512]{1,0:T(8,128)(2,1)} fusion(bf16[512,512]{1,0:T(8,128)(2,1)} %x.1, s32[1024]{0:T(1024)S(1)} %eq.10), kind=kOutput, calls=%fused_computation.3 | convolution fusion | flops 537919488 | bytes 1576960 | tf_op jit(solution)/shard_map/dot_general | solution.py:28
  7.3 10.5 %all-to-all-start = ((bf16[32,32,512]{2,1,0:T(8,128)(2,1)}), bf16[32,32,512]{2,1,0:T(8,128)(2,1)}, u32[]{:S(2)}, u32[]{:S(2)}) async-start(bf16[32,32,512]{2,1,0:T(8,128)(2,1)} %bitcast.1), calls=%async_computation | async-start | bytes 2097152 | tf_op jit(solution)/shard_map/all_to_all | solution.py:382
  17.9 0.0 collective-permute-done.1
  17.9 1.0 collective-permute-start.2
  18.9 0.8 constant_dynamic-update-slice_fusion.3
  19.8 0.1 copy.18.mask
  19.9 0.1 copy.17
  20.0 0.2 reshape.50.idx
  20.2 0.0 copy-start.3
  20.2 0.0 copy-start.8
  20.2 0.0 collective-permute-done
  20.3 2.0 constant_dynamic-update-slice_fusion.2
  22.3 1.9 constant_dynamic-update-slice_fusion.1
  24.1 1.1 constant_dynamic-update-slice_fusion.4.cot
  25.2 0.0 collective-permute-done.2
  25.2 2.2 %constant_dynamic-update-slice_fusion.xa = bf16[2048,512]{1,0:T(8,128)(2,1)} fusion(bf16[2048,512]{1,0:T(8,128)(2,1)} %constant_dynamic-update-slice_fusion.1, bf16[512,512]{1,0:T(8,128)(2,1)} %collective-permute-done.2), kind=kLoop, calls=%fused_computation.27 | loop fusion | bytes 1048576 | tf_op jit(solution)/shard_map/concatenate | solution.py:395
  27.5 1.6 copy-done.6
  29.1 16.0 %attention.2 = (bf16[512,512]{1,0:T(8,128)(2,1)S(1)}, bf16[1024,128]{1,0:T(8,128)(2,1)S(1)}, bf16[2048,512]{1,0:T(8,128)(2,1)S(1)}) custom-call(s32[1]{0:T(128)} %bitcast.core, bf16[2048,512]{1,0:T(8,128)(2,1)S(1)} %copy-done.6, bf16[1024,512]{1,0:T(8,128)(2,1)S(1)} %constant_dynamic-update-slice_fusion.4.cot, bf16[512,1536]{1,0:T(8,128)(2,1)S(1)} %copy-done.8, ...), custom_call_target="tpu_custom_call" | custom-call | flops 16000000000 | bytes 8388608 | tf_op jit(solution)/shard_map/attention/pallas_call | solution.py:171
  45.1 0.0 copy-start.13
  45.2 1.3 copy-done.13
  46.5 0.8 copy-done.16
  47.3 0.0 all-to-all-done
  47.3 1.0 copy-done.12
  48.3 31.0 %edges.1 = (f32[512,512]{1,0:T(8,128)}, f32[512,512]{1,0:T(8,128)}, bf16[1024,512]{1,0:T(8,128)(2,1)}, f32[512,768]{1,0:T(8,128)}, bf16[512,768]{1,0:T(8,128)(2,1)}) custom-call(s32[1]{0:T(128)} %bitcast.core, s32[4096]{0:T(1024)S(1)} %reshape.50.idx, bf16[512,512]{1,0:T(8,128)(2,1)S(1)} %copy-done.1, bf16[1024,512]{1,0:T(8,128)(2,1)} %bitcast.2.inc, ...), custom_call_target="tpu_custom_call" | custom-call | flops 20000000000 | bytes 8388608 | tf_op jit(solution)/shard_map/edges/pallas_call | solution.py:313
  79.3 0.0 collective-permute-start.4
  79.3 9.9 %all-to-all-start.1 = ((bf16[32,32,512]{2,1,0:T(8,128)(2,1)}), bf16[32,32,512]{2,1,0:T(8,128)(2,1)}, u32[]{:S(2)}, u32[]{:S(2)}) async-start(bf16[32,32,512]{2,1,0:T(8,128)(2,1)} %bitcast.54), calls=%async_computation.1 | async-start | bytes 2097152 | tf_op jit(solution)/shard_map/all_to_all | solution.py:382
  89.2 0.9 copy-done.10
  90.1 1.2 copy-done.5
  91.4 1.6 copy-done.7
  93.0 1.4 copy-done.9
  94.4 1.1 copy-done.11
  95.5 1.6 copy-done.14
  97.1 1.4 copy-done.15
  98.5 1.0 copy-done.17
  99.5 16.3 %attention.3 = (bf16[512,1792]{1,0:T(8,128)(2,1)S(1)}, bf16[1024,128]{1,0:T(8,128)(2,1)S(1)}, bf16[2048,512]{1,0:T(8,128)(2,1)S(1)}) custom-call(s32[1]{0:T(128)} %bitcast.core, bf16[2048,512]{1,0:T(8,128)(2,1)S(1)} %copy-done.7, bf16[1024,512]{1,0:T(8,128)(2,1)S(1)} %copy-done.5, bf16[512,1536]{1,0:T(8,128)(2,1)S(1)} %copy-done.9, ...), custom_call_target="tpu_custom_call" | custom-call | flops 16000000000 | bytes 8388608 | tf_op jit(solution)/shard_map/attention/pallas_call | solution.py:171
  115.9 0.0 copy-start
  115.9 1.2 copy-done
  117.1 0.0 all-to-all-done.1
  117.1 10.0 %all-to-all-start.2 = ((bf16[64,8,1792]{2,1,0:T(8,128)(2,1)}), bf16[64,8,1792]{2,1,0:T(8,128)(2,1)}, u32[]{:S(2)}, u32[]{:S(2)}) async-start(bf16[64,8,1792]{2,1,0:T(8,128)(2,1)} %bitcast.51), calls=%async_computation.2 | async-start | bytes 3670016 | tf_op jit(solution)/shard_map/all_to_all | solution.py:378
  127.1 1.0 slice_bitcast_fusion.2
  128.2 1.3 collective-permute-start.6
  129.4 22.4 %all-to-all-done.2.got = bf16[64,8,1792]{2,1,0:T(8,128)(2,1)} async-done(((bf16[64,8,1792]{2,1,0:T(8,128)(2,1)}), bf16[64,8,1792]{2,1,0:T(8,128)(2,1)}, u32[]{:S(2)}, u32[]{:S(2)}) %all-to-all-start.2) | async-done | bytes 1835040 | tf_op jit(solution)/shard_map/all_to_all | solution.py:378
  151.8 3.0 %sum_spread.1 = bf16[64,8,1792]{2,1,0:T(8,128)(2,1)} custom-call(bf16[64,8,1792]{2,1,0:T(8,128)(2,1)} %all-to-all-done.2.got), custom_call_target="tpu_custom_call" | custom-call | flops 917504 | bytes 3670016 | tf_op jit(solution)/shard_map/sum_spread/pallas_call | solution.py:332
  154.9 5.5 %all-to-all-start.3 = ((bf16[64,8,1792]{2,1,0:T(8,128)(2,1)}), bf16[64,8,1792]{2,1,0:T(8,128)(2,1)}, u32[]{:S(2)}, u32[]{:S(2)}) async-start(bf16[64,8,1792]{2,1,0:T(8,128)(2,1)} %sum_spread.1), calls=%async_computation.3 | async-start | bytes 3670016 | tf_op jit(solution)/shard_map/all_to_all | solution.py:378
  160.5 0.1 constant_dynamic-update-slice_fusion.6
  160.6 2.9 %collective-permute-start.5 = (bf16[512,256]{1,0:T(8,128)(2,1)S(1)}, bf16[512,256]{1,0:T(8,128)(2,1)S(1)}, u32[]{:S(2)}, u32[]{:S(2)}) collective-permute-start(bf16[512,256]{1,0:T(8,128)(2,1)S(1)} %slice.29), channel_id=1, source_target_pairs={{0,32},{32,0},{1,33},{33,1},{2,34},{34,2},{3,35},{35,3},{4,36},{36... | collective-permute-start | bytes 786440 | tf_op jit(solution)/shard_map/ppermute | solution.py:374
  163.4 2.2 %fusion = f32[512,512]{1,0:T(8,128)S(1)} fusion(bf16[1024,512]{1,0:T(8,128)(2,1)} %bitcast.4, s32[1024]{0:T(1024)S(1)} %eq.10), kind=kOutput, calls=%fused_computation.1 | convolution fusion | flops 537395200 | bytes 2101248 | tf_op jit(solution)/shard_map/dot_general | solution.py:28
  165.7 0.0 collective-permute-done.6
  165.7 1.5 convert_element_type.35
  167.2 0.0 copy-start.19
  167.2 0.2 fusion.6
  167.4 1.4 collective-permute-start.7
  168.8 0.3 fusion.14
  169.1 1.1 fusion.4
  170.2 19.8 %collective-permute-done.7 = bf16[512,512]{1,0:T(8,128)(2,1)S(1)} collective-permute-done((bf16[512,512]{1,0:T(8,128)(2,1)S(1)}, bf16[512,512]{1,0:T(8,128)(2,1)S(1)}, u32[]{:S(2)}, u32[]{:S(2)}) %collective-permute-start.7) | collective-permute-done | bytes 524320 | tf_op jit(solution)/shard_map/ppermute | solution.py:374
  190.0 1.3 fusion.10
  191.3 3.7 %collective-permute-start.8 = (bf16[512,1792]{1,0:T(8,128)(2,1)}, bf16[512,1792]{1,0:T(8,128)(2,1)S(1)}, u32[]{:S(2)}, u32[]{:S(2)}) collective-permute-start(bf16[512,1792]{1,0:T(8,128)(2,1)} %bitcast.6.own), channel_id=1, source_target_pairs={{0,32},{32,0},{1,33},{33,1},{2,34},{34,2},{3,35},{35,3},{4,36},{36... | collective-permute-start | bytes 5505032 | tf_op jit(solution)/shard_map/ppermute | solution.py:374
  195.0 3.6 %collective-permute-done.8.other = bf16[512,1792]{1,0:T(8,128)(2,1)S(1)} collective-permute-done((bf16[512,1792]{1,0:T(8,128)(2,1)}, bf16[512,1792]{1,0:T(8,128)(2,1)S(1)}, u32[]{:S(2)}, u32[]{:S(2)}) %collective-permute-start.8) | collective-permute-done | bytes 1835040 | tf_op jit(solution)/shard_map/ppermute | solution.py:374
  198.6 1.3 copy-done.18
  199.8 5.9 %place.1 = (f32[512,512]{1,0:T(8,128)}, f32[512,1024]{1,0:T(8,128)}, f32[512,1536]{1,0:T(8,128)}, f32[512,512]{1,0:T(8,128)}) custom-call(s32[1]{0:T(128)} %bitcast.core, bf16[512,1792]{1,0:T(8,128)(2,1)} %bitcast.6.own, bf16[512,1792]{1,0:T(8,128)(2,1)} %copy-done.18), custom_call_target="tpu_custom_call" | custom-call | tf_op jit(solution)/shard_map/place/pallas_call | solution.py:364
  (35 shorter events, 0.2 us)
Async XLA Ops:
  0.6 17.2 %collective-permute-start.1 = (bf16[512,512]{1,0:T(8,128)(2,1)}, bf16[512,512]{1,0:T(8,128)(2,1)}, u32[]{:S(2)}, u32[]{:S(2)}) collective-permute-start(bf16[512,512]{1,0:T(8,128)(2,1)} %x.1), channel_id=1, source_target_pairs={{0,64},{64,0},{1,65},{65,1},{2,66},{66,2},{3,67},{67,3},{4,68},{68... | collective-permute-start | bytes 1572872 | tf_op jit(solution)/shard_map/ppermute | solution.py:374
  2.8 17.5 %collective-permute-start = (bf16[512,512]{1,0:T(8,128)(2,1)}, bf16[512,512]{1,0:T(8,128)(2,1)}, u32[]{:S(2)}, u32[]{:S(2)}) collective-permute-start(bf16[512,512]{1,0:T(8,128)(2,1)} %x.1), channel_id=1, source_target_pairs={{0,32},{32,0},{1,33},{33,1},{2,34},{34,2},{3,35},{35,3},{4,36},{36... | collective-permute-start | bytes 1572872 | tf_op jit(solution)/shard_map/ppermute | solution.py:374
  3.7 20.4 %collective-permute-start.3 = (bf16[512,512]{1,0:T(8,128)(2,1)}, bf16[512,512]{1,0:T(8,128)(2,1)}, u32[]{:S(2)}, u32[]{:S(2)}) collective-permute-start(bf16[512,512]{1,0:T(8,128)(2,1)} %cot.1), channel_id=1, source_target_pairs={{0,32},{32,0},{1,33},{33,1},{2,34},{34,2},{3,35},{35,3},{4,36},{36... | collective-permute-start | bytes 1572872 | tf_op jit(solution)/shard_map/ppermute | solution.py:374
  4.5 13.3 %copy-start.21 = (s32[512,8]{0,1:T(8,128)S(1)}, s32[512,8]{0,1:T(8,128)}, u32[]{:S(2)}) copy-start(s32[512,8]{0,1:T(8,128)} %param.12) | copy-start | bytes 49156
  4.5 13.3 %copy-start.22 = (s32[512,8]{0,1:T(8,128)S(1)}, s32[512,8]{0,1:T(8,128)}, u32[]{:S(2)}) copy-start(s32[512,8]{0,1:T(8,128)} %param.11) | copy-start | bytes 49156
  4.5 14.4 %copy-start.1 = (bf16[512,512]{1,0:T(8,128)(2,1)S(1)}, bf16[512,512]{1,0:T(8,128)(2,1)}, u32[]{:S(2)}) copy-start(bf16[512,512]{1,0:T(8,128)(2,1)} %x.1) | copy-start | bytes 1572868
  7.3 12.8 %copy-start.2 = (bf16[512,512]{1,0:T(8,128)(2,1)S(1)}, bf16[512,512]{1,0:T(8,128)(2,1)}, u32[]{:S(2)}) copy-start(bf16[512,512]{1,0:T(8,128)(2,1)} %cot.1) | copy-start | bytes 1572868
  7.3 39.9 %all-to-all-start = ((bf16[32,32,512]{2,1,0:T(8,128)(2,1)}), bf16[32,32,512]{2,1,0:T(8,128)(2,1)}, u32[]{:S(2)}, u32[]{:S(2)}) async-start(bf16[32,32,512]{2,1,0:T(8,128)(2,1)} %bitcast.1), calls=%async_computation | async-start | bytes 2097152 | tf_op jit(solution)/shard_map/all_to_all | solution.py:382
  17.9 7.4 %collective-permute-start.2 = (bf16[512,512]{1,0:T(8,128)(2,1)}, bf16[512,512]{1,0:T(8,128)(2,1)}, u32[]{:S(2)}, u32[]{:S(2)}) collective-permute-start(bf16[512,512]{1,0:T(8,128)(2,1)} %collective-permute-done.1), channel_id=1, source_target_pairs={{0,32},{32,0},{1,33},{33,1},{2,34},{34,2},{3,35},{35,3},{4,36},{36... | collective-permute-start | bytes 1572872 | tf_op jit(solution)/shard_map/ppermute | solution.py:374
  20.2 7.3 %copy-start.3 = (bf16[512,512]{1,0:T(8,128)(2,1)S(1)}, bf16[512,512]{1,0:T(8,128)(2,1)}, u32[]{:S(2)}) copy-start(bf16[512,512]{1,0:T(8,128)(2,1)} %wo.3) | copy-start | bytes 1572868
  20.2 7.3 %copy-start.8 = (bf16[512,1536]{1,0:T(8,128)(2,1)S(1)}, bf16[512,1536]{1,0:T(8,128)(2,1)}, u32[]{:S(2)}) copy-start(bf16[512,1536]{1,0:T(8,128)(2,1)} %wqkv.3) | copy-start | bytes 4718596
  25.2 19.9 %copy-start.4 = (bf16[1024,512]{1,0:T(8,128)(2,1)}, bf16[1024,512]{1,0:T(8,128)(2,1)S(1)}, u32[]{:S(2)}) copy-start(bf16[1024,512]{1,0:T(8,128)(2,1)S(1)} %constant_dynamic-update-slice_fusion.4.cot) | copy-start | bytes 3145732
  27.5 1.6 copy-start.6
  45.1 1.3 copy-start.13
  46.5 0.8 copy-start.16
  47.3 1.0 copy-start.12
  79.3 9.9 %collective-permute-start.4 = (bf16[512,768]{1,0:T(8,128)(2,1)}, bf16[512,768]{1,0:T(8,128)(2,1)S(1)}, u32[]{:S(2)}, u32[]{:S(2)}) collective-permute-start(bf16[512,768]{1,0:T(8,128)(2,1)} %get-tuple-element.32), channel_id=1, source_target_pairs={{0,32},{32,0},{1,33},{33,1},{2,34},{34,2},{3,35},{35,3},{4,36},{36... | collective-permute-start | bytes 2359304 | tf_op jit(solution)/shard_map/ppermute | solution.py:374
  79.3 37.8 %all-to-all-start.1 = ((bf16[32,32,512]{2,1,0:T(8,128)(2,1)}), bf16[32,32,512]{2,1,0:T(8,128)(2,1)}, u32[]{:S(2)}, u32[]{:S(2)}) async-start(bf16[32,32,512]{2,1,0:T(8,128)(2,1)} %bitcast.54), calls=%async_computation.1 | async-start | bytes 2097152 | tf_op jit(solution)/shard_map/all_to_all | solution.py:382
  89.2 0.9 copy-start.10
  90.1 1.2 copy-start.5
  91.4 1.6 copy-start.7
  93.0 1.4 copy-start.9
  94.4 1.1 copy-start.11
  95.5 1.6 copy-start.14
  97.1 1.4 copy-start.15
  98.5 1.0 copy-start.17
  115.9 1.2 copy-start
  117.1 34.7 %all-to-all-start.2 = ((bf16[64,8,1792]{2,1,0:T(8,128)(2,1)}), bf16[64,8,1792]{2,1,0:T(8,128)(2,1)}, u32[]{:S(2)}, u32[]{:S(2)}) async-start(bf16[64,8,1792]{2,1,0:T(8,128)(2,1)} %bitcast.51), calls=%async_computation.2 | async-start | bytes 3670016 | tf_op jit(solution)/shard_map/all_to_all | solution.py:378
  128.2 37.5 %collective-permute-start.6 = (bf16[2,512,512]{2,1,0:T(8,128)(2,1)}, bf16[2,512,512]{2,1,0:T(8,128)(2,1)}, u32[]{:S(2)}, u32[]{:S(2)}) collective-permute-start(bf16[2,512,512]{2,1,0:T(8,128)(2,1)} %slice_bitcast_fusion.2), channel_id=1, source_target_pairs={{0,32},{32,0},{1,33},{33,1},{2,34},{34,2},{3,35},{35,3},{4,36},{36... | collective-permute-start | bytes 3145736 | tf_op jit(solution)/shard_map/ppermute | solution.py:374
  154.9 36.4 %all-to-all-start.3 = ((bf16[64,8,1792]{2,1,0:T(8,128)(2,1)}), bf16[64,8,1792]{2,1,0:T(8,128)(2,1)}, u32[]{:S(2)}, u32[]{:S(2)}) async-start(bf16[64,8,1792]{2,1,0:T(8,128)(2,1)} %sum_spread.1), calls=%async_computation.3 | async-start | bytes 3670016 | tf_op jit(solution)/shard_map/all_to_all | solution.py:378
  160.6 8.2 %collective-permute-start.5 = (bf16[512,256]{1,0:T(8,128)(2,1)S(1)}, bf16[512,256]{1,0:T(8,128)(2,1)S(1)}, u32[]{:S(2)}, u32[]{:S(2)}) collective-permute-start(bf16[512,256]{1,0:T(8,128)(2,1)S(1)} %slice.29), channel_id=1, source_target_pairs={{0,32},{32,0},{1,33},{33,1},{2,34},{34,2},{3,35},{35,3},{4,36},{36... | collective-permute-start | bytes 786440 | tf_op jit(solution)/shard_map/ppermute | solution.py:374
  167.2 1.9 copy-start.19
  167.4 22.6 %collective-permute-start.7 = (bf16[512,512]{1,0:T(8,128)(2,1)S(1)}, bf16[512,512]{1,0:T(8,128)(2,1)S(1)}, u32[]{:S(2)}, u32[]{:S(2)}) collective-permute-start(bf16[512,512]{1,0:T(8,128)(2,1)S(1)} %fusion.6), channel_id=1, source_target_pairs={{0,64},{64,0},{1,65},{65,1},{2,66},{66,2},{3,67},{67,3},{4,68},{68... | collective-permute-start | bytes 1572872 | tf_op jit(solution)/shard_map/ppermute | solution.py:374
  168.8 21.2 %copy-start.20 = (f32[512,512]{1,0:T(8,128)S(1)}, f32[512,512]{1,0:T(8,128)}, u32[]{:S(2)}) copy-start(f32[512,512]{1,0:T(8,128)} %get-tuple-element.40) | copy-start | bytes 3145732
  191.3 7.3 %collective-permute-start.8 = (bf16[512,1792]{1,0:T(8,128)(2,1)}, bf16[512,1792]{1,0:T(8,128)(2,1)S(1)}, u32[]{:S(2)}, u32[]{:S(2)}) collective-permute-start(bf16[512,1792]{1,0:T(8,128)(2,1)} %bitcast.6.own), channel_id=1, source_target_pairs={{0,32},{32,0},{1,33},{33,1},{2,34},{34,2},{3,35},{35,3},{4,36},{36... | collective-permute-start | bytes 5505032 | tf_op jit(solution)/shard_map/ppermute | solution.py:374
  198.6 1.3 copy-start.18

commit v3 on v2

--- a/solution.py
+++ b/solution.py
@@ -28,16 +28,23 @@
     return lax.dot_general(a, b, dims, preferred_element_type=F32)
 
 
-def attn_kernel(pair, core, xa, cot, wqkv, wo, *rest):
+def attn_kernel(pair, core, x0, x1, x2, x3, cot0, cot1, wqkv, wo, *rest):
     if pair:
-        g_first, keep, got, d_first, joint_o, mixed_o, part_o = rest[:7]
-        rest = rest[7:]
+        g_first, keep, got, joint_o, mixed_o, part_o = rest[:6]
+        rest = rest[6:]
     else:
         grad_o, mixed_o, part_o = rest[:3]
         rest = rest[3:]
     k_s, v_s, kt_s, vt_s, qt_s, dmt_s, s_s, e_s, dka, dva, mt_s, dqt_s = rest
-    seq = xa.shape[0]
-    nq = cot.shape[0]
+    xs = (x0, x1, x2, x3)
+    cots = (cot0, cot1)
+    n = x0.shape[0]
+    seq = n * len(xs)
+    nq = n * len(cots)
+
+    def of(refs, r):
+        return refs[r.start // n][r.start % n : r.start % n + CK, :]
+
     chunks = [slice(c * CK, c * CK + CK) for c in range(seq // CK)]
     scale = 0.125
     c2 = scale * LOG2E
@@ -48,15 +55,15 @@
     wo_own = wo[pl.ds(off, 128), :]
     wkv = jnp.concatenate([wk, wv], axis=1)
     for r in chunks:
-        kv = dot(xa[r, :], wkv, NN)
+        kv = dot(of(xs, r), wkv, NN)
         k_s[r, :] = kv[:, :128].astype(BF)
         v_s[r, :] = kv[:, 128:].astype(BF)
         kvt = kv.T
         kt_s[:, r] = kvt[:128].astype(BF)
         vt_s[:, r] = kvt[128:].astype(BF)
     for r in chunks[: nq // CK]:
-        qt_s[:, r] = dot(xa[r, :], wq, NN).T.astype(BF)
-        dmt_s[:, r] = dot(cot[r, :], wo_own, NT).T.astype(BF)
+        qt_s[:, r] = dot(of(xs, r), wq, NN).T.astype(BF)
+        dmt_s[:, r] = dot(of(cots, r), wo_own, NT).T.astype(BF)
     row = lax.broadcasted_iota(jnp.int32, (128, QB), 0)
     heads = [slice(h * 64, h * 64 + 64) for h in range(2)]
     lanes = [slice(h * QB, h * QB + QB) for h in range(2)]
@@ -135,12 +142,11 @@
     dqt = dqt_s[...].astype(BF)
     dkt = dka[...].astype(BF)
     dvt = dva[...].astype(BF)
-    grads = (
-        dot(dqt, xa[:nq, :], NN),
-        dot(dkt, xa[...], NN),
-        dot(dvt, xa[...], NN),
-        dot(mt_s[...], cot[...], NN),
-    )
+
+    def over(lhs, refs):
+        return sum(dot(lhs[:, i * n : i * n + n], ref[...], NN) for i, ref in enumerate(refs))
+
+    grads = (over(dqt, xs[: len(cots)]), over(dkt, xs), over(dvt, xs), over(mt_s[...], cots))
     for i, g in enumerate(grads):
         if pair:
             joint_o[i * 128 : i * 128 + 128, 512:1024] = g.astype(BF)
@@ -156,14 +162,13 @@
         part = dot(dkv[r, :], wkv, NT)
         if r.start < nq:
             part = part + dot(dq[r, :], wq, NT)
-        if pair:
-            part = part + d_first[r, :].astype(F32)
         part_o[r, :] = part.astype(BF)
 
 
-def attention(pair, core, xa, cot, wqkv, wo, *first):
-    seq, d = xa.shape
-    nq = cot.shape[0]
+def attention(pair, core, xs, cots, wqkv, wo, *first):
+    n, d = xs[0].shape
+    seq = n * len(xs)
+    nq = n * len(cots)
     hw = 128
     sd = jax.ShapeDtypeStruct
     V = pltpu.VMEM
@@ -171,7 +176,7 @@
     return pl.pallas_call(
         functools.partial(attn_kernel, pair),
         out_shape=(sd((512, 1792 if pair else 512), BF), sd((nq, hw), BF), sd((seq, d), BF)),
-        in_specs=[pl.BlockSpec(memory_space=pltpu.SMEM)] + [vm] * (4 + len(first)),
+        in_specs=[pl.BlockSpec(memory_space=pltpu.SMEM)] + [vm] * (8 + len(first)),
         out_specs=(vm,) * 3,
         scratch_shapes=[V((seq, hw), BF)] * 2
         + [V((hw, seq), BF)] * 2
@@ -179,10 +184,10 @@
         + [V((2, seq, 2 * QB), F32), V((2, seq, 2 * QB), BF)]
         + [V((hw, seq), F32)] * 2
         + [V((hw, nq), BF), V((hw, nq), F32)],
-        compiler_params=pltpu.CompilerParams(vmem_limit_bytes=40 * MIB),
+        compiler_params=pltpu.CompilerParams(vmem_limit_bytes=32 * MIB),
         cost_estimate=pl.CostEstimate(flops=16 * 10**9, bytes_accessed=8 * MIB, transcendentals=4 * MIB),
         name="attention",
-    )(core, xa, cot, wqkv, wo, *first)
+    )(core, *xs, *cots, wqkv, wo, *first)
 
 
 def edges_kernel(core, idx, x, inc, cot, mask, wg, ws, base_o, local_o, remote_o, keep_o, give_o, a_s, b_s, gt_s, up_s, dsrc, dgate, e_s, *accs):
@@ -297,7 +302,7 @@
         e_s[:, cs] = dot(xt, dsrc[:n, cs], NN) + dot(it, dsrc[n:, cs], NN)
     e_s[:, 1024:] = dot(xt, dgate[...], NN)
     half = e_s.shape[1] // 2
-    keep_o[...] = e_s[:, pl.ds(pl.multiple_of(core[0] * half, 128), half)]
+    keep_o[...] = e_s[:, pl.ds(pl.multiple_of(core[0] * half, 128), half)].astype(BF)
     give_o[...] = e_s[:, pl.ds(pl.multiple_of((1 - core[0]) * half, 128), half)].astype(BF)
 
 
@@ -312,11 +317,11 @@
     per_node = V((n * 8, 128), F32)
     return pl.pallas_call(
         edges_kernel,
-        out_shape=(sd((n, d), F32), sd((n, d), F32), sd(inc.shape, BF), sd((d, 768), F32), sd((d, 768), BF)),
+        out_shape=(sd((n, d), F32), sd((n, d), F32), sd(inc.shape, BF), sd((d, 768), BF), sd((d, 768), BF)),
         in_specs=[sm, sm] + [vm] * 6,
         out_specs=(vm,) * 5,
         scratch_shapes=[table, table, per_node, per_node, V((rows, 2 * d), BF), V((n, d), BF), V((d, 3 * d), F32)] + [table] * NACC,
-        compiler_params=pltpu.CompilerParams(vmem_limit_bytes=52 * MIB),
+        compiler_params=pltpu.CompilerParams(vmem_limit_bytes=48 * MIB),
         cost_estimate=pl.CostEstimate(flops=20 * 10**9, bytes_accessed=8 * MIB, transcendentals=4 * MIB),
         name="edges",
     )(core, idx, x, inc, cot, mask, wg, ws)
@@ -339,35 +344,63 @@
     )(got)
 
 
-def place_kernel(core, own, other, gate, source, qkv, out):
-    for c in range(2):
-
-        @pl.when(core[0] == c)
-        def _():
-            for mine, src in ((c, own), (1 - c, other)):
-                for p in range(2):
-                    cols = slice(p * 512, p * 512 + 512)
-                    at = mine * 256 + p * 128
-                    for i in range(3):
-                        qkv[:, i * 512 + at : i * 512 + at + 128] = src[i * 128 : i * 128 + 128, cols].astype(F32).T
-                    out[at : at + 128, :] = src[384:, cols].astype(F32)
-                if mine == 0:
-                    source[:, :768] = src[:, 1024:].astype(F32)
-                else:
-                    source[:, 768:] = src[:, 1024:1280].astype(F32)
-                    gate[...] = src[:, 1280:].astype(F32)
-
-
-def place(core, own, other):
-    vm = pl.BlockSpec(memory_space=pltpu.VMEM)
+def place_kernel(which, *refs):
+    core, src = refs[:2]
+    gate_o, source_o, qkv_o, out_o, qkv_s, rest_s, sems = refs[-7:]
+    mine = core[0] if which == 0 else 1 - core[0]
+    copies = []
+    for p in range(2):
+        at = pl.multiple_of(mine * 256 + p * 128, 128)
+        cols = slice(p * 512, p * 512 + 512)
+        for i in range(3):
+            k = p * 3 + i
+            qkv_s[k] = src[i * 128 : i * 128 + 128, cols].astype(F32).T
+            to = qkv_o.at[:, pl.ds(pl.multiple_of(at + i * 512, 128), 128)]
+            copies.append(pltpu.make_async_copy(qkv_s.at[k], to, sems.at[k]))
+            copies[-1].start()
+        rows = slice(p * 128, p * 128 + 128)
+        rest_s[rows, :512] = src[384:, cols].astype(F32)
+        copies.append(pltpu.make_async_copy(rest_s.at[rows, :512], out_o.at[pl.ds(at, 128), :], sems.at[6 + p]))
+        copies[-1].start()
+    rest_s[:, 512:] = src[:, 1024:].astype(F32)
+    low = rest_s.at[:, 512:768]
+    high = rest_s.at[:, 768:1280]
+
+    @pl.when(mine == 0)
+    def _():
+        one = pltpu.make_async_copy(low, source_o.at[:, :256], sems.at[8])
+        two = pltpu.make_async_copy(high, source_o.at[:, 256:768], sems.at[9])
+        one.start()
+        two.start()
+        one.wait()
+        two.wait()
+
+    @pl.when(mine == 1)
+    def _():
+        one = pltpu.make_async_copy(low, source_o.at[:, 768:], sems.at[8])
+        two = pltpu.make_async_copy(high, gate_o, sems.at[9])
+        one.start()
+        two.start()
+        one.wait()
+        two.wait()
+
+    for copy in copies:
+        copy.wait()
+
+
+def place(which, core, src, *before):
     sd = jax.ShapeDtypeStruct
+    anywhere = pl.BlockSpec(memory_space=pl.ANY)
     return pl.pallas_call(
-        place_kernel,
+        functools.partial(place_kernel, which),
         out_shape=(sd((512, 512), F32), sd((512, 1024), F32), sd((512, 1536), F32), sd((512, 512), F32)),
-        in_specs=[pl.BlockSpec(memory_space=pltpu.SMEM), vm, vm],
-        out_specs=(vm,) * 4,
+        in_specs=[pl.BlockSpec(memory_space=pltpu.SMEM), pl.BlockSpec(memory_space=pltpu.VMEM)] + [anywhere] * len(before),
+        out_specs=(anywhere,) * 4,
+        input_output_aliases={2 + i: i for i in range(len(before))},
+        scratch_shapes=[pltpu.VMEM((6, 512, 128), F32), pltpu.VMEM((512, 1280), F32), pltpu.SemaphoreType.DMA((10,))],
+        compiler_params=pltpu.CompilerParams(vmem_limit_bytes=16 * MIB),
         name="place",
-    )(core, own, other)
+    )(core, src, *before)
 
 
 def swap(a, axis):
@@ -392,15 +425,15 @@
     pick = (rows[:, None] == lax.broadcasted_iota(jnp.int32, (rows.shape[0], n), 1)).astype(BF)
     incoming = domains(dot(pick, x, NN).astype(BF))
     x_far_sib = swap(x_far, "c")
-    xa = jnp.concatenate([x, x_sib, x_far, x_far_sib], axis=0)
-    ca = jnp.concatenate([cot, cot_sib], axis=0)
-    grad_first, mixed_first, part_first = attention(0, core, xa, ca, wqkv, wo)
+    xs = (x, x_sib, x_far, x_far_sib)
+    cots = (cot, cot_sib)
+    grad_first, mixed_first, part_first = attention(0, core, xs, cots, wqkv, wo)
     idx = (jnp.where(mask > 0, slots, 3 * n) * 8).reshape(-1)
     incoming, grad_first = lax.optimization_barrier((incoming, grad_first))
     base, local, remote, keep, give = edges(core, idx, x, incoming, cot, mask, wg, ws)
     returned = domains(remote)
     got = swap(give, "c")
-    joint, mixed_second, part = attention(1, core, xa, ca, wqkv, wo, grad_first, keep, got, part_first)
+    joint, mixed_second, part_second = attention(1, core, xs, cots, wqkv, wo, grad_first, keep, got)
     joint, returned = lax.optimization_barrier((joint, returned))
     parts = chips(joint.reshape(64, 8, -1))
     mixed = jnp.concatenate([mixed_first, mixed_second], axis=1)
@@ -410,15 +443,16 @@
     wo_sib = lax.dynamic_index_in_dim(wo2, 1 - core[0], 0, keepdims=False)
     attended = dot(mixed[:n], wo_own, NN) + dot(mixed_sib, wo_sib, NN)
     layer_out = (base + attended).astype(BF)
-    part4 = part.reshape(2, 2, n, d)
-    from_sib = swap(part4[:, 1], "c").astype(F32)
-    from_far = swap((part4[1, 0].astype(F32) + from_sib[1]).astype(BF), "xl")
+    part4 = (part_first.astype(F32) + part_second.astype(F32)).reshape(2, 2, n, d)
+    from_sib = swap(part4[:, 1].astype(BF), "c").astype(F32)
+    from_far = swap((part4[1, 0] + from_sib[1]).astype(BF), "xl")
     feats_grad = (
-        local + part4[0, 0].astype(F32) + from_sib[0] + from_far.astype(F32) + dot(pick, returned, TN)
+        local + part4[0, 0] + from_sib[0] + from_far.astype(F32) + dot(pick, returned, TN)
     ).astype(BF)
     own = chips(sum_spread(parts)).reshape(512, -1)
     own, layer_out, feats_grad = lax.optimization_barrier((own, layer_out, feats_grad))
-    gate_grad, source_grad, qkv_grad, out_grad = place(core, own, swap(own, "c"))
+    other = swap(own, "c")
+    gate_grad, source_grad, qkv_grad, out_grad = place(1, core, other, *place(0, core, own))
     return layer_out, feats_grad, gate_grad, source_grad, qkv_grad, out_grad
 
 

time: 210 us -> 225 us (1.071)
  waiting for transfers between devices: 45.9 us -> 53.1 us
  local copies, waits for them, and re-layouts: 28 us -> 35 us
  other arithmetic: 2.94 us -> 5.31 us
    ppermute x9, waiting for transfers between devices: 23.4 us -> 34.3 us  [swap(): return lax.ppermute(a, axis, SWAP)]
    unnamed x52 -> x80, local copies, waits for them, and re-layouts: 22.5 us -> 32.7 us
    all_to_all x2, waiting for transfers between devices: 22.4 us -> 18.7 us  [chips(): return lax.all_to_all(a, CHIPS, 0, 0, tiled=True)]
    concatenate x2 -> x0, local copies, waits for them, and re-layouts: 3.32 us -> none  [the longest x1 2.25 us: body(): xa = jnp.concatenate([x, x_sib, x_far, x_far_sib], axis=0)]
    pallas_call x1 -> x2, Pallas kernels: 5.87 us -> 4.07 us  [place(): pl.pallas_call(functools.partial(place_kernel, which), out_shape=(sd((512...]
  transfers between devices with their start and end apart: 13 -> 13, of which waited for: 3 -> 4; matrix products, arithmetic and copies ran while one was open for 10% -> 7% of each run, Pallas kernels for 17% -> 17%
where the time goes in v3:
time: 225 us; the launch traced here: 221 us
  Pallas kernels  70.9 us (32%)
  waiting for transfers between devices  53.1 us (24%)
  starting transfers between devices  48.7 us (22%)
  local copies, waits for them, and re-layouts  35 us (16%)
  matrix products  6.54 us (3%)
  other arithmetic  5.31 us (2%)
    ppermute x9, waiting for transfers between devices, swap(): return lax.ppermute(a, axis, SWAP)  34.3 us
    pallas_call x2, Pallas kernels, attention(): pl.pallas_call(functools.partial(attn_kernel, pair), out_shape=(sd((512,...  33.5 us
    unnamed x80, local copies, waits for them, and re-layouts  32.7 us
    pallas_call x1, Pallas kernels, edges(): pl.pallas_call(edges_kernel, out_shape=(sd((n, d), F32), sd((n, d), F32),...  30.3 us
    all_to_all x2, starting transfers between devices, domains(): lax.all_to_all(a.reshape(32, 32, -1), DOM, 0, 0, tiled=True)  21.1 us
    all_to_all x2, waiting for transfers between devices, chips(): return lax.all_to_all(a, CHIPS, 0, 0, tiled=True)  18.7 us
    all_to_all x2, starting transfers between devices, chips(): return lax.all_to_all(a, CHIPS, 0, 0, tiled=True)  16.3 us
    ppermute x9, starting transfers between devices, swap(): return lax.ppermute(a, axis, SWAP)  11.2 us
  transfers between devices with their start and end apart: 13, of which 4 were waited for; matrix products, arithmetic and copies ran while one was open for 7% of the time, Pallas kernels for 17%

profile of v3, /device:TPU:1, one launch (start us, length us, event | category | flops | bytes accessed | tf_op | source)
XLA Modules:
  0.0 220.6 jit_solution(535395098604638724)
XLA Ops:
  0.6 2.1 collective-permute-start.1
  2.8 1.0 collective-permute-start
  3.7 10.4 %collective-permute-done.1.x2 = bf16[512,512]{1,0:T(8,128)(2,1)S(1)} collective-permute-done((bf16[512,512]{1,0:T(8,128)(2,1)}, bf16[512,512]{1,0:T(8,128)(2,1)S(1)}, u32[]{:S(2)}, u32[]{:S(2)}) %collective-permute-start.1) | collective-permute-done | bytes 524320 | tf_op jit(solution)/shard_map/ppermute | solution.py:407
  14.1 1.7 collective-permute-start.2
  15.8 0.8 eq.10
  16.6 2.8 %fusion.2 = bf16[1024,512]{1,0:T(8,128)(2,1)} fusion(bf16[512,512]{1,0:T(8,128)(2,1)} %x0.3, s32[1024]{0:T(1024)S(1)} %eq.10), kind=kOutput, calls=%fused_computation.5 | convolution fusion | flops 537919488 | bytes 1576960 | tf_op jit(solution)/shard_map/dot_general | solution.py:28
  19.4 11.2 %all-to-all-start = ((bf16[32,32,512]{2,1,0:T(8,128)(2,1)}), bf16[32,32,512]{2,1,0:T(8,128)(2,1)}, u32[]{:S(2)}, u32[]{:S(2)}) async-start(bf16[32,32,512]{2,1,0:T(8,128)(2,1)} %bitcast.54), calls=%async_computation | async-start | bytes 2097152 | tf_op jit(solution)/shard_map/all_to_all | solution.py:415
  30.6 0.8 copy.22.mask
  31.6 0.2 reshape.47.idx
  31.8 0.8 copy-done.25
  32.6 0.8 copy-done.22
  33.4 0.8 copy-done.28
  34.2 1.4 copy-done.10
  35.6 1.0 copy-done.16
  36.6 1.0 copy-done.20
  37.7 1.0 copy-done.23
  38.7 1.0 copy-done.26
  39.8 1.0 copy-done.29
  40.8 16.0 %attention.2 = (bf16[512,512]{1,0:T(8,128)(2,1)S(1)}, bf16[1024,128]{1,0:T(8,128)(2,1)S(1)}, bf16[2048,512]{1,0:T(8,128)(2,1)S(1)}) custom-call(s32[1]{0:T(128)} %bitcast.core.refs_0_, bf16[512,512]{1,0:T(8,128)(2,1)S(1)} %copy-done.13, bf16[512,512]{1,0:T(8,128)(2,1)S(1)} %copy-done.23, bf16[512,512]{1,0:T(8,128)(2,1)S(1)} %copy-done.20, ...), custom_call_target="tpu_custom_call" | custom-call | flops 16000000000 | bytes 8388608 | tf_op jit(solution)/shard_map/attention/pallas_call | solution.py:176
  56.9 0.8 copy-done.33
  57.7 0.9 copy-done.9
  58.6 1.0 copy-done.12
  59.7 1.0 copy-done.14
  60.7 1.0 copy-done.17
  61.7 30.3 %edges.1 = (f32[512,512]{1,0:T(8,128)S(1)}, f32[512,512]{1,0:T(8,128)S(1)}, bf16[1024,512]{1,0:T(8,128)(2,1)}, bf16[512,768]{1,0:T(8,128)(2,1)S(1)}, bf16[512,768]{1,0:T(8,128)(2,1)}) custom-call(s32[1]{0:T(128)} %bitcast.core.refs_0_, s32[4096]{0:T(1024)S(1)} %reshape.47.idx, bf16[512,512]{1,0:T(8,128)(2,1)S(1)} %copy-done.14, ...), custom_call_target="tpu_custom_call" | custom-call | flops 20000000000 | bytes 8388608 | tf_op jit(solution)/shard_map/edges/pallas_call | solution.py:318
  92.1 1.0 copy-done.2
  93.0 0.9 copy-done.31
  93.9 0.4 collective-permute-start.4
  94.3 10.0 %all-to-all-start.1 = ((bf16[32,32,512]{2,1,0:T(8,128)(2,1)}), bf16[32,32,512]{2,1,0:T(8,128)(2,1)}, u32[]{:S(2)}, u32[]{:S(2)}) async-start(bf16[32,32,512]{2,1,0:T(8,128)(2,1)} %bitcast.55), calls=%async_computation.1 | async-start | bytes 2097152 | tf_op jit(solution)/shard_map/all_to_all | solution.py:415
  104.3 1.0 copy-done.5
  105.3 1.4 copy-done.11
  106.7 1.0 copy-done.15
  107.8 1.0 copy-done.18
  108.8 1.0 copy-done.21
  109.9 1.0 copy-done.24
  110.9 1.0 copy-done.27
  111.9 1.0 copy-done.30
  113.0 1.1 copy-done.32
  114.1 1.0 copy-done.34
  115.2 17.5 %attention.3 = (bf16[512,1792]{1,0:T(8,128)(2,1)S(1)}, bf16[1024,128]{1,0:T(8,128)(2,1)S(1)}, bf16[2048,512]{1,0:T(8,128)(2,1)S(1)}) custom-call(s32[1]{0:T(128)} %bitcast.core.refs_0_, bf16[512,512]{1,0:T(8,128)(2,1)S(1)} %copy-done.15, bf16[512,512]{1,0:T(8,128)(2,1)S(1)} %copy-done.24, bf16[512,512]{1,0:T(8,128)(2,1)S(1)} %copy-done.21, ...), custom_call_target="tpu_custom_call" | custom-call | flops 16000000000 | bytes 8388608 | tf_op jit(solution)/shard_map/attention/pallas_call | solution.py:176
  132.6 1.3 copy-done
  133.9 1.2 copy-done.1
  135.2 0.7 copy-done.7
  135.9 10.0 %all-to-all-start.2 = ((bf16[64,8,1792]{2,1,0:T(8,128)(2,1)}), bf16[64,8,1792]{2,1,0:T(8,128)(2,1)}, u32[]{:S(2)}, u32[]{:S(2)}) async-start(bf16[64,8,1792]{2,1,0:T(8,128)(2,1)} %bitcast.48), calls=%async_computation.2 | async-start | bytes 3670016 | tf_op jit(solution)/shard_map/all_to_all | solution.py:411
  145.9 2.2 convert_add_fusion
  148.1 2.0 copy-done.35
  150.1 1.1 fusion.5
  151.2 0.8 collective-permute-start.6
  152.0 18.7 %all-to-all-done.2.got = bf16[64,8,1792]{2,1,0:T(8,128)(2,1)} async-done(((bf16[64,8,1792]{2,1,0:T(8,128)(2,1)}), bf16[64,8,1792]{2,1,0:T(8,128)(2,1)}, u32[]{:S(2)}, u32[]{:S(2)}) %all-to-all-start.2) | async-done | bytes 1835040 | tf_op jit(solution)/shard_map/all_to_all | solution.py:411
  170.7 3.0 %sum_spread.1 = bf16[64,8,1792]{2,1,0:T(8,128)(2,1)} custom-call(bf16[64,8,1792]{2,1,0:T(8,128)(2,1)} %all-to-all-done.2.got), custom_call_target="tpu_custom_call" | custom-call | flops 917504 | bytes 3670016 | tf_op jit(solution)/shard_map/sum_spread/pallas_call | solution.py:337
  173.8 6.3 %all-to-all-start.3 = ((bf16[64,8,1792]{2,1,0:T(8,128)(2,1)}), bf16[64,8,1792]{2,1,0:T(8,128)(2,1)S(1)}, u32[]{:S(2)}, u32[]{:S(2)}) async-start(bf16[64,8,1792]{2,1,0:T(8,128)(2,1)} %sum_spread.1), calls=%async_computation.3 | async-start | bytes 3670016 | tf_op jit(solution)/shard_map/all_to_all | solution.py:411
  180.3 1.4 collective-permute-start.5
  181.7 2.4 %fusion = f32[512,512]{1,0:T(8,128)S(1)} fusion(bf16[1024,512]{1,0:T(8,128)(2,1)} %bitcast.4, s32[1024]{0:T(1024)S(1)} %eq.10), kind=kOutput, calls=%fused_computation.3 | convolution fusion | flops 537395200 | bytes 2101248 | tf_op jit(solution)/shard_map/dot_general | solution.py:28
  184.1 1.5 convert_element_type.34
  185.6 0.3 fusion.7
  185.9 1.5 collective-permute-start.7
  187.4 0.3 fusion.16
  187.7 1.1 fusion.4
  188.8 22.5 %collective-permute-done.7 = bf16[512,512]{1,0:T(8,128)(2,1)S(1)} collective-permute-done((bf16[512,512]{1,0:T(8,128)(2,1)S(1)}, bf16[512,512]{1,0:T(8,128)(2,1)S(1)}, u32[]{:S(2)}, u32[]{:S(2)}) %collective-permute-start.7) | collective-permute-done | bytes 524320 | tf_op jit(solution)/shard_map/ppermute | solution.py:407
  211.3 1.4 fusion.11
  212.7 2.3 %collective-permute-start.8 = (bf16[512,1792]{1,0:T(8,128)(2,1)S(1)}, bf16[512,1792]{1,0:T(8,128)(2,1)S(1)}, u32[]{:S(2)}, u32[]{:S(2)}) collective-permute-start(bf16[512,1792]{1,0:T(8,128)(2,1)S(1)} %bitcast.46), channel_id=1, source_target_pairs={{0,32},{32,0},{1,33},{33,1},{2,34},{34,2},{3,35},{35,3},{4,36},{36... | collective-permute-start | bytes 5505032 | tf_op jit(solution)/shard_map/ppermute | solution.py:407
  214.9 2.0 place.2
  217.0 1.4 collective-permute-done.8.refs_1_
  218.4 2.0 place.3
  (63 shorter events, 0.4 us)
Async XLA Ops:
  0.6 13.5 %collective-permute-start.1 = (bf16[512,512]{1,0:T(8,128)(2,1)}, bf16[512,512]{1,0:T(8,128)(2,1)S(1)}, u32[]{:S(2)}, u32[]{:S(2)}) collective-permute-start(bf16[512,512]{1,0:T(8,128)(2,1)} %x0.3), channel_id=1, source_target_pairs={{0,64},{64,0},{1,65},{65,1},{2,66},{66,2},{3,67},{67,3},{4,68},{68... | collective-permute-start | bytes 1572872 | tf_op jit(solution)/shard_map/ppermute | solution.py:407
  2.8 29.8 %collective-permute-start = (bf16[512,512]{1,0:T(8,128)(2,1)}, bf16[512,512]{1,0:T(8,128)(2,1)S(1)}, u32[]{:S(2)}, u32[]{:S(2)}) collective-permute-start(bf16[512,512]{1,0:T(8,128)(2,1)} %x0.3), channel_id=1, source_target_pairs={{0,32},{32,0},{1,33},{33,1},{2,34},{34,2},{3,35},{35,3},{4,36},{36... | collective-permute-start | bytes 1572872 | tf_op jit(solution)/shard_map/ppermute | solution.py:407
  3.7 28.1 %collective-permute-start.3 = (bf16[512,512]{1,0:T(8,128)(2,1)}, bf16[512,512]{1,0:T(8,128)(2,1)S(1)}, u32[]{:S(2)}, u32[]{:S(2)}) collective-permute-start(bf16[512,512]{1,0:T(8,128)(2,1)} %cot0.3), channel_id=1, source_target_pairs={{0,32},{32,0},{1,33},{33,1},{2,34},{34,2},{3,35},{35,3},{4,36},{36... | collective-permute-start | bytes 1572872 | tf_op jit(solution)/shard_map/ppermute | solution.py:407
  14.1 5.3 %copy-start.19 = (bf16[512,512]{1,0:T(8,128)(2,1)}, bf16[512,512]{1,0:T(8,128)(2,1)S(1)}, u32[]{:S(2)}) copy-start(bf16[512,512]{1,0:T(8,128)(2,1)S(1)} %collective-permute-done.1.x2) | copy-start | bytes 1572868
  14.1 19.3 %collective-permute-start.2 = (bf16[512,512]{1,0:T(8,128)(2,1)S(1)}, bf16[512,512]{1,0:T(8,128)(2,1)S(1)}, u32[]{:S(2)}, u32[]{:S(2)}) collective-permute-start(bf16[512,512]{1,0:T(8,128)(2,1)S(1)} %collective-permute-done.1.x2), channel_id=1, source_target_pairs={{0,32},{32,0},{1,33},{33,1},{2,34},{34,2},{3,35},{35,3},{4,36},{36... | collective-permute-start | bytes 1572872 | tf_op jit(solution)/shard_map/ppermute | solution.py:407
  16.6 14.0 %copy-start.37 = (s32[512,8]{0,1:T(8,128)S(1)}, s32[512,8]{0,1:T(8,128)}, u32[]{:S(2)}) copy-start(s32[512,8]{0,1:T(8,128)} %param.12) | copy-start | bytes 49156
  16.6 14.9 %copy-start.38 = (s32[512,8]{0,1:T(8,128)S(1)}, s32[512,8]{0,1:T(8,128)}, u32[]{:S(2)}) copy-start(s32[512,8]{0,1:T(8,128)} %param.11) | copy-start | bytes 49156
  19.4 14.8 %copy-start.4 = (bf16[512,512]{1,0:T(8,128)(2,1)S(1)}, bf16[512,512]{1,0:T(8,128)(2,1)}, u32[]{:S(2)}) copy-start(bf16[512,512]{1,0:T(8,128)(2,1)} %wo.3) | copy-start | bytes 1572868
  19.4 14.8 %copy-start.13 = (bf16[512,512]{1,0:T(8,128)(2,1)S(1)}, bf16[512,512]{1,0:T(8,128)(2,1)}, u32[]{:S(2)}) copy-start(bf16[512,512]{1,0:T(8,128)(2,1)} %x0.3) | copy-start | bytes 1572868
  19.4 38.2 %all-to-all-start = ((bf16[32,32,512]{2,1,0:T(8,128)(2,1)}), bf16[32,32,512]{2,1,0:T(8,128)(2,1)}, u32[]{:S(2)}, u32[]{:S(2)}) async-start(bf16[32,32,512]{2,1,0:T(8,128)(2,1)} %bitcast.54), calls=%async_computation | async-start | bytes 2097152 | tf_op jit(solution)/shard_map/all_to_all | solution.py:415
  31.8 0.8 copy-start.25
  32.6 0.8 copy-start.22
  33.4 0.8 copy-start.28
  34.2 1.4 copy-start.10
  35.6 1.0 copy-start.16
  36.6 1.0 copy-start.20
  37.7 1.0 copy-start.23
  38.7 1.0 copy-start.26
  39.8 1.0 copy-start.29
  56.8 0.8 copy-start.33
  57.7 1.0 copy-start.9
  58.6 1.0 copy-start.12
  59.6 1.0 copy-start.14
  60.7 1.0 copy-start.17
  92.1 1.0 copy-start.2
  93.0 0.9 copy-start.31
  93.9 10.3 %collective-permute-start.4 = (bf16[512,768]{1,0:T(8,128)(2,1)}, bf16[512,768]{1,0:T(8,128)(2,1)}, u32[]{:S(2)}, u32[]{:S(2)}) collective-permute-start(bf16[512,768]{1,0:T(8,128)(2,1)} %get-tuple-element.36), channel_id=1, source_target_pairs={{0,32},{32,0},{1,33},{33,1},{2,34},{34,2},{3,35},{35,3},{4,36},{36... | collective-permute-start | bytes 2359304 | tf_op jit(solution)/shard_map/ppermute | solution.py:407
  94.3 41.6 %all-to-all-start.1 = ((bf16[32,32,512]{2,1,0:T(8,128)(2,1)}), bf16[32,32,512]{2,1,0:T(8,128)(2,1)}, u32[]{:S(2)}, u32[]{:S(2)}) async-start(bf16[32,32,512]{2,1,0:T(8,128)(2,1)} %bitcast.55), calls=%async_computation.1 | async-start | bytes 2097152 | tf_op jit(solution)/shard_map/all_to_all | solution.py:415
  104.3 1.0 copy-start.5
  105.3 1.4 copy-start.11
  106.7 1.0 copy-start.15
  107.8 1.0 copy-start.18
  108.8 1.0 copy-start.21
  109.9 1.0 copy-start.24
  110.9 1.0 copy-start.27
  111.9 1.0 copy-start.30
  113.0 1.1 copy-start.32
  114.1 1.0 copy-start.34
  132.6 1.3 copy-start
  133.9 1.2 copy-start.1
  135.2 0.7 copy-start.7
  135.9 34.8 %all-to-all-start.2 = ((bf16[64,8,1792]{2,1,0:T(8,128)(2,1)}), bf16[64,8,1792]{2,1,0:T(8,128)(2,1)}, u32[]{:S(2)}, u32[]{:S(2)}) async-start(bf16[64,8,1792]{2,1,0:T(8,128)(2,1)} %bitcast.48), calls=%async_computation.2 | async-start | bytes 3670016 | tf_op jit(solution)/shard_map/all_to_all | solution.py:411
  148.1 2.0 copy-start.35
  151.2 32.9 %collective-permute-start.6 = (bf16[2,512,512]{2,1,0:T(8,128)(2,1)}, bf16[2,512,512]{2,1,0:T(8,128)(2,1)}, u32[]{:S(2)}, u32[]{:S(2)}) collective-permute-start(bf16[2,512,512]{2,1,0:T(8,128)(2,1)} %fusion.5), channel_id=1, source_target_pairs={{0,32},{32,0},{1,33},{33,1},{2,34},{34,2},{3,35},{35,3},{4,36},{36... | collective-permute-start | bytes 3145736 | tf_op jit(solution)/shard_map/ppermute | solution.py:407
  173.8 6.4 %copy-start.8 = (bf16[1024,128]{1,0:T(8,128)(2,1)S(1)}, bf16[1024,128]{1,0:T(8,128)(2,1)}, u32[]{:S(2)}) copy-start(bf16[1024,128]{1,0:T(8,128)(2,1)} %copy-done.7) | copy-start | bytes 786436
  173.8 38.9 %all-to-all-start.3 = ((bf16[64,8,1792]{2,1,0:T(8,128)(2,1)}), bf16[64,8,1792]{2,1,0:T(8,128)(2,1)S(1)}, u32[]{:S(2)}, u32[]{:S(2)}) async-start(bf16[64,8,1792]{2,1,0:T(8,128)(2,1)} %sum_spread.1), calls=%async_computation.3 | async-start | bytes 3670016 | tf_op jit(solution)/shard_map/all_to_all | solution.py:411
  180.3 7.1 %collective-permute-start.5 = (bf16[512,256]{1,0:T(8,128)(2,1)S(1)}, bf16[512,256]{1,0:T(8,128)(2,1)S(1)}, u32[]{:S(2)}, u32[]{:S(2)}) collective-permute-start(bf16[512,256]{1,0:T(8,128)(2,1)S(1)} %slice.30), channel_id=1, source_target_pairs={{0,32},{32,0},{1,33},{33,1},{2,34},{34,2},{3,35},{35,3},{4,36},{36... | collective-permute-start | bytes 786440 | tf_op jit(solution)/shard_map/ppermute | solution.py:407
  181.7 3.9 %copy-start.36 = (f32[2048,512]{1,0:T(8,128)S(1)}, f32[2048,512]{1,0:T(8,128)}, u32[]{:S(2)}) copy-start(f32[2048,512]{1,0:T(8,128)} %copy-done.35) | copy-start | bytes 12582916
  185.6 1.8 copy-start.6
  185.6 2.1 copy-start.3
  185.9 25.4 %collective-permute-start.7 = (bf16[512,512]{1,0:T(8,128)(2,1)S(1)}, bf16[512,512]{1,0:T(8,128)(2,1)S(1)}, u32[]{:S(2)}, u32[]{:S(2)}) collective-permute-start(bf16[512,512]{1,0:T(8,128)(2,1)S(1)} %fusion.7), channel_id=1, source_target_pairs={{0,64},{64,0},{1,65},{65,1},{2,66},{66,2},{3,67},{67,3},{4,68},{68... | collective-permute-start | bytes 1572872 | tf_op jit(solution)/shard_map/ppermute | solution.py:407
  212.7 5.7 %collective-permute-start.8 = (bf16[512,1792]{1,0:T(8,128)(2,1)S(1)}, bf16[512,1792]{1,0:T(8,128)(2,1)S(1)}, u32[]{:S(2)}, u32[]{:S(2)}) collective-permute-start(bf16[512,1792]{1,0:T(8,128)(2,1)S(1)} %bitcast.46), channel_id=1, source_target_pairs={{0,32},{32,0},{1,33},{33,1},{2,34},{34,2},{3,35},{35,3},{4,36},{36... | collective-permute-start | bytes 5505032 | tf_op jit(solution)/shard_map/ppermute | solution.py:407

commit v4 on v3

--- a/solution.py
+++ b/solution.py
@@ -30,40 +30,52 @@
 
 def attn_kernel(pair, core, x0, x1, x2, x3, cot0, cot1, wqkv, wo, *rest):
     if pair:
-        g_first, keep, got, joint_o, mixed_o, part_o = rest[:6]
-        rest = rest[6:]
-    else:
-        grad_o, mixed_o, part_o = rest[:3]
+        g_first, keep, got = rest[:3]
         rest = rest[3:]
-    k_s, v_s, kt_s, vt_s, qt_s, dmt_s, s_s, e_s, dka, dva, mt_s, dqt_s = rest
-    xs = (x0, x1, x2, x3)
-    cots = (cot0, cot1)
+    grad_o, mixed_o, part_o, x_s, cot_s, w_s, wo_s, grad_s, part_s, mix_s, edge_s, sems = rest[:12]
+    k_s, v_s, kt_s, vt_s, qt_s, dmt_s, s_s, e_s, dka, dva, mt_s, dqt_s = rest[12:]
     n = x0.shape[0]
-    seq = n * len(xs)
-    nq = n * len(cots)
-
-    def of(refs, r):
-        return refs[r.start // n][r.start % n : r.start % n + CK, :]
-
+    seq = x_s.shape[0]
+    nq = cot_s.shape[0]
     chunks = [slice(c * CK, c * CK + CK) for c in range(seq // CK)]
     scale = 0.125
     c2 = scale * LOG2E
     off = pl.multiple_of(core[0] * 256 + pair * 128, 128)
-    wq = wqkv[:, pl.ds(off, 128)]
-    wk = wqkv[:, pl.ds(pl.multiple_of(off + 512, 128), 128)]
-    wv = wqkv[:, pl.ds(pl.multiple_of(off + 1024, 128), 128)]
-    wo_own = wo[pl.ds(off, 128), :]
-    wkv = jnp.concatenate([wk, wv], axis=1)
+    fetch = []
+
+    def start(src, dst):
+        fetch.append(pltpu.make_async_copy(src, dst, sems.at[len(fetch)]))
+        fetch[-1].start()
+
+    for i in range(3):
+        start(wqkv.at[:, pl.ds(pl.multiple_of(off + 512 * i, 128), 128)], w_s.at[:, i * 128 : i * 128 + 128])
+    for i, src in enumerate((x0, x1, x2, x3)):
+        start(src, x_s.at[i * n : i * n + n, :])
+    start(wo.at[pl.ds(off, 128), :], wo_s)
+    for i, src in enumerate((cot0, cot1)):
+        start(src, cot_s.at[i * n : i * n + n, :])
+    if pair:
+        start(g_first, grad_s.at[:, :512])
+        start(keep, edge_s.at[0])
+        start(got, edge_s.at[1])
+    for copy in fetch[:3]:
+        copy.wait()
+    wq = w_s[:, :128]
+    wkv = w_s[:, 128:]
     for r in chunks:
-        kv = dot(of(xs, r), wkv, NN)
+        if r.start % n == 0:
+            fetch[3 + r.start // n].wait()
+        kv = dot(x_s[r, :], wkv, NN)
         k_s[r, :] = kv[:, :128].astype(BF)
         v_s[r, :] = kv[:, 128:].astype(BF)
         kvt = kv.T
         kt_s[:, r] = kvt[:128].astype(BF)
         vt_s[:, r] = kvt[128:].astype(BF)
+    for copy in fetch[7:]:
+        copy.wait()
     for r in chunks[: nq // CK]:
-        qt_s[:, r] = dot(of(xs, r), wq, NN).T.astype(BF)
-        dmt_s[:, r] = dot(of(cots, r), wo_own, NT).T.astype(BF)
+        qt_s[:, r] = dot(x_s[r, :], wq, NN).T.astype(BF)
+        dmt_s[:, r] = dot(cot_s[r, :], wo_s[...], NT).T.astype(BF)
     row = lax.broadcasted_iota(jnp.int32, (128, QB), 0)
     heads = [slice(h * 64, h * 64 + 64) for h in range(2)]
     lanes = [slice(h * QB, h * QB + QB) for h in range(2)]
@@ -139,30 +151,40 @@
             next(coming, None)
         for _ in coming:
             pass
-    dqt = dqt_s[...].astype(BF)
-    dkt = dka[...].astype(BF)
-    dvt = dva[...].astype(BF)
-
-    def over(lhs, refs):
-        return sum(dot(lhs[:, i * n : i * n + n], ref[...], NN) for i, ref in enumerate(refs))
-
-    grads = (over(dqt, xs[: len(cots)]), over(dkt, xs), over(dvt, xs), over(mt_s[...], cots))
-    for i, g in enumerate(grads):
-        if pair:
-            joint_o[i * 128 : i * 128 + 128, 512:1024] = g.astype(BF)
-        else:
-            grad_o[i * 128 : i * 128 + 128, :] = g.astype(BF)
-    if pair:
-        joint_o[:, :512] = g_first[...]
-        joint_o[:, 1024:] = (keep[...].astype(F32) + got[...].astype(F32)).astype(BF)
-    mixed_o[...] = mt_s[...].T
+    leave = []
+
+    def send(src, dst):
+        leave.append(pltpu.make_async_copy(src, dst, sems.at[13 + len(leave)]))
+        leave[-1].start()
+
+    mix_s[...] = mt_s[...].T
+    send(mix_s, mixed_o)
     dkv = jnp.concatenate([dka[...], dva[...]], axis=0).T.astype(BF)
     dq = dqt_s[...].T.astype(BF)
     for r in chunks:
         part = dot(dkv[r, :], wkv, NT)
         if r.start < nq:
             part = part + dot(dq[r, :], wq, NT)
-        part_o[r, :] = part.astype(BF)
+        part_s[r, :] = part.astype(BF)
+        if r.stop % n == 0:
+            send(part_s.at[r.stop - n : r.stop, :], part_o.at[r.stop - n : r.stop, :])
+    grads = (
+        dot(dqt_s[...].astype(BF), x_s[:nq, :], NN),
+        dot(dka[...].astype(BF), x_s[...], NN),
+        dot(dva[...].astype(BF), x_s[...], NN),
+        dot(mt_s[...], cot_s[...], NN),
+    )
+    for i, g in enumerate(grads):
+        grad_s[i * 128 : i * 128 + 128, pair * 512 : pair * 512 + 512] = g.astype(BF)
+    if pair:
+        grad_s[:, 1024:] = (edge_s[0].astype(F32) + edge_s[1].astype(F32)).astype(BF)
+    send(grad_s, grad_o)
+    for copy in leave:
+        copy.wait()
+
+
+def in_hbm(*arrays):
+    return [pltpu.with_memory_space_constraint(a, pltpu.HBM) for a in arrays]
 
 
 def attention(pair, core, xs, cots, wqkv, wo, *first):
@@ -170,36 +192,68 @@
     seq = n * len(xs)
     nq = n * len(cots)
     hw = 128
-    sd = jax.ShapeDtypeStruct
+    wide = 1792 if pair else 512
     V = pltpu.VMEM
-    vm = pl.BlockSpec(memory_space=pltpu.VMEM)
+    hbm = pl.BlockSpec(memory_space=pltpu.HBM)
     return pl.pallas_call(
         functools.partial(attn_kernel, pair),
-        out_shape=(sd((512, 1792 if pair else 512), BF), sd((nq, hw), BF), sd((seq, d), BF)),
-        in_specs=[pl.BlockSpec(memory_space=pltpu.SMEM)] + [vm] * (8 + len(first)),
-        out_specs=(vm,) * 3,
-        scratch_shapes=[V((seq, hw), BF)] * 2
+        out_shape=(pltpu.HBM((512, wide), BF), pltpu.HBM((nq, hw), BF), pltpu.HBM((seq, d), BF)),
+        in_specs=[pl.BlockSpec(memory_space=pltpu.SMEM)] + [hbm] * (8 + len(first)),
+        out_specs=(hbm,) * 3,
+        scratch_shapes=[V((seq, d), BF), V((nq, d), BF), V((d, 3 * hw), BF), V((hw, d), BF)]
+        + [V((512, wide), BF), V((seq, d), BF), V((nq, hw), BF), V((2, 512, 768) if pair else (2, 8, 128), BF)]
+        + [pltpu.SemaphoreType.DMA((19,))]
+        + [V((seq, hw), BF)] * 2
         + [V((hw, seq), BF)] * 2
         + [V((hw, nq), BF)] * 2
         + [V((2, seq, 2 * QB), F32), V((2, seq, 2 * QB), BF)]
         + [V((hw, seq), F32)] * 2
         + [V((hw, nq), BF), V((hw, nq), F32)],
-        compiler_params=pltpu.CompilerParams(vmem_limit_bytes=32 * MIB),
+        compiler_params=pltpu.CompilerParams(vmem_limit_bytes=40 * MIB),
         cost_estimate=pl.CostEstimate(flops=16 * 10**9, bytes_accessed=8 * MIB, transcendentals=4 * MIB),
         name="attention",
-    )(core, *xs, *cots, wqkv, wo, *first)
-
-
-def edges_kernel(core, idx, x, inc, cot, mask, wg, ws, base_o, local_o, remote_o, keep_o, give_o, a_s, b_s, gt_s, up_s, dsrc, dgate, e_s, *accs):
-    n, d = x.shape
-    rows = n + inc.shape[0]
+    )(core, *in_hbm(*xs, *cots, wqkv, wo, *first))
+
+
+def slots_kernel(slots, mask, idx, inv):
+    on = mask[...]
+    idx[...] = jnp.where(on > 0, slots[...], 1536) * 8
+    inv[...] = 1.0 / jnp.maximum(jnp.sum(on.astype(F32), axis=1, keepdims=True), 1.0)
+
+
+def read_slots(slots, mask):
+    vm = pl.BlockSpec(memory_space=pltpu.VMEM)
+    return pl.pallas_call(
+        slots_kernel,
+        out_shape=(jax.ShapeDtypeStruct(slots.shape, jnp.int32), jax.ShapeDtypeStruct((slots.shape[0], 1), F32)),
+        in_specs=[vm, vm],
+        out_specs=(vm, vm),
+        cost_estimate=pl.CostEstimate(flops=20 * 10**9, bytes_accessed=MIB, transcendentals=0),
+        name="slots",
+    )(slots, mask)
+
+
+def edges_kernel(core, idx, inv, x_i, inc_i, cot_i, wg_i, ws_i, base_o, local_o, remote_o, keep_o, give_o, *rest):
+    tab, cot, wg, ws, base_s, local_s, remote_s, pair_s, sems, a_s, b_s, gt_s, up_s, dsrc, dgate, e_s = rest[:16]
+    accs = rest[16:]
+    n, d = cot.shape
+    rows = tab.shape[0]
     R = 128
-
-    def fill(src, first):
+    fetch = []
+    for src, dst in ((ws_i, ws), (x_i, tab.at[:n, :]), (inc_i, tab.at[n:, :]), (wg_i, wg), (cot_i, cot)):
+        fetch.append(pltpu.make_async_copy(src, dst, sems.at[len(fetch)]))
+        fetch[-1].start()
+    leave = []
+
+    def send(src, dst):
+        leave.append(pltpu.make_async_copy(src, dst, sems.at[5 + len(leave)]))
+        leave[-1].start()
+
+    def fill(first, count):
         def step(i, _):
-            base = pl.multiple_of(i * R, R)
-            at = (base + first) * 8
-            t = dot(src[pl.ds(base, R), :], ws[...], NN)
+            base = pl.multiple_of(i * R + first, R)
+            at = base * 8
+            t = dot(tab[pl.ds(base, R), :], ws[...], NN)
             for c in range(4):
                 g = t[:, c * 128 : c * 128 + 128] * 0.5
                 v = t[:, 512 + c * 128 : 512 + c * 128 + 128]
@@ -211,21 +265,22 @@
                 acc[pl.ds(pl.multiple_of(at, 8), R * 8), :] = jnp.zeros((R * 8, 128), F32)
             return 0
 
-        lax.fori_loop(0, src.shape[0] // R, step, 0)
-
-    fill(x, 0)
-    fill(inc, n)
+        lax.fori_loop(0, count // R, step, 0)
+
+    fetch[0].wait()
+    fetch[1].wait()
+    fill(0, n)
+    fetch[2].wait()
+    fill(n, rows - n)
+    fetch[3].wait()
+    fetch[4].wait()
     for ref in (a_s, b_s, *accs):
         ref[pl.ds(rows * 8, 8), :] = jnp.zeros((8, 128), F32)
 
-    def inverse(base):
-        count = jnp.sum(mask[pl.ds(base, R), :].astype(F32), axis=1, keepdims=True)
-        return 1.0 / jnp.maximum(count, 1.0)
-
     def fill_nodes(i, _):
         base = pl.multiple_of(i * R, R)
-        t = dot(x[pl.ds(base, R), :], wg[...], NN) * 0.5
-        u = cot[pl.ds(base, R), :].astype(F32) * (inverse(base) * 0.25)
+        t = dot(tab[pl.ds(base, R), :], wg[...], NN) * 0.5
+        u = cot[pl.ds(base, R), :].astype(F32) * (inv[pl.ds(base, R), :] * 0.25)
         for c in range(4):
             cs = slice(c * 128, c * 128 + 128)
             for h in (0, 4):
@@ -271,15 +326,24 @@
                 v = v + acc[pl.ds(base * 8 + c, R, stride=8), :]
             dsrc[pl.ds(base, R), c * 128 : c * 128 + 128] = v.astype(BF)
 
+    def read_remote(i, _):
+        base = pl.multiple_of(i * R, R)
+        read(base + n)
+        remote_s[pl.ds(base, R), :] = dot(dsrc[pl.ds(base + n, R), :], ws[...], NT).astype(BF)
+        return 0
+
+    lax.fori_loop(0, (rows - n) // R, read_remote, 0)
+    send(remote_s, remote_o)
+
     def read_local(i, _):
         base = pl.multiple_of(i * R, R)
         read(base)
-        inv = inverse(base) * 0.5
+        weight = inv[pl.ds(base, R), :] * 0.5
         for c in range(4):
             cs = slice(c * 128, c * 128 + 128)
-            base_o[pl.ds(base, R), cs] = x[pl.ds(base, R), cs].astype(F32) + gt_s[pl.ds(base * 8 + c, R, stride=8), :] * inv
+            base_s[pl.ds(base, R), cs] = tab[pl.ds(base, R), cs].astype(F32) + gt_s[pl.ds(base * 8 + c, R, stride=8), :] * weight
             dgate[pl.ds(base, R), cs] = up_s[pl.ds(base * 8 + c, R, stride=8), :].astype(BF)
-        local_o[pl.ds(base, R), :] = (
+        local_s[pl.ds(base, R), :] = (
             cot[pl.ds(base, R), :].astype(F32)
             + dot(dsrc[pl.ds(base, R), :], ws[...], NT)
             + dot(dgate[pl.ds(base, R), :], wg[...], NT)
@@ -287,44 +351,44 @@
         return 0
 
     lax.fori_loop(0, n // R, read_local, 0)
-
-    def read_remote(i, _):
-        base = pl.multiple_of(i * R, R)
-        read(base + n)
-        remote_o[pl.ds(base, R), :] = dot(dsrc[pl.ds(base + n, R), :], ws[...], NT).astype(BF)
-        return 0
-
-    lax.fori_loop(0, inc.shape[0] // R, read_remote, 0)
-    xt = x[...].T
-    it = inc[...].T
+    send(base_s, base_o)
+    send(local_s, local_o)
+    tt = tab[...].T
     for c in range(4):
         cs = slice(c * 256, c * 256 + 256)
-        e_s[:, cs] = dot(xt, dsrc[:n, cs], NN) + dot(it, dsrc[n:, cs], NN)
-    e_s[:, 1024:] = dot(xt, dgate[...], NN)
+        e_s[:, cs] = dot(tt, dsrc[:, cs], NN)
+    e_s[:, 1024:] = dot(tt[:, :n], dgate[...], NN)
     half = e_s.shape[1] // 2
-    keep_o[...] = e_s[:, pl.ds(pl.multiple_of(core[0] * half, 128), half)].astype(BF)
-    give_o[...] = e_s[:, pl.ds(pl.multiple_of((1 - core[0]) * half, 128), half)].astype(BF)
-
-
-def edges(core, idx, x, inc, cot, mask, wg, ws):
+    pair_s[0] = e_s[:, pl.ds(pl.multiple_of((1 - core[0]) * half, 128), half)].astype(BF)
+    send(pair_s.at[0], give_o)
+    pair_s[1] = e_s[:, pl.ds(pl.multiple_of(core[0] * half, 128), half)].astype(BF)
+    send(pair_s.at[1], keep_o)
+    for copy in leave:
+        copy.wait()
+
+
+def edges(core, idx, inv, x, inc, cot, wg, ws):
     n, d = x.shape
     rows = n + inc.shape[0]
-    sd = jax.ShapeDtypeStruct
+    H = pltpu.HBM
     V = pltpu.VMEM
-    vm = pl.BlockSpec(memory_space=pltpu.VMEM)
+    hbm = pl.BlockSpec(memory_space=pltpu.HBM)
     sm = pl.BlockSpec(memory_space=pltpu.SMEM)
     table = V(((rows + 1) * 8, 128), F32)
     per_node = V((n * 8, 128), F32)
     return pl.pallas_call(
         edges_kernel,
-        out_shape=(sd((n, d), F32), sd((n, d), F32), sd(inc.shape, BF), sd((d, 768), BF), sd((d, 768), BF)),
-        in_specs=[sm, sm] + [vm] * 6,
-        out_specs=(vm,) * 5,
-        scratch_shapes=[table, table, per_node, per_node, V((rows, 2 * d), BF), V((n, d), BF), V((d, 3 * d), F32)] + [table] * NACC,
-        compiler_params=pltpu.CompilerParams(vmem_limit_bytes=48 * MIB),
+        out_shape=(H((n, d), F32), H((n, d), F32), H(inc.shape, BF), H((d, 768), BF), H((d, 768), BF)),
+        in_specs=[sm, sm, pl.BlockSpec(memory_space=pltpu.VMEM)] + [hbm] * 5,
+        out_specs=(hbm,) * 5,
+        scratch_shapes=[V((rows, d), BF), V((n, d), BF), V(wg.shape, BF), V(ws.shape, BF)]
+        + [V((n, d), F32), V((n, d), F32), V(inc.shape, BF), V((2, d, 768), BF), pltpu.SemaphoreType.DMA((10,))]
+        + [table, table, per_node, per_node, V((rows, 2 * d), BF), V((n, d), BF), V((d, 3 * d), F32)]
+        + [table] * NACC,
+        compiler_params=pltpu.CompilerParams(vmem_limit_bytes=56 * MIB),
         cost_estimate=pl.CostEstimate(flops=20 * 10**9, bytes_accessed=8 * MIB, transcendentals=4 * MIB),
         name="edges",
-    )(core, idx, x, inc, cot, mask, wg, ws)
+    )(core, idx, inv, *in_hbm(x, inc, cot, wg, ws))
 
 
 def spread_kernel(got, out):
@@ -423,14 +487,17 @@
     cot_sib = swap(cot, "c")
     rows = send_rows.reshape(-1)
     pick = (rows[:, None] == lax.broadcasted_iota(jnp.int32, (rows.shape[0], n), 1)).astype(BF)
-    incoming = domains(dot(pick, x, NN).astype(BF))
+    outgoing = dot(pick, x, NN).astype(BF)
+    incoming = domains(outgoing)
     x_far_sib = swap(x_far, "c")
     xs = (x, x_sib, x_far, x_far_sib)
     cots = (cot, cot_sib)
-    grad_first, mixed_first, part_first = attention(0, core, xs, cots, wqkv, wo)
-    idx = (jnp.where(mask > 0, slots, 3 * n) * 8).reshape(-1)
+    slot_rows, inv = read_slots(slots, mask)
+    idx = slot_rows.reshape(-1)
+    early, idx = lax.optimization_barrier((core, idx))
+    grad_first, mixed_first, part_first = attention(0, early, xs, cots, wqkv, wo)
     incoming, grad_first = lax.optimization_barrier((incoming, grad_first))
-    base, local, remote, keep, give = edges(core, idx, x, incoming, cot, mask, wg, ws)
+    base, local, remote, keep, give = edges(core, idx, inv, x, incoming, cot, wg, ws)
     returned = domains(remote)
     got = swap(give, "c")
     joint, mixed_second, part_second = attention(1, core, xs, cots, wqkv, wo, grad_first, keep, got)

time: 225 us -> 197 us (0.88)
  local copies, waits for them, and re-layouts: 35 us -> 13.2 us
  waiting for transfers between devices: 53.1 us -> 40.7 us
  Pallas kernels: 70.9 us -> 79.7 us
    unnamed x80 -> x37, local copies, waits for them, and re-layouts: 32.7 us -> 9.49 us
    ppermute x9, waiting for transfers between devices: 34.3 us -> 23.2 us  [swap(): return lax.ppermute(a, axis, SWAP)]
    pallas_call x3 -> x4, Pallas kernels: 63.8 us -> 72.6 us  [the longest x2 39.3 us: attention(): pl.pallas_call(functools.partial(attn_kernel, pair), out_shape=(pltpu.HBM...]
  transfers between devices with their start and end apart: 13 -> 13, of which waited for: 4 -> 3; matrix products, arithmetic and copies ran while one was open for 7% -> 9% of each run, Pallas kernels for 17% -> 24%
where the time goes in v4:
time: 197 us; the launch traced here: 194 us
  Pallas kernels  79.7 us (40%)
  starting transfers between devices  48.1 us (24%)
  waiting for transfers between devices  40.7 us (21%)
  local copies, waits for them, and re-layouts  13.2 us (7%)
  matrix products  6.55 us (3%)
  other arithmetic  4.73 us (2%)
    pallas_call x2, Pallas kernels, attention(): pl.pallas_call(functools.partial(attn_kernel, pair), out_shape=(pltpu.HBM...  39.3 us
    pallas_call x1, Pallas kernels, edges(): pl.pallas_call(edges_kernel, out_shape=(H((n, d), F32), H((n, d), F32), H...  31.4 us
    ppermute x9, waiting for transfers between devices, swap(): return lax.ppermute(a, axis, SWAP)  23.2 us
    all_to_all x2, starting transfers between devices, domains(): lax.all_to_all(a.reshape(32, 32, -1), DOM, 0, 0, tiled=True)  20.1 us
    all_to_all x2, waiting for transfers between devices, chips(): return lax.all_to_all(a, CHIPS, 0, 0, tiled=True)  17.5 us
    all_to_all x2, starting transfers between devices, chips(): return lax.all_to_all(a, CHIPS, 0, 0, tiled=True)  15.3 us
    ppermute x9, starting transfers between devices, swap(): return lax.ppermute(a, axis, SWAP)  12.6 us
    unnamed x37, local copies, waits for them, and re-layouts  9.49 us
  transfers between devices with their start and end apart: 13, of which 3 were waited for; matrix products, arithmetic and copies ran while one was open for 9% of the time, Pallas kernels for 24%

profile of v4, /device:TPU:1, one launch (start us, length us, event | category | flops | bytes accessed | tf_op | source)
XLA Modules:
  0.0 194.1 jit_solution(17722866717617570379)
XLA Ops:
  0.6 2.1 %collective-permute-start.1 = (bf16[512,512]{1,0:T(8,128)(2,1)}, bf16[512,512]{1,0:T(8,128)(2,1)S(1)}, u32[]{:S(2)}, u32[]{:S(2)}) collective-permute-start(bf16[512,512]{1,0:T(8,128)(2,1)} %x0.3), channel_id=1, source_target_pairs={{0,64},{64,0},{1,65},{65,1},{2,66},{66,2},{3,67},{67,3},{4,68},{68... | collective-permute-start | bytes 1572872 | tf_op jit(solution)/shard_map/ppermute | solution.py:471
  2.8 1.0 collective-permute-start
  3.7 0.0 collective-permute-start.3
  3.7 0.8 eq.10
  4.5 2.8 %fusion.2 = bf16[1024,512]{1,0:T(8,128)(2,1)} fusion(bf16[512,512]{1,0:T(8,128)(2,1)} %x0.3, s32[1024]{0:T(1024)S(1)} %eq.10), kind=kOutput, calls=%fused_computation.5 | convolution fusion | flops 537919488 | bytes 1576960 | tf_op jit(solution)/shard_map/dot_general | solution.py:28
  7.3 10.2 %all-to-all-start = ((bf16[32,32,512]{2,1,0:T(8,128)(2,1)}), bf16[32,32,512]{2,1,0:T(8,128)(2,1)S(1)}, u32[]{:S(2)}, u32[]{:S(2)}) async-start(bf16[32,32,512]{2,1,0:T(8,128)(2,1)} %bitcast.1), calls=%async_computation | async-start | bytes 2097152 | tf_op jit(solution)/shard_map/all_to_all | solution.py:479
  17.5 0.0 copy-done.10
  17.5 0.8 copy.22.slots
  18.4 0.8 copy.23.mask
  19.2 0.0 collective-permute-done.1.x2
  19.2 0.9 collective-permute-start.2
  20.1 1.9 slots.2
  22.0 0.0 copy-done.13
  22.0 1.7 reshape.47.idx
  23.7 0.0 collective-permute-done.3.cot1
  23.7 0.0 collective-permute-done.x1
  23.7 0.0 copy-start.14
  23.7 0.0 collective-permute-done.2.x3
  23.7 0.8 copy-done.15
  24.5 0.2 copy-done.14
  24.7 0.8 copy-done.16
  25.5 19.3 %attention.2 = (bf16[512,512]{1,0:T(8,128)(2,1)}, bf16[1024,128]{1,0:T(8,128)(2,1)}, bf16[2048,512]{1,0:T(8,128)(2,1)}) custom-call(s32[1]{0:T(128)} %bitcast.core.refs_0_, bf16[512,512]{1,0:T(8,128)(2,1)} %x0.3, bf16[512,512]{1,0:T(8,128)(2,1)} %copy-done.14, bf16[512,512]{1,0:T(8,128)(2,1)} %copy-done.13, bf16[512,512]{1,0:T(8,128)(2,1)} %copy-done.16, ...), custom_call_target="tpu_custom_call" | custom-call | flops 16000000000 | bytes 8388608 | tf_op jit(solution)/shard_map/attention/pallas_call | solution.py:198
  44.8 0.0 all-to-all-done
  44.8 0.0 copy-start.6
  44.8 1.0 copy-done.6
  45.8 31.4 %edges.1 = (f32[512,512]{1,0:T(8,128)}, f32[512,512]{1,0:T(8,128)}, bf16[1024,512]{1,0:T(8,128)(2,1)}, bf16[512,768]{1,0:T(8,128)(2,1)}, bf16[512,768]{1,0:T(8,128)(2,1)}) custom-call(s32[1]{0:T(128)} %bitcast.core.refs_0_, s32[4096]{0:T(1024)} %reshape.47.idx, f32[512,1]{1,0:T(8,128)} %get-tuple-element.41.inv, bf16[512,512]{1,0:T(8,128)(2,1)} %x0.3, ...), custom_call_target="tpu_custom_call" | custom-call | flops 20000000000 | bytes 8388608 | tf_op jit(solution)/shard_map/edges/pallas_call | solution.py:379
  77.1 0.1 collective-permute-start.4
  77.3 9.9 %all-to-all-start.1 = ((bf16[32,32,512]{2,1,0:T(8,128)(2,1)}), bf16[32,32,512]{2,1,0:T(8,128)(2,1)S(1)}, u32[]{:S(2)}, u32[]{:S(2)}) async-start(bf16[32,32,512]{2,1,0:T(8,128)(2,1)} %bitcast.54), calls=%async_computation.1 | async-start | bytes 2097152 | tf_op jit(solution)/shard_map/all_to_all | solution.py:479
  87.2 0.0 collective-permute-done.4.rest_2_
  87.2 0.0 copy-start.12
  87.2 0.9 copy-done.12
  88.1 20.0 %attention.3 = (bf16[512,1792]{1,0:T(8,128)(2,1)}, bf16[1024,128]{1,0:T(8,128)(2,1)}, bf16[2048,512]{1,0:T(8,128)(2,1)}) custom-call(s32[1]{0:T(128)} %bitcast.core.refs_0_, bf16[512,512]{1,0:T(8,128)(2,1)} %x0.3, bf16[512,512]{1,0:T(8,128)(2,1)} %copy-done.14, bf16[512,512]{1,0:T(8,128)(2,1)} %copy-done.13, bf16[512,512]{1,0:T(8,128)(2,1)} %copy-done.16, ...), custom_call_target="tpu_custom_call" | custom-call | flops 16000000000 | bytes 8388608 | tf_op jit(solution)/shard_map/attention/pallas_call | solution.py:198
  108.1 0.0 all-to-all-done.1
  108.2 0.0 copy-start.5
  108.2 1.0 copy-done.5
  109.1 9.8 %all-to-all-start.2 = ((bf16[64,8,1792]{2,1,0:T(8,128)(2,1)}), bf16[64,8,1792]{2,1,0:T(8,128)(2,1)S(1)}, u32[]{:S(2)}, u32[]{:S(2)}) async-start(bf16[64,8,1792]{2,1,0:T(8,128)(2,1)} %bitcast.51), calls=%async_computation.2 | async-start | bytes 3670016 | tf_op jit(solution)/shard_map/all_to_all | solution.py:475
  119.0 2.8 %convert_add_fusion = f32[2048,512]{1,0:T(8,128)S(1)} fusion(bf16[2048,512]{1,0:T(8,128)(2,1)} %get-tuple-element.53, bf16[2048,512]{1,0:T(8,128)(2,1)} %get-tuple-element.52), kind=kLoop, calls=%fused_computation | loop fusion | flops 3145728 | bytes 8388608 | tf_op jit(solution)/shard_map/add | solution.py:513
  121.8 2.0 %copy-done = f32[2048,512]{1,0:T(8,128)} copy-done((f32[2048,512]{1,0:T(8,128)}, f32[2048,512]{1,0:T(8,128)S(1)}, u32[]{:S(2)}) %copy-start) | copy-done | bytes 4194328
  123.8 1.2 fusion.5
  125.0 1.3 collective-permute-start.6
  126.3 17.5 %all-to-all-done.2.got = bf16[64,8,1792]{2,1,0:T(8,128)(2,1)S(1)} async-done(((bf16[64,8,1792]{2,1,0:T(8,128)(2,1)}), bf16[64,8,1792]{2,1,0:T(8,128)(2,1)S(1)}, u32[]{:S(2)}, u32[]{:S(2)}) %all-to-all-start.2) | async-done | bytes 1835040 | tf_op jit(solution)/shard_map/all_to_all | solution.py:475
  143.8 1.2 copy-done.2
  145.0 3.0 %sum_spread.1 = bf16[64,8,1792]{2,1,0:T(8,128)(2,1)} custom-call(bf16[64,8,1792]{2,1,0:T(8,128)(2,1)} %copy-done.2), custom_call_target="tpu_custom_call" | custom-call | flops 917504 | bytes 3670016 | tf_op jit(solution)/shard_map/sum_spread/pallas_call | solution.py:401
  148.1 5.5 %all-to-all-start.3 = ((bf16[64,8,1792]{2,1,0:T(8,128)(2,1)}), bf16[64,8,1792]{2,1,0:T(8,128)(2,1)S(1)}, u32[]{:S(2)}, u32[]{:S(2)}) async-start(bf16[64,8,1792]{2,1,0:T(8,128)(2,1)} %sum_spread.1), calls=%async_computation.3 | async-start | bytes 3670016 | tf_op jit(solution)/shard_map/all_to_all | solution.py:475
  153.6 0.1 constant_dynamic-update-slice_fusion
  153.7 2.4 %collective-permute-start.5 = (bf16[512,256]{1,0:T(8,128)(2,1)S(1)}, bf16[512,256]{1,0:T(8,128)(2,1)S(1)}, u32[]{:S(2)}, u32[]{:S(2)}) collective-permute-start(bf16[512,256]{1,0:T(8,128)(2,1)S(1)} %slice.30), channel_id=1, source_target_pairs={{0,32},{32,0},{1,33},{33,1},{2,34},{34,2},{3,35},{35,3},{4,36},{36... | collective-permute-start | bytes 786440 | tf_op jit(solution)/shard_map/ppermute | solution.py:471
  156.2 2.4 %fusion = f32[512,512]{1,0:T(8,128)S(1)} fusion(bf16[1024,512]{1,0:T(8,128)(2,1)} %bitcast.52, s32[1024]{0:T(1024)S(1)} %eq.10), kind=kOutput, calls=%fused_computation.3 | convolution fusion | flops 537395200 | bytes 2101248 | tf_op jit(solution)/shard_map/dot_general | solution.py:28
  158.5 0.0 collective-permute-done.6
  158.5 0.3 convert_element_type.34
  158.8 0.0 copy-start.7
  158.9 0.0 copy-start.4
  158.9 0.3 fusion.7
  159.1 1.5 collective-permute-start.7
  160.6 0.0 collective-permute-done.5
  160.6 0.0 copy-done.7
  160.6 0.3 fusion.16
  160.9 1.1 fusion.4
  162.0 21.8 %collective-permute-done.7 = bf16[512,512]{1,0:T(8,128)(2,1)S(1)} collective-permute-done((bf16[512,512]{1,0:T(8,128)(2,1)S(1)}, bf16[512,512]{1,0:T(8,128)(2,1)S(1)}, u32[]{:S(2)}, u32[]{:S(2)}) %collective-permute-start.7) | collective-permute-done | bytes 524320 | tf_op jit(solution)/shard_map/ppermute | solution.py:471
  183.8 1.4 fusion.11
  185.1 0.0 all-to-all-done.3
  185.2 3.3 %collective-permute-start.8 = (bf16[512,1792]{1,0:T(8,128)(2,1)S(1)}, bf16[512,1792]{1,0:T(8,128)(2,1)S(1)}, u32[]{:S(2)}, u32[]{:S(2)}) collective-permute-start(bf16[512,1792]{1,0:T(8,128)(2,1)S(1)} %bitcast.46), channel_id=1, source_target_pairs={{0,32},{32,0},{1,33},{33,1},{2,34},{34,2},{3,35},{35,3},{4,36},{36... | collective-permute-start | bytes 5505032 | tf_op jit(solution)/shard_map/ppermute | solution.py:471
  188.4 2.0 %place.2 = (f32[512,512]{1,0:T(8,128)}, f32[512,1024]{1,0:T(8,128)}, f32[512,1536]{1,0:T(8,128)}, f32[512,512]{1,0:T(8,128)}) custom-call(s32[1]{0:T(128)} %bitcast.core.refs_0_, bf16[512,1792]{1,0:T(8,128)(2,1)S(1)} %bitcast.47), custom_call_target="tpu_custom_call" | custom-call | tf_op jit(solution)/shard_map/place/pallas_call | solution.py:458
  190.5 1.4 collective-permute-done.8.refs_1_
  191.8 2.0 %place.3 = (f32[512,512]{1,0:T(8,128)}, f32[512,1024]{1,0:T(8,128)}, f32[512,1536]{1,0:T(8,128)}, f32[512,512]{1,0:T(8,128)}) custom-call(s32[1]{0:T(128)} %bitcast.core.refs_0_, bf16[512,1792]{1,0:T(8,128)(2,1)S(1)} %collective-permute-done.8.refs_1_, ...), custom_call_target="tpu_custom_call", output_to_operand_aliasing={{0}: (2, {}), {1}: (3, {}), {2}: (4, {}), {3}: (5, {})} | custom-call | tf_op jit(solution)/shard_map/place/pallas_call | solution.py:458
  (19 shorter events, 0.1 us)
Async XLA Ops:
  0.6 18.6 %collective-permute-start.1 = (bf16[512,512]{1,0:T(8,128)(2,1)}, bf16[512,512]{1,0:T(8,128)(2,1)S(1)}, u32[]{:S(2)}, u32[]{:S(2)}) collective-permute-start(bf16[512,512]{1,0:T(8,128)(2,1)} %x0.3), channel_id=1, source_target_pairs={{0,64},{64,0},{1,65},{65,1},{2,66},{66,2},{3,67},{67,3},{4,68},{68... | collective-permute-start | bytes 1572872 | tf_op jit(solution)/shard_map/ppermute | solution.py:471
  2.8 21.0 %collective-permute-start = (bf16[512,512]{1,0:T(8,128)(2,1)}, bf16[512,512]{1,0:T(8,128)(2,1)S(1)}, u32[]{:S(2)}, u32[]{:S(2)}) collective-permute-start(bf16[512,512]{1,0:T(8,128)(2,1)} %x0.3), channel_id=1, source_target_pairs={{0,32},{32,0},{1,33},{33,1},{2,34},{34,2},{3,35},{35,3},{4,36},{36... | collective-permute-start | bytes 1572872 | tf_op jit(solution)/shard_map/ppermute | solution.py:471
  3.7 20.0 %collective-permute-start.3 = (bf16[512,512]{1,0:T(8,128)(2,1)}, bf16[512,512]{1,0:T(8,128)(2,1)S(1)}, u32[]{:S(2)}, u32[]{:S(2)}) collective-permute-start(bf16[512,512]{1,0:T(8,128)(2,1)} %cot0.3), channel_id=1, source_target_pairs={{0,32},{32,0},{1,33},{33,1},{2,34},{34,2},{3,35},{35,3},{4,36},{36... | collective-permute-start | bytes 1572872 | tf_op jit(solution)/shard_map/ppermute | solution.py:471
  4.5 13.0 %copy-start.10 = (s32[512,8]{0,1:T(8,128)S(1)}, s32[512,8]{0,1:T(8,128)}, u32[]{:S(2)}) copy-start(s32[512,8]{0,1:T(8,128)} %param.11) | copy-start | bytes 49156
  4.5 13.9 %copy-start.11 = (s32[512,8]{0,1:T(8,128)S(1)}, s32[512,8]{0,1:T(8,128)}, u32[]{:S(2)}) copy-start(s32[512,8]{0,1:T(8,128)} %param.12) | copy-start | bytes 49156
  7.3 37.5 %all-to-all-start = ((bf16[32,32,512]{2,1,0:T(8,128)(2,1)}), bf16[32,32,512]{2,1,0:T(8,128)(2,1)S(1)}, u32[]{:S(2)}, u32[]{:S(2)}) async-start(bf16[32,32,512]{2,1,0:T(8,128)(2,1)} %bitcast.1), calls=%async_computation | async-start | bytes 2097152 | tf_op jit(solution)/shard_map/all_to_all | solution.py:479
  19.2 2.8 %copy-start.13 = (bf16[512,512]{1,0:T(8,128)(2,1)}, bf16[512,512]{1,0:T(8,128)(2,1)S(1)}, u32[]{:S(2)}) copy-start(bf16[512,512]{1,0:T(8,128)(2,1)S(1)} %collective-permute-done.1.x2) | copy-start | bytes 1572868
  19.2 4.5 %collective-permute-start.2 = (bf16[512,512]{1,0:T(8,128)(2,1)S(1)}, bf16[512,512]{1,0:T(8,128)(2,1)S(1)}, u32[]{:S(2)}, u32[]{:S(2)}) collective-permute-start(bf16[512,512]{1,0:T(8,128)(2,1)S(1)} %collective-permute-done.1.x2), channel_id=1, source_target_pairs={{0,32},{32,0},{1,33},{33,1},{2,34},{34,2},{3,35},{35,3},{4,36},{36... | collective-permute-start | bytes 1572872 | tf_op jit(solution)/shard_map/ppermute | solution.py:471
  23.7 0.8 copy-start.15
  23.7 1.0 copy-start.14
  24.7 0.8 copy-start.16
  44.8 1.0 copy-start.6
  77.1 10.1 %collective-permute-start.4 = (bf16[512,768]{1,0:T(8,128)(2,1)}, bf16[512,768]{1,0:T(8,128)(2,1)S(1)}, u32[]{:S(2)}, u32[]{:S(2)}) collective-permute-start(bf16[512,768]{1,0:T(8,128)(2,1)} %get-tuple-element.44), channel_id=1, source_target_pairs={{0,32},{32,0},{1,33},{33,1},{2,34},{34,2},{3,35},{35,3},{4,36},{36... | collective-permute-start | bytes 2359304 | tf_op jit(solution)/shard_map/ppermute | solution.py:471
  77.3 30.9 %all-to-all-start.1 = ((bf16[32,32,512]{2,1,0:T(8,128)(2,1)}), bf16[32,32,512]{2,1,0:T(8,128)(2,1)S(1)}, u32[]{:S(2)}, u32[]{:S(2)}) async-start(bf16[32,32,512]{2,1,0:T(8,128)(2,1)} %bitcast.54), calls=%async_computation.1 | async-start | bytes 2097152 | tf_op jit(solution)/shard_map/all_to_all | solution.py:479
  87.2 0.9 copy-start.12
  108.2 1.0 copy-start.5
  109.1 34.6 %all-to-all-start.2 = ((bf16[64,8,1792]{2,1,0:T(8,128)(2,1)}), bf16[64,8,1792]{2,1,0:T(8,128)(2,1)S(1)}, u32[]{:S(2)}, u32[]{:S(2)}) async-start(bf16[64,8,1792]{2,1,0:T(8,128)(2,1)} %bitcast.51), calls=%async_computation.2 | async-start | bytes 3670016 | tf_op jit(solution)/shard_map/all_to_all | solution.py:475
  121.8 2.0 %copy-start = (f32[2048,512]{1,0:T(8,128)}, f32[2048,512]{1,0:T(8,128)S(1)}, u32[]{:S(2)}) copy-start(f32[2048,512]{1,0:T(8,128)S(1)} %convert_add_fusion) | copy-start | bytes 12582916
  125.0 33.5 %collective-permute-start.6 = (bf16[2,512,512]{2,1,0:T(8,128)(2,1)}, bf16[2,512,512]{2,1,0:T(8,128)(2,1)S(1)}, u32[]{:S(2)}, u32[]{:S(2)}) collective-permute-start(bf16[2,512,512]{2,1,0:T(8,128)(2,1)} %fusion.5), channel_id=1, source_target_pairs={{0,32},{32,0},{1,33},{33,1},{2,34},{34,2},{3,35},{35,3},{4,36},{36... | collective-permute-start | bytes 3145736 | tf_op jit(solution)/shard_map/ppermute | solution.py:471
  143.8 1.2 copy-start.2
  148.1 5.5 %copy-start.8 = (bf16[1024,128]{1,0:T(8,128)(2,1)S(1)}, bf16[1024,128]{1,0:T(8,128)(2,1)}, u32[]{:S(2)}) copy-start(bf16[1024,128]{1,0:T(8,128)(2,1)} %get-tuple-element.49) | copy-start | bytes 786436
  148.1 5.6 %copy-start.9 = (bf16[1024,128]{1,0:T(8,128)(2,1)S(1)}, bf16[1024,128]{1,0:T(8,128)(2,1)}, u32[]{:S(2)}) copy-start(bf16[1024,128]{1,0:T(8,128)(2,1)} %get-tuple-element.50) | copy-start | bytes 786436
  148.1 37.1 %all-to-all-start.3 = ((bf16[64,8,1792]{2,1,0:T(8,128)(2,1)}), bf16[64,8,1792]{2,1,0:T(8,128)(2,1)S(1)}, u32[]{:S(2)}, u32[]{:S(2)}) async-start(bf16[64,8,1792]{2,1,0:T(8,128)(2,1)} %sum_spread.1), calls=%async_computation.3 | async-start | bytes 3670016 | tf_op jit(solution)/shard_map/all_to_all | solution.py:475
  153.7 6.9 %collective-permute-start.5 = (bf16[512,256]{1,0:T(8,128)(2,1)S(1)}, bf16[512,256]{1,0:T(8,128)(2,1)S(1)}, u32[]{:S(2)}, u32[]{:S(2)}) collective-permute-start(bf16[512,256]{1,0:T(8,128)(2,1)S(1)} %slice.30), channel_id=1, source_target_pairs={{0,32},{32,0},{1,33},{33,1},{2,34},{34,2},{3,35},{35,3},{4,36},{36... | collective-permute-start | bytes 786440 | tf_op jit(solution)/shard_map/ppermute | solution.py:471
  156.2 2.7 %copy-start.1 = (f32[2048,512]{1,0:T(8,128)S(1)}, f32[2048,512]{1,0:T(8,128)}, u32[]{:S(2)}) copy-start(f32[2048,512]{1,0:T(8,128)} %copy-done) | copy-start | bytes 12582916
  158.8 1.8 copy-start.7
  158.9 2.1 %copy-start.4 = (f32[512,512]{1,0:T(8,128)S(1)}, f32[512,512]{1,0:T(8,128)}, u32[]{:S(2)}) copy-start(f32[512,512]{1,0:T(8,128)} %get-tuple-element.48) | copy-start | bytes 3145732
  159.1 24.7 %collective-permute-start.7 = (bf16[512,512]{1,0:T(8,128)(2,1)S(1)}, bf16[512,512]{1,0:T(8,128)(2,1)S(1)}, u32[]{:S(2)}, u32[]{:S(2)}) collective-permute-start(bf16[512,512]{1,0:T(8,128)(2,1)S(1)} %fusion.7), channel_id=1, source_target_pairs={{0,64},{64,0},{1,65},{65,1},{2,66},{66,2},{3,67},{67,3},{4,68},{68... | collective-permute-start | bytes 1572872 | tf_op jit(solution)/shard_map/ppermute | solution.py:471
  160.6 23.2 %copy-start.3 = (f32[512,512]{1,0:T(8,128)S(1)}, f32[512,512]{1,0:T(8,128)}, u32[]{:S(2)}) copy-start(f32[512,512]{1,0:T(8,128)} %get-tuple-element.51) | copy-start | bytes 3145732
  185.2 6.7 %collective-permute-start.8 = (bf16[512,1792]{1,0:T(8,128)(2,1)S(1)}, bf16[512,1792]{1,0:T(8,128)(2,1)S(1)}, u32[]{:S(2)}, u32[]{:S(2)}) collective-permute-start(bf16[512,1792]{1,0:T(8,128)(2,1)S(1)} %bitcast.46), channel_id=1, source_target_pairs={{0,32},{32,0},{1,33},{33,1},{2,34},{34,2},{3,35},{35,3},{4,36},{36... | collective-permute-start | bytes 5505032 | tf_op jit(solution)/shard_map/ppermute | solution.py:471

commit v5 on v4

--- a/solution.py
+++ b/solution.py
@@ -73,6 +73,8 @@
         vt_s[:, r] = kvt[128:].astype(BF)
     for copy in fetch[7:]:
         copy.wait()
+    if pair:
+        grad_s[:, 1024:] = (edge_s[0].astype(F32) + edge_s[1].astype(F32)).astype(BF)
     for r in chunks[: nq // CK]:
         qt_s[:, r] = dot(x_s[r, :], wq, NN).T.astype(BF)
         dmt_s[:, r] = dot(cot_s[r, :], wo_s[...], NT).T.astype(BF)
@@ -169,16 +171,15 @@
         if r.stop % n == 0:
             send(part_s.at[r.stop - n : r.stop, :], part_o.at[r.stop - n : r.stop, :])
     grads = (
-        dot(dqt_s[...].astype(BF), x_s[:nq, :], NN),
-        dot(dka[...].astype(BF), x_s[...], NN),
-        dot(dva[...].astype(BF), x_s[...], NN),
-        dot(mt_s[...], cot_s[...], NN),
+        lambda: dot(dqt_s[...].astype(BF), x_s[:nq, :], NN),
+        lambda: dot(dka[...].astype(BF), x_s[...], NN),
+        lambda: dot(dva[...].astype(BF), x_s[...], NN),
+        lambda: dot(mt_s[...], cot_s[...], NN),
     )
-    for i, g in enumerate(grads):
-        grad_s[i * 128 : i * 128 + 128, pair * 512 : pair * 512 + 512] = g.astype(BF)
-    if pair:
-        grad_s[:, 1024:] = (edge_s[0].astype(F32) + edge_s[1].astype(F32)).astype(BF)
-    send(grad_s, grad_o)
+    for i, grad in enumerate(grads):
+        rows = slice(i * 128, i * 128 + 128)
+        grad_s[rows, pair * 512 : pair * 512 + 512] = grad().astype(BF)
+        send(grad_s.at[rows, :], grad_o.at[rows, :])
     for copy in leave:
         copy.wait()
 
@@ -202,7 +203,7 @@
         out_specs=(hbm,) * 3,
         scratch_shapes=[V((seq, d), BF), V((nq, d), BF), V((d, 3 * hw), BF), V((hw, d), BF)]
         + [V((512, wide), BF), V((seq, d), BF), V((nq, hw), BF), V((2, 512, 768) if pair else (2, 8, 128), BF)]
-        + [pltpu.SemaphoreType.DMA((19,))]
+        + [pltpu.SemaphoreType.DMA((22,))]
         + [V((seq, hw), BF)] * 2
         + [V((hw, seq), BF)] * 2
         + [V((hw, nq), BF)] * 2
@@ -218,14 +219,15 @@
 def slots_kernel(slots, mask, idx, inv):
     on = mask[...]
     idx[...] = jnp.where(on > 0, slots[...], 1536) * 8
-    inv[...] = 1.0 / jnp.maximum(jnp.sum(on.astype(F32), axis=1, keepdims=True), 1.0)
+    count = jnp.broadcast_to(jnp.sum(on.astype(F32), axis=0, keepdims=True), on.shape)
+    inv[...] = (1.0 / jnp.maximum(count, 1.0)).T
 
 
 def read_slots(slots, mask):
     vm = pl.BlockSpec(memory_space=pltpu.VMEM)
     return pl.pallas_call(
         slots_kernel,
-        out_shape=(jax.ShapeDtypeStruct(slots.shape, jnp.int32), jax.ShapeDtypeStruct((slots.shape[0], 1), F32)),
+        out_shape=(jax.ShapeDtypeStruct(slots.shape, jnp.int32), jax.ShapeDtypeStruct(slots.shape[::-1], F32)),
         in_specs=[vm, vm],
         out_specs=(vm, vm),
         cost_estimate=pl.CostEstimate(flops=20 * 10**9, bytes_accessed=MIB, transcendentals=0),
@@ -280,7 +282,7 @@
     def fill_nodes(i, _):
         base = pl.multiple_of(i * R, R)
         t = dot(tab[pl.ds(base, R), :], wg[...], NN) * 0.5
-        u = cot[pl.ds(base, R), :].astype(F32) * (inv[pl.ds(base, R), :] * 0.25)
+        u = cot[pl.ds(base, R), :].astype(F32) * (inv[pl.ds(base, R), :1] * 0.25)
         for c in range(4):
             cs = slice(c * 128, c * 128 + 128)
             for h in (0, 4):
@@ -298,7 +300,7 @@
         ps = []
         ds = []
         for k in range(8):
-            j = pl.multiple_of(idx[i * 8 + k], 8)
+            j = pl.multiple_of(idx[k, i], 8)
             t = jnp.tanh(a_s[pl.ds(j, 8), :] + gt)
             p = (1.0 + t) * b_s[pl.ds(j, 8), :]
             g = p * (1.0 - t * gate_half) * up
@@ -338,7 +340,7 @@
     def read_local(i, _):
         base = pl.multiple_of(i * R, R)
         read(base)
-        weight = inv[pl.ds(base, R), :] * 0.5
+        weight = inv[pl.ds(base, R), :1] * 0.5
         for c in range(4):
             cs = slice(c * 128, c * 128 + 128)
             base_s[pl.ds(base, R), cs] = tab[pl.ds(base, R), cs].astype(F32) + gt_s[pl.ds(base * 8 + c, R, stride=8), :] * weight
@@ -391,21 +393,44 @@
     )(core, idx, inv, *in_hbm(x, inc, cot, wg, ws))
 
 
-def spread_kernel(got, out):
-    total = jnp.sum(got[...].astype(F32), axis=0).astype(BF)
-    out[...] = jnp.broadcast_to(total[None], out.shape)
+def spread_kernel(got, out, got_s, sum_s, sems):
+    chips, _, w = got.shape
+    steps = 8
+    part = chips // steps
+    fetch = [
+        pltpu.make_async_copy(got.at[i * part : i * part + part], got_s.at[i * part : i * part + part], sems.at[i])
+        for i in range(steps)
+    ]
+    for copy in fetch:
+        copy.start()
+    total = jnp.zeros((8, w), F32)
+    for i, copy in enumerate(fetch):
+        copy.wait()
+        for j in range(part):
+            total = total + got_s[i * part + j].astype(F32)
+    sum_s[...] = jnp.broadcast_to(total.astype(BF)[None], sum_s.shape)
+    leave = [pltpu.make_async_copy(sum_s, out.at[i * part : i * part + part], sems.at[i]) for i in range(steps)]
+    for copy in leave:
+        copy.start()
+    for copy in leave:
+        copy.wait()
 
 
 def sum_spread(got):
-    vm = pl.BlockSpec(memory_space=pltpu.VMEM)
+    hbm = pl.BlockSpec(memory_space=pltpu.HBM)
     return pl.pallas_call(
         spread_kernel,
-        out_shape=jax.ShapeDtypeStruct(got.shape, BF),
-        in_specs=[vm],
-        out_specs=vm,
+        out_shape=pltpu.HBM(got.shape, BF),
+        in_specs=[hbm],
+        out_specs=hbm,
+        scratch_shapes=[
+            pltpu.VMEM(got.shape, BF),
+            pltpu.VMEM((8,) + got.shape[1:], BF),
+            pltpu.SemaphoreType.DMA((8,)),
+        ],
         cost_estimate=pl.CostEstimate(flops=got.size, bytes_accessed=got.size * 4, transcendentals=0),
         name="sum_spread",
-    )(got)
+    )(*in_hbm(got))
 
 
 def place_kernel(which, *refs):
@@ -492,8 +517,7 @@
     x_far_sib = swap(x_far, "c")
     xs = (x, x_sib, x_far, x_far_sib)
     cots = (cot, cot_sib)
-    slot_rows, inv = read_slots(slots, mask)
-    idx = slot_rows.reshape(-1)
+    idx, inv = read_slots(slots.T, mask.T)
     early, idx = lax.optimization_barrier((core, idx))
     grad_first, mixed_first, part_first = attention(0, early, xs, cots, wqkv, wo)
     incoming, grad_first = lax.optimization_barrier((incoming, grad_first))
@@ -512,7 +536,9 @@
     layer_out = (base + attended).astype(BF)
     part4 = (part_first.astype(F32) + part_second.astype(F32)).reshape(2, 2, n, d)
     from_sib = swap(part4[:, 1].astype(BF), "c").astype(F32)
-    from_far = swap((part4[1, 0] + from_sib[1]).astype(BF), "xl")
+    to_far = (part4[1, 0] + from_sib[1]).astype(BF)
+    parts, to_far = lax.optimization_barrier((parts, to_far))
+    from_far = swap(to_far, "xl")
     feats_grad = (
         local + part4[0, 0] + from_sib[0] + from_far.astype(F32) + dot(pick, returned, TN)
     ).astype(BF)

time: 197 us -> 194 us (0.985)
  local copies, waits for them, and re-layouts: 13.2 us -> 9.79 us
  matrix products: 6.55 us -> 9.37 us
    dot_general x4, matrix products: 6.55 us -> 9.37 us  [dot(): return lax.dot_general(a, b, dims, preferred_element_type=F32)]
    unnamed x37 -> x25, local copies, waits for them, and re-layouts: 9.49 us -> 7.13 us
    all_to_all x2, waiting for transfers between devices: 17.5 us -> 15.5 us  [chips(): return lax.all_to_all(a, CHIPS, 0, 0, tiled=True)]
  transfers between devices with their start and end apart: 13 -> 13, of which waited for: 3 -> 5; matrix products, arithmetic and copies ran while one was open for 9% -> 9% of each run, Pallas kernels for 24% -> 22%
where the time goes in v5:
time: 194 us; the launch traced here: 191 us
  Pallas kernels  78.9 us (41%)
  starting transfers between devices  47.9 us (25%)
  waiting for transfers between devices  39.5 us (20%)
  local copies, waits for them, and re-layouts  9.79 us (5%)
  matrix products  9.37 us (5%)
  other arithmetic  4.07 us (2%)
    pallas_call x2, Pallas kernels, attention(): pl.pallas_call(functools.partial(attn_kernel, pair), out_shape=(pltpu.HBM...  38.8 us
    pallas_call x1, Pallas kernels, edges(): pl.pallas_call(edges_kernel, out_shape=(H((n, d), F32), H((n, d), F32), H...  31.6 us
    ppermute x9, waiting for transfers between devices, swap(): return lax.ppermute(a, axis, SWAP)  24.1 us
    all_to_all x2, starting transfers between devices, domains(): lax.all_to_all(a.reshape(32, 32, -1), DOM, 0, 0, tiled=True)  20.1 us
    all_to_all x2, waiting for transfers between devices, chips(): return lax.all_to_all(a, CHIPS, 0, 0, tiled=True)  15.5 us
    all_to_all x2, starting transfers between devices, chips(): return lax.all_to_all(a, CHIPS, 0, 0, tiled=True)  15.4 us
    ppermute x9, starting transfers between devices, swap(): return lax.ppermute(a, axis, SWAP)  12.4 us
    dot_general x4, matrix products, dot(): return lax.dot_general(a, b, dims, preferred_element_type=F32)  9.37 us
  transfers between devices with their start and end apart: 13, of which 5 were waited for; matrix products, arithmetic and copies ran while one was open for 9% of the time, Pallas kernels for 22%

profile of v5, /device:TPU:1, one launch (start us, length us, event | category | flops | bytes accessed | tf_op | source)
XLA Modules:
  0.0 190.7 jit_solution(12242718855095368802)
XLA Ops:
  0.6 2.1 %collective-permute-start.1 = (bf16[512,512]{1,0:T(8,128)(2,1)}, bf16[512,512]{1,0:T(8,128)(2,1)S(1)}, u32[]{:S(2)}, u32[]{:S(2)}) collective-permute-start(bf16[512,512]{1,0:T(8,128)(2,1)} %x0.3), channel_id=1, source_target_pairs={{0,64},{64,0},{1,65},{65,1},{2,66},{66,2},{3,67},{67,3},{4,68},{68... | collective-permute-start | bytes 1572872 | tf_op jit(solution)/shard_map/ppermute | solution.py:496
  2.8 1.0 collective-permute-start
  3.7 0.0 collective-permute-start.3
  3.7 0.8 eq.10
  4.5 2.8 %fusion.2 = bf16[1024,512]{1,0:T(8,128)(2,1)} fusion(bf16[512,512]{1,0:T(8,128)(2,1)} %x0.3, s32[1024]{0:T(1024)S(1)} %eq.10), kind=kOutput, calls=%fused_computation.5 | convolution fusion | flops 537919488 | bytes 1576960 | tf_op jit(solution)/shard_map/dot_general | solution.py:28
  7.3 10.2 %all-to-all-start = ((bf16[32,32,512]{2,1,0:T(8,128)(2,1)}), bf16[32,32,512]{2,1,0:T(8,128)(2,1)S(1)}, u32[]{:S(2)}, u32[]{:S(2)}) async-start(bf16[32,32,512]{2,1,0:T(8,128)(2,1)} %bitcast.1), calls=%async_computation | async-start | bytes 2097152 | tf_op jit(solution)/shard_map/all_to_all | solution.py:504
  17.5 0.0 collective-permute-done.1.x2
  17.5 0.0 copy-start.7
  17.5 1.0 collective-permute-start.2
  18.6 1.6 slots.1
  20.2 0.0 copy-done.7
  20.2 0.0 collective-permute-done.3.cot1
  20.2 0.0 copy-start.9
  20.2 0.0 collective-permute-done.x1
  20.2 0.0 copy-start.8
  20.2 0.0 collective-permute-done.2.x3
  20.2 0.8 copy-done.9
  21.0 0.2 copy-done.8
  21.1 0.8 copy-done.10
  21.9 19.2 %attention.2 = (bf16[512,512]{1,0:T(8,128)(2,1)}, bf16[1024,128]{1,0:T(8,128)(2,1)}, bf16[2048,512]{1,0:T(8,128)(2,1)}) custom-call(s32[1]{0:T(128)} %bitcast.core.refs_0_, bf16[512,512]{1,0:T(8,128)(2,1)} %x0.3, bf16[512,512]{1,0:T(8,128)(2,1)} %copy-done.8, bf16[512,512]{1,0:T(8,128)(2,1)} %copy-done.7, bf16[512,512]{1,0:T(8,128)(2,1)} %copy-done.10, ...), custom_call_target="tpu_custom_call" | custom-call | flops 16000000000 | bytes 8388608 | tf_op jit(solution)/shard_map/attention/pallas_call | solution.py:199
  41.1 0.0 all-to-all-done
  41.1 0.0 copy-start.5
  41.1 1.0 copy-done.5
  42.1 31.6 %edges.1 = (f32[512,512]{1,0:T(8,128)}, f32[512,512]{1,0:T(8,128)}, bf16[1024,512]{1,0:T(8,128)(2,1)}, bf16[512,768]{1,0:T(8,128)(2,1)}, bf16[512,768]{1,0:T(8,128)(2,1)}) custom-call(s32[1]{0:T(128)} %bitcast.core.refs_0_, s32[8,512]{1,0:T(8,128)} %get-tuple-element.42.idx, f32[512,8]{1,0:T(8,128)} %get-tuple-element.43.inv, bf16[512,512]{1,0:T(8,128)(2,1)} %x0.3, ...), custom_call_target="tpu_custom_call" | custom-call | flops 20000000000 | bytes 8388608 | tf_op jit(solution)/shard_map/edges/pallas_call | solution.py:381
  73.7 0.1 collective-permute-start.4
  73.8 9.8 %all-to-all-start.1 = ((bf16[32,32,512]{2,1,0:T(8,128)(2,1)}), bf16[32,32,512]{2,1,0:T(8,128)(2,1)S(1)}, u32[]{:S(2)}, u32[]{:S(2)}) async-start(bf16[32,32,512]{2,1,0:T(8,128)(2,1)} %bitcast.56), calls=%async_computation.1 | async-start | bytes 2097152 | tf_op jit(solution)/shard_map/all_to_all | solution.py:504
  83.6 0.0 collective-permute-done.4.rest_2_
  83.6 0.0 copy-start.6
  83.6 0.9 copy-done.6
  84.5 19.6 %attention.3 = (bf16[512,1792]{1,0:T(8,128)(2,1)}, bf16[1024,128]{1,0:T(8,128)(2,1)}, bf16[2048,512]{1,0:T(8,128)(2,1)}) custom-call(s32[1]{0:T(128)} %bitcast.core.refs_0_, bf16[512,512]{1,0:T(8,128)(2,1)} %x0.3, bf16[512,512]{1,0:T(8,128)(2,1)} %copy-done.8, bf16[512,512]{1,0:T(8,128)(2,1)} %copy-done.7, bf16[512,512]{1,0:T(8,128)(2,1)} %copy-done.10, ...), custom_call_target="tpu_custom_call" | custom-call | flops 16000000000 | bytes 8388608 | tf_op jit(solution)/shard_map/attention/pallas_call | solution.py:199
  104.1 0.0 all-to-all-done.1
  104.1 9.9 %all-to-all-start.2 = ((bf16[64,8,1792]{2,1,0:T(8,128)(2,1)}), bf16[64,8,1792]{2,1,0:T(8,128)(2,1)S(1)}, u32[]{:S(2)}, u32[]{:S(2)}) async-start(bf16[64,8,1792]{2,1,0:T(8,128)(2,1)} %bitcast.53), calls=%async_computation.2 | async-start | bytes 3670016 | tf_op jit(solution)/shard_map/all_to_all | solution.py:500
  114.0 2.8 %convert_add_fusion = f32[2048,512]{1,0:T(8,128)S(1)} fusion(bf16[2048,512]{1,0:T(8,128)(2,1)} %get-tuple-element.51, bf16[2048,512]{1,0:T(8,128)(2,1)} %get-tuple-element.50), kind=kLoop, calls=%fused_computation | loop fusion | flops 3145728 | bytes 8388608 | tf_op jit(solution)/shard_map/add | solution.py:537
  116.8 0.0 copy-start
  116.9 0.1 fusion.5
  117.0 1.4 collective-permute-start.5
  118.4 2.3 %collective-permute-done.5 = bf16[2,512,512]{2,1,0:T(8,128)(2,1)S(1)} collective-permute-done((bf16[2,512,512]{2,1,0:T(8,128)(2,1)S(1)}, bf16[2,512,512]{2,1,0:T(8,128)(2,1)S(1)}, u32[]{:S(2)}, u32[]{:S(2)}) %collective-permute-start.5) | collective-permute-done | bytes 1048608 | tf_op jit(solution)/shard_map/ppermute | solution.py:496
  120.7 0.3 convert_element_type.33
  121.0 0.0 copy-done
  121.0 0.0 copy-start.2
  121.0 1.3 copy-done.2
  122.3 0.9 fusion.12
  123.3 15.5 %all-to-all-done.2.got = bf16[64,8,1792]{2,1,0:T(8,128)(2,1)S(1)} async-done(((bf16[64,8,1792]{2,1,0:T(8,128)(2,1)}), bf16[64,8,1792]{2,1,0:T(8,128)(2,1)S(1)}, u32[]{:S(2)}, u32[]{:S(2)}) %all-to-all-start.2) | async-done | bytes 1835040 | tf_op jit(solution)/shard_map/all_to_all | solution.py:500
  138.7 1.2 copy-done.1
  139.9 2.9 %sum_spread.1 = bf16[64,8,1792]{2,1,0:T(8,128)(2,1)} custom-call(bf16[64,8,1792]{2,1,0:T(8,128)(2,1)} %copy-done.1), custom_call_target="tpu_custom_call" | custom-call | flops 917504 | bytes 3670016 | tf_op jit(solution)/shard_map/sum_spread/pallas_call | solution.py:421
  142.9 5.6 %all-to-all-start.3 = ((bf16[64,8,1792]{2,1,0:T(8,128)(2,1)}), bf16[64,8,1792]{2,1,0:T(8,128)(2,1)S(1)}, u32[]{:S(2)}, u32[]{:S(2)}) async-start(bf16[64,8,1792]{2,1,0:T(8,128)(2,1)} %sum_spread.1), calls=%async_computation.3 | async-start | bytes 3670016 | tf_op jit(solution)/shard_map/all_to_all | solution.py:500
  148.4 1.0 constant_dynamic-update-slice_fusion.1
  149.4 1.0 constant_dynamic-update-slice_fusion
  150.5 0.7 slice.33
  151.2 2.3 %collective-permute-start.6 = (bf16[512,256]{1,0:T(8,128)(2,1)}, bf16[512,256]{1,0:T(8,128)(2,1)}, u32[]{:S(2)}, u32[]{:S(2)}) collective-permute-start(bf16[512,256]{1,0:T(8,128)(2,1)} %slice.33), channel_id=1, source_target_pairs={{0,32},{32,0},{1,33},{33,1},{2,34},{34,2},{3,35},{35,3},{4,36},{36... | collective-permute-start | bytes 786440 | tf_op jit(solution)/shard_map/ppermute | solution.py:496
  153.4 1.4 collective-permute-start.7
  154.8 0.1 collective-permute-done.6
  155.0 1.5 fusion.16
  156.4 0.0 copy-done.4
  156.4 2.0 %fusion.4 = bf16[512,512]{1,0:T(8,128)(2,1)} fusion(f32[512,512]{1,0:T(8,128)S(1)} %copy-done.4, f32[512,512]{1,0:T(8,128)S(1)} %fusion.16, bf16[1024,256]{1,0:T(8,128)(2,1)S(1)} %constant_dynamic-update-slice_fusion, bf16[2,256,512]{2,1,0:T(8,128)(2,1)} %bitcast.58, s32[]{:T(128)S(6)} %select_n.7), kind=kOutput, calls=%fused_computation.8 | convolution fusion | flops 135004160 | bytes 3145732 | tf_op jit(solution)/shard_map/dot_general | solution.py:28
  158.5 20.3 %collective-permute-done.7 = bf16[512,512]{1,0:T(8,128)(2,1)S(1)} collective-permute-done((bf16[512,512]{1,0:T(8,128)(2,1)}, bf16[512,512]{1,0:T(8,128)(2,1)S(1)}, u32[]{:S(2)}, u32[]{:S(2)}) %collective-permute-start.7) | collective-permute-done | bytes 524320 | tf_op jit(solution)/shard_map/ppermute | solution.py:496
  178.8 0.0 copy-done.3
  178.8 0.0 copy-done.11
  178.8 3.1 %fusion.9 = bf16[512,512]{1,0:T(8,128)(2,1)} fusion(f32[2,512,512]{2,1,0:T(8,128)S(1)} %copy-done.3, f32[512,512]{1,0:T(8,128)S(1)} %copy-done.11, f32[2,2,512,512]{3,2,1,0:T(8,128)} %bitcast.52, bf16[512,512]{1,0:T(8,128)(2,1)S(1)} %collective-permute-done.7, bf16[1024,512]{1,0:T(8,128)(2,1)S(1)} %bitcast.54, s32[1024]{0:T(1024)S(1)} %eq.10), kind=kOutput, calls=%fused_computation.14 | convolution fusion | flops 538968064 | bytes 5246976 | tf_op jit(solution)/shard_map/dot_general | solution.py:28
  181.9 0.0 all-to-all-done.3
  181.9 3.2 %collective-permute-start.8 = (bf16[512,1792]{1,0:T(8,128)(2,1)S(1)}, bf16[512,1792]{1,0:T(8,128)(2,1)S(1)}, u32[]{:S(2)}, u32[]{:S(2)}) collective-permute-start(bf16[512,1792]{1,0:T(8,128)(2,1)S(1)} %bitcast.48), channel_id=1, source_target_pairs={{0,32},{32,0},{1,33},{33,1},{2,34},{34,2},{3,35},{35,3},{4,36},{36... | collective-permute-start | bytes 5505032 | tf_op jit(solution)/shard_map/ppermute | solution.py:496
  185.0 2.0 %place.2 = (f32[512,512]{1,0:T(8,128)}, f32[512,1024]{1,0:T(8,128)}, f32[512,1536]{1,0:T(8,128)}, f32[512,512]{1,0:T(8,128)}) custom-call(s32[1]{0:T(128)} %bitcast.core.refs_0_, bf16[512,1792]{1,0:T(8,128)(2,1)S(1)} %bitcast.49), custom_call_target="tpu_custom_call" | custom-call | tf_op jit(solution)/shard_map/place/pallas_call | solution.py:483
  187.1 1.4 collective-permute-done.8.refs_1_
  188.5 2.0 %place.3 = (f32[512,512]{1,0:T(8,128)}, f32[512,1024]{1,0:T(8,128)}, f32[512,1536]{1,0:T(8,128)}, f32[512,512]{1,0:T(8,128)}) custom-call(s32[1]{0:T(128)} %bitcast.core.refs_0_, bf16[512,1792]{1,0:T(8,128)(2,1)S(1)} %collective-permute-done.8.refs_1_, ...), custom_call_target="tpu_custom_call", output_to_operand_aliasing={{0}: (2, {}), {1}: (3, {}), {2}: (4, {}), {3}: (5, {})} | custom-call | tf_op jit(solution)/shard_map/place/pallas_call | solution.py:483
  (5 shorter events, 0.0 us)
Async XLA Ops:
  0.6 16.9 %collective-permute-start.1 = (bf16[512,512]{1,0:T(8,128)(2,1)}, bf16[512,512]{1,0:T(8,128)(2,1)S(1)}, u32[]{:S(2)}, u32[]{:S(2)}) collective-permute-start(bf16[512,512]{1,0:T(8,128)(2,1)} %x0.3), channel_id=1, source_target_pairs={{0,64},{64,0},{1,65},{65,1},{2,66},{66,2},{3,67},{67,3},{4,68},{68... | collective-permute-start | bytes 1572872 | tf_op jit(solution)/shard_map/ppermute | solution.py:496
  2.8 17.4 %collective-permute-start = (bf16[512,512]{1,0:T(8,128)(2,1)}, bf16[512,512]{1,0:T(8,128)(2,1)S(1)}, u32[]{:S(2)}, u32[]{:S(2)}) collective-permute-start(bf16[512,512]{1,0:T(8,128)(2,1)} %x0.3), channel_id=1, source_target_pairs={{0,32},{32,0},{1,33},{33,1},{2,34},{34,2},{3,35},{35,3},{4,36},{36... | collective-permute-start | bytes 1572872 | tf_op jit(solution)/shard_map/ppermute | solution.py:496
  3.7 16.5 %collective-permute-start.3 = (bf16[512,512]{1,0:T(8,128)(2,1)}, bf16[512,512]{1,0:T(8,128)(2,1)S(1)}, u32[]{:S(2)}, u32[]{:S(2)}) collective-permute-start(bf16[512,512]{1,0:T(8,128)(2,1)} %cot0.3), channel_id=1, source_target_pairs={{0,32},{32,0},{1,33},{33,1},{2,34},{34,2},{3,35},{35,3},{4,36},{36... | collective-permute-start | bytes 1572872 | tf_op jit(solution)/shard_map/ppermute | solution.py:496
  7.3 33.8 %all-to-all-start = ((bf16[32,32,512]{2,1,0:T(8,128)(2,1)}), bf16[32,32,512]{2,1,0:T(8,128)(2,1)S(1)}, u32[]{:S(2)}, u32[]{:S(2)}) async-start(bf16[32,32,512]{2,1,0:T(8,128)(2,1)} %bitcast.1), calls=%async_computation | async-start | bytes 2097152 | tf_op jit(solution)/shard_map/all_to_all | solution.py:504
  17.5 2.6 %copy-start.7 = (bf16[512,512]{1,0:T(8,128)(2,1)}, bf16[512,512]{1,0:T(8,128)(2,1)S(1)}, u32[]{:S(2)}) copy-start(bf16[512,512]{1,0:T(8,128)(2,1)S(1)} %collective-permute-done.1.x2) | copy-start | bytes 1572868
  17.5 2.7 %collective-permute-start.2 = (bf16[512,512]{1,0:T(8,128)(2,1)S(1)}, bf16[512,512]{1,0:T(8,128)(2,1)S(1)}, u32[]{:S(2)}, u32[]{:S(2)}) collective-permute-start(bf16[512,512]{1,0:T(8,128)(2,1)S(1)} %collective-permute-done.1.x2), channel_id=1, source_target_pairs={{0,32},{32,0},{1,33},{33,1},{2,34},{34,2},{3,35},{35,3},{4,36},{36... | collective-permute-start | bytes 1572872 | tf_op jit(solution)/shard_map/ppermute | solution.py:496
  20.2 0.8 copy-start.9
  20.2 1.0 copy-start.8
  21.1 0.8 copy-start.10
  41.1 1.0 copy-start.5
  73.7 9.9 %collective-permute-start.4 = (bf16[512,768]{1,0:T(8,128)(2,1)}, bf16[512,768]{1,0:T(8,128)(2,1)S(1)}, u32[]{:S(2)}, u32[]{:S(2)}) collective-permute-start(bf16[512,768]{1,0:T(8,128)(2,1)} %get-tuple-element.46), channel_id=1, source_target_pairs={{0,32},{32,0},{1,33},{33,1},{2,34},{34,2},{3,35},{35,3},{4,36},{36... | collective-permute-start | bytes 2359304 | tf_op jit(solution)/shard_map/ppermute | solution.py:496
  73.8 30.4 %all-to-all-start.1 = ((bf16[32,32,512]{2,1,0:T(8,128)(2,1)}), bf16[32,32,512]{2,1,0:T(8,128)(2,1)S(1)}, u32[]{:S(2)}, u32[]{:S(2)}) async-start(bf16[32,32,512]{2,1,0:T(8,128)(2,1)} %bitcast.56), calls=%async_computation.1 | async-start | bytes 2097152 | tf_op jit(solution)/shard_map/all_to_all | solution.py:504
  83.6 0.9 copy-start.6
  104.1 34.6 %all-to-all-start.2 = ((bf16[64,8,1792]{2,1,0:T(8,128)(2,1)}), bf16[64,8,1792]{2,1,0:T(8,128)(2,1)S(1)}, u32[]{:S(2)}, u32[]{:S(2)}) async-start(bf16[64,8,1792]{2,1,0:T(8,128)(2,1)} %bitcast.53), calls=%async_computation.2 | async-start | bytes 3670016 | tf_op jit(solution)/shard_map/all_to_all | solution.py:500
  116.8 4.1 %copy-start = (f32[2048,512]{1,0:T(8,128)}, f32[2048,512]{1,0:T(8,128)S(1)}, u32[]{:S(2)}) copy-start(f32[2048,512]{1,0:T(8,128)S(1)} %convert_add_fusion) | copy-start | bytes 12582916
  117.0 3.7 %collective-permute-start.5 = (bf16[2,512,512]{2,1,0:T(8,128)(2,1)S(1)}, bf16[2,512,512]{2,1,0:T(8,128)(2,1)S(1)}, u32[]{:S(2)}, u32[]{:S(2)}) collective-permute-start(bf16[2,512,512]{2,1,0:T(8,128)(2,1)S(1)} %fusion.5), channel_id=1, source_target_pairs={{0,32},{32,0},{1,33},{33,1},{2,34},{34,2},{3,35},{35,3},{4,36},{36... | collective-permute-start | bytes 3145736 | tf_op jit(solution)/shard_map/ppermute | solution.py:496
  121.0 1.3 copy-start.2
  138.7 1.2 copy-start.1
  142.9 39.0 %all-to-all-start.3 = ((bf16[64,8,1792]{2,1,0:T(8,128)(2,1)}), bf16[64,8,1792]{2,1,0:T(8,128)(2,1)S(1)}, u32[]{:S(2)}, u32[]{:S(2)}) async-start(bf16[64,8,1792]{2,1,0:T(8,128)(2,1)} %sum_spread.1), calls=%async_computation.3 | async-start | bytes 3670016 | tf_op jit(solution)/shard_map/all_to_all | solution.py:500
  151.2 3.8 %collective-permute-start.6 = (bf16[512,256]{1,0:T(8,128)(2,1)}, bf16[512,256]{1,0:T(8,128)(2,1)}, u32[]{:S(2)}, u32[]{:S(2)}) collective-permute-start(bf16[512,256]{1,0:T(8,128)(2,1)} %slice.33), channel_id=1, source_target_pairs={{0,32},{32,0},{1,33},{33,1},{2,34},{34,2},{3,35},{35,3},{4,36},{36... | collective-permute-start | bytes 786440 | tf_op jit(solution)/shard_map/ppermute | solution.py:496
  153.4 3.0 %copy-start.4 = (f32[512,512]{1,0:T(8,128)S(1)}, f32[512,512]{1,0:T(8,128)}, u32[]{:S(2)}) copy-start(f32[512,512]{1,0:T(8,128)} %get-tuple-element.53) | copy-start | bytes 3145732
  153.4 25.3 %collective-permute-start.7 = (bf16[512,512]{1,0:T(8,128)(2,1)}, bf16[512,512]{1,0:T(8,128)(2,1)S(1)}, u32[]{:S(2)}, u32[]{:S(2)}) collective-permute-start(bf16[512,512]{1,0:T(8,128)(2,1)} %fusion.12), channel_id=1, source_target_pairs={{0,64},{64,0},{1,65},{65,1},{2,66},{66,2},{3,67},{67,3},{4,68},{68... | collective-permute-start | bytes 1572872 | tf_op jit(solution)/shard_map/ppermute | solution.py:496
  154.9 23.8 %copy-start.3 = (f32[2,512,512]{2,1,0:T(8,128)S(1)}, f32[2,512,512]{2,1,0:T(8,128)}, u32[]{:S(2)}) copy-start(f32[2,512,512]{2,1,0:T(8,128)} %copy-done.2) | copy-start | bytes 6291460
  154.9 23.8 %copy-start.11 = (f32[512,512]{1,0:T(8,128)S(1)}, f32[512,512]{1,0:T(8,128)}, u32[]{:S(2)}) copy-start(f32[512,512]{1,0:T(8,128)} %get-tuple-element.56) | copy-start | bytes 3145732
  181.9 6.6 %collective-permute-start.8 = (bf16[512,1792]{1,0:T(8,128)(2,1)S(1)}, bf16[512,1792]{1,0:T(8,128)(2,1)S(1)}, u32[]{:S(2)}, u32[]{:S(2)}) collective-permute-start(bf16[512,1792]{1,0:T(8,128)(2,1)S(1)} %bitcast.48), channel_id=1, source_target_pairs={{0,32},{32,0},{1,33},{33,1},{2,34},{34,2},{3,35},{35,3},{4,36},{36... | collective-permute-start | bytes 5505032 | tf_op jit(solution)/shard_map/ppermute | solution.py:496

commit v6 on v5

--- a/solution.py
+++ b/solution.py
@@ -32,8 +32,8 @@
     if pair:
         g_first, keep, got = rest[:3]
         rest = rest[3:]
-    grad_o, mixed_o, part_o, x_s, cot_s, w_s, wo_s, grad_s, part_s, mix_s, edge_s, sems = rest[:12]
-    k_s, v_s, kt_s, vt_s, qt_s, dmt_s, s_s, e_s, dka, dva, mt_s, dqt_s = rest[12:]
+    grad_o, mixed_o, own_o, sib_o, x_s, cot_s, w_s, wo_s, grad_s, part_s, mix_s, edge_s, sems = rest[:13]
+    k_s, v_s, kt_s, vt_s, qt_s, dmt_s, s_s, e_s, dka, dva, mt_s, dqt_s = rest[13:]
     n = x0.shape[0]
     seq = x_s.shape[0]
     nq = cot_s.shape[0]
@@ -49,8 +49,11 @@
 
     for i in range(3):
         start(wqkv.at[:, pl.ds(pl.multiple_of(off + 512 * i, 128), 128)], w_s.at[:, i * 128 : i * 128 + 128])
-    for i, src in enumerate((x0, x1, x2, x3)):
-        start(src, x_s.at[i * n : i * n + n, :])
+    start(x0, x_s.at[:n, :])
+    for copy in fetch:
+        copy.wait()
+    for i, src in enumerate((x1, x2, x3)):
+        start(src, x_s.at[i * n + n : i * n + 2 * n, :])
     start(wo.at[pl.ds(off, 128), :], wo_s)
     for i, src in enumerate((cot0, cot1)):
         start(src, cot_s.at[i * n : i * n + n, :])
@@ -58,12 +61,10 @@
         start(g_first, grad_s.at[:, :512])
         start(keep, edge_s.at[0])
         start(got, edge_s.at[1])
-    for copy in fetch[:3]:
-        copy.wait()
     wq = w_s[:, :128]
     wkv = w_s[:, 128:]
     for r in chunks:
-        if r.start % n == 0:
+        if r.start and r.start % n == 0:
             fetch[3 + r.start // n].wait()
         kv = dot(x_s[r, :], wkv, NN)
         k_s[r, :] = kv[:, :128].astype(BF)
@@ -169,7 +170,8 @@
             part = part + dot(dq[r, :], wq, NT)
         part_s[r, :] = part.astype(BF)
         if r.stop % n == 0:
-            send(part_s.at[r.stop - n : r.stop, :], part_o.at[r.stop - n : r.stop, :])
+            block = r.start // n
+            send(part_s.at[r.stop - n : r.stop, :], (own_o, sib_o)[block % 2].at[block // 2])
     grads = (
         lambda: dot(dqt_s[...].astype(BF), x_s[:nq, :], NN),
         lambda: dot(dka[...].astype(BF), x_s[...], NN),
@@ -198,9 +200,9 @@
     hbm = pl.BlockSpec(memory_space=pltpu.HBM)
     return pl.pallas_call(
         functools.partial(attn_kernel, pair),
-        out_shape=(pltpu.HBM((512, wide), BF), pltpu.HBM((nq, hw), BF), pltpu.HBM((seq, d), BF)),
+        out_shape=(pltpu.HBM((512, wide), BF), pltpu.HBM((nq, hw), BF), pltpu.HBM((2, n, d), BF), pltpu.HBM((2, n, d), BF)),
         in_specs=[pl.BlockSpec(memory_space=pltpu.SMEM)] + [hbm] * (8 + len(first)),
-        out_specs=(hbm,) * 3,
+        out_specs=(hbm,) * 4,
         scratch_shapes=[V((seq, d), BF), V((nq, d), BF), V((d, 3 * hw), BF), V((hw, d), BF)]
         + [V((512, wide), BF), V((seq, d), BF), V((nq, hw), BF), V((2, 512, 768) if pair else (2, 8, 128), BF)]
         + [pltpu.SemaphoreType.DMA((22,))]
@@ -244,7 +246,8 @@
     fetch = []
     for src, dst in ((ws_i, ws), (x_i, tab.at[:n, :]), (inc_i, tab.at[n:, :]), (wg_i, wg), (cot_i, cot)):
         fetch.append(pltpu.make_async_copy(src, dst, sems.at[len(fetch)]))
-        fetch[-1].start()
+    fetch[0].start()
+    fetch[1].start()
     leave = []
 
     def send(src, dst):
@@ -271,6 +274,8 @@
 
     fetch[0].wait()
     fetch[1].wait()
+    for copy in fetch[2:]:
+        copy.start()
     fill(0, n)
     fetch[2].wait()
     fill(n, rows - n)
@@ -421,7 +426,7 @@
     return pl.pallas_call(
         spread_kernel,
         out_shape=pltpu.HBM(got.shape, BF),
-        in_specs=[hbm],
+        in_specs=[pl.BlockSpec(memory_space=pl.ANY)],
         out_specs=hbm,
         scratch_shapes=[
             pltpu.VMEM(got.shape, BF),
@@ -430,7 +435,7 @@
         ],
         cost_estimate=pl.CostEstimate(flops=got.size, bytes_accessed=got.size * 4, transcendentals=0),
         name="sum_spread",
-    )(*in_hbm(got))
+    )(got)
 
 
 def place_kernel(which, *refs):
@@ -519,12 +524,12 @@
     cots = (cot, cot_sib)
     idx, inv = read_slots(slots.T, mask.T)
     early, idx = lax.optimization_barrier((core, idx))
-    grad_first, mixed_first, part_first = attention(0, early, xs, cots, wqkv, wo)
+    grad_first, mixed_first, own_first, sib_first = attention(0, early, xs, cots, wqkv, wo)
     incoming, grad_first = lax.optimization_barrier((incoming, grad_first))
     base, local, remote, keep, give = edges(core, idx, inv, x, incoming, cot, wg, ws)
     returned = domains(remote)
     got = swap(give, "c")
-    joint, mixed_second, part_second = attention(1, core, xs, cots, wqkv, wo, grad_first, keep, got)
+    joint, mixed_second, own_second, sib_second = attention(1, core, xs, cots, wqkv, wo, grad_first, keep, got)
     joint, returned = lax.optimization_barrier((joint, returned))
     parts = chips(joint.reshape(64, 8, -1))
     mixed = jnp.concatenate([mixed_first, mixed_second], axis=1)
@@ -534,13 +539,11 @@
     wo_sib = lax.dynamic_index_in_dim(wo2, 1 - core[0], 0, keepdims=False)
     attended = dot(mixed[:n], wo_own, NN) + dot(mixed_sib, wo_sib, NN)
     layer_out = (base + attended).astype(BF)
-    part4 = (part_first.astype(F32) + part_second.astype(F32)).reshape(2, 2, n, d)
-    from_sib = swap(part4[:, 1].astype(BF), "c").astype(F32)
-    to_far = (part4[1, 0] + from_sib[1]).astype(BF)
-    parts, to_far = lax.optimization_barrier((parts, to_far))
-    from_far = swap(to_far, "xl")
+    pieces = (own_first, own_second, swap(sib_first, "c"), swap(sib_second, "c"))
+    from_far = swap(sum(a[1].astype(F32) for a in pieces).astype(BF), "xl")
+    parts, from_far = lax.optimization_barrier((parts, from_far))
     feats_grad = (
-        local + part4[0, 0] + from_sib[0] + from_far.astype(F32) + dot(pick, returned, TN)
+        local + sum(a[0].astype(F32) for a in pieces) + from_far.astype(F32) + dot(pick, returned, TN)
     ).astype(BF)
     own = chips(sum_spread(parts)).reshape(512, -1)
     own, layer_out, feats_grad = lax.optimization_barrier((own, layer_out, feats_grad))

time: 194 us -> 200 us (1.031)
  waiting for transfers between devices: 39.5 us -> 45.5 us
  starting transfers between devices: 47.9 us -> 51 us
  matrix products: 9.37 us -> 6.39 us
    ppermute x9 -> x10, waiting for transfers between devices: 24.1 us -> 30.9 us  [swap(): return lax.ppermute(a, axis, SWAP)]
    all_to_all x2, starting transfers between devices: 15.4 us -> 19.8 us  [chips(): return lax.all_to_all(a, CHIPS, 0, 0, tiled=True)]
    dot_general x4, matrix products: 9.37 us -> 6.39 us  [dot(): return lax.dot_general(a, b, dims, preferred_element_type=F32)]
    ppermute x9 -> x10, starting transfers between devices: 12.4 us -> 11 us  [swap(): return lax.ppermute(a, axis, SWAP)]
    unnamed x25 -> x27, local copies, waits for them, and re-layouts: 7.13 us -> 6.9 us
  transfers between devices with their start and end apart: 13 -> 14, of which waited for: 5 -> 3; matrix products, arithmetic and copies ran while one was open for 9% -> 7% of each run, Pallas kernels for 22% -> 22%
where the time goes in v6:
time: 200 us; the launch traced here: 197 us
  Pallas kernels  80.1 us (40%)
  starting transfers between devices  51 us (26%)
  waiting for transfers between devices  45.5 us (23%)
  local copies, waits for them, and re-layouts  8.72 us (4%)
  matrix products  6.39 us (3%)
  other arithmetic  4.12 us (2%)
    pallas_call x2, Pallas kernels, attention(): pl.pallas_call(functools.partial(attn_kernel, pair), out_shape=(pltpu.HBM...  40.1 us
    pallas_call x1, Pallas kernels, edges(): pl.pallas_call(edges_kernel, out_shape=(H((n, d), F32), H((n, d), F32), H...  31.5 us
    ppermute x10, waiting for transfers between devices, swap(): return lax.ppermute(a, axis, SWAP)  30.9 us
    all_to_all x2, starting transfers between devices, domains(): lax.all_to_all(a.reshape(32, 32, -1), DOM, 0, 0, tiled=True)  20.2 us
    all_to_all x2, starting transfers between devices, chips(): return lax.all_to_all(a, CHIPS, 0, 0, tiled=True)  19.8 us
    all_to_all x2, waiting for transfers between devices, chips(): return lax.all_to_all(a, CHIPS, 0, 0, tiled=True)  14.6 us
    ppermute x10, starting transfers between devices, swap(): return lax.ppermute(a, axis, SWAP)  11 us
    unnamed x27, local copies, waits for them, and re-layouts  6.9 us
  transfers between devices with their start and end apart: 14, of which 3 were waited for; matrix products, arithmetic and copies ran while one was open for 7% of the time, Pallas kernels for 22%

profile of v6, /device:TPU:1, one launch (start us, length us, event | category | flops | bytes accessed | tf_op | source)
XLA Modules:
  0.0 197.0 jit_solution(4298884810121855105)
XLA Ops:
  0.6 2.1 %collective-permute-start.1 = (bf16[512,512]{1,0:T(8,128)(2,1)}, bf16[512,512]{1,0:T(8,128)(2,1)S(1)}, u32[]{:S(2)}, u32[]{:S(2)}) collective-permute-start(bf16[512,512]{1,0:T(8,128)(2,1)} %x0.3), channel_id=1, source_target_pairs={{0,64},{64,0},{1,65},{65,1},{2,66},{66,2},{3,67},{67,3},{4,68},{68... | collective-permute-start | bytes 1572872 | tf_op jit(solution)/shard_map/ppermute | solution.py:501
  2.8 1.0 collective-permute-start
  3.7 0.0 collective-permute-start.3
  3.7 0.8 eq.10
  4.5 2.8 %fusion.2 = bf16[1024,512]{1,0:T(8,128)(2,1)} fusion(bf16[512,512]{1,0:T(8,128)(2,1)} %x0.3, s32[1024]{0:T(1024)S(1)} %eq.10), kind=kOutput, calls=%fused_computation.3 | convolution fusion | flops 537919488 | bytes 1576960 | tf_op jit(solution)/shard_map/dot_general | solution.py:28
  7.3 10.2 %all-to-all-start = ((bf16[32,32,512]{2,1,0:T(8,128)(2,1)}), bf16[32,32,512]{2,1,0:T(8,128)(2,1)S(1)}, u32[]{:S(2)}, u32[]{:S(2)}) async-start(bf16[32,32,512]{2,1,0:T(8,128)(2,1)} %bitcast.1), calls=%async_computation | async-start | bytes 2097152 | tf_op jit(solution)/shard_map/all_to_all | solution.py:509
  17.5 0.0 collective-permute-done.1.x2
  17.5 0.0 copy-start.9
  17.5 1.0 collective-permute-start.2
  18.6 1.6 slots.1
  20.2 0.0 copy-done.9
  20.2 0.0 collective-permute-done.3.cot1
  20.2 0.0 collective-permute-done.x1
  20.2 0.0 copy-start.10
  20.2 0.0 collective-permute-done.2.x3
  20.2 0.8 copy-done.11
  21.0 0.1 copy-done.10
  21.1 0.8 copy-done.12
  21.9 19.8 %attention.2 = (bf16[512,512]{1,0:T(8,128)(2,1)}, bf16[1024,128]{1,0:T(8,128)(2,1)}, bf16[2,512,512]{2,1,0:T(8,128)(2,1)}, bf16[2,512,512]{2,1,0:T(8,128)(2,1)}) custom-call(s32[1]{0:T(128)} %bitcast.core.refs_0_, bf16[512,512]{1,0:T(8,128)(2,1)} %x0.3, bf16[512,512]{1,0:T(8,128)(2,1)} %copy-done.10, bf16[512,512]{1,0:T(8,128)(2,1)} %copy-done.9, ...), custom_call_target="tpu_custom_call" | custom-call | flops 16000000000 | bytes 8388608 | tf_op jit(solution)/shard_map/attention/pallas_call | solution.py:201
  41.7 0.0 all-to-all-done
  41.7 0.0 copy-start.6
  41.8 1.0 copy-done.6
  42.7 31.5 %edges.1 = (f32[512,512]{1,0:T(8,128)}, f32[512,512]{1,0:T(8,128)}, bf16[1024,512]{1,0:T(8,128)(2,1)}, bf16[512,768]{1,0:T(8,128)(2,1)}, bf16[512,768]{1,0:T(8,128)(2,1)}) custom-call(s32[1]{0:T(128)} %bitcast.core.refs_0_, s32[8,512]{1,0:T(8,128)} %get-tuple-element.44.idx, f32[512,8]{1,0:T(8,128)} %get-tuple-element.45.inv, bf16[512,512]{1,0:T(8,128)(2,1)} %x0.3, ...), custom_call_target="tpu_custom_call" | custom-call | flops 20000000000 | bytes 8388608 | tf_op jit(solution)/shard_map/edges/pallas_call | solution.py:386
  74.2 0.2 collective-permute-start.4
  74.4 0.4 collective-permute-start.5
  74.8 10.0 %all-to-all-start.1 = ((bf16[32,32,512]{2,1,0:T(8,128)(2,1)}), bf16[32,32,512]{2,1,0:T(8,128)(2,1)S(1)}, u32[]{:S(2)}, u32[]{:S(2)}) async-start(bf16[32,32,512]{2,1,0:T(8,128)(2,1)} %bitcast.34), calls=%async_computation.1 | async-start | bytes 2097152 | tf_op jit(solution)/shard_map/all_to_all | solution.py:509
  84.8 0.0 collective-permute-done.4.rest_2_
  84.8 0.0 copy-start.8
  84.8 0.9 copy-done.8
  85.7 20.3 %attention.3 = (bf16[512,1792]{1,0:T(8,128)(2,1)}, bf16[1024,128]{1,0:T(8,128)(2,1)}, bf16[2,512,512]{2,1,0:T(8,128)(2,1)}, bf16[2,512,512]{2,1,0:T(8,128)(2,1)}) custom-call(s32[1]{0:T(128)} %bitcast.core.refs_0_, bf16[512,512]{1,0:T(8,128)(2,1)} %x0.3, bf16[512,512]{1,0:T(8,128)(2,1)} %copy-done.10, bf16[512,512]{1,0:T(8,128)(2,1)} %copy-done.9, ...), custom_call_target="tpu_custom_call" | custom-call | flops 16000000000 | bytes 8388608 | tf_op jit(solution)/shard_map/attention/pallas_call | solution.py:201
  106.1 0.0 copy-start.1
  106.1 0.4 collective-permute-start.6
  106.5 0.0 all-to-all-done.1
  106.5 1.0 copy-done.5
  107.5 10.1 %all-to-all-start.2 = ((bf16[64,8,1792]{2,1,0:T(8,128)(2,1)}), bf16[64,8,1792]{2,1,0:T(8,128)(2,1)S(1)}, u32[]{:S(2)}, u32[]{:S(2)}) async-start(bf16[64,8,1792]{2,1,0:T(8,128)(2,1)} %bitcast.31), calls=%async_computation.2 | async-start | bytes 3670016 | tf_op jit(solution)/shard_map/all_to_all | solution.py:505
  117.6 0.0 collective-permute-done.5
  117.6 0.0 collective-permute-done.6
  117.6 1.6 fusion.10
  119.3 1.2 collective-permute-start.7
  120.5 29.5 %collective-permute-done.7 = bf16[512,512]{1,0:T(8,128)(2,1)S(1)} collective-permute-done((bf16[512,512]{1,0:T(8,128)(2,1)S(1)}, bf16[512,512]{1,0:T(8,128)(2,1)S(1)}, u32[]{:S(2)}, u32[]{:S(2)}) %collective-permute-start.7) | collective-permute-done | bytes 524320 | tf_op jit(solution)/shard_map/ppermute | solution.py:501
  150.0 0.0 all-to-all-done.2.got
  150.0 1.2 copy-done
  151.2 2.9 %sum_spread.1 = bf16[64,8,1792]{2,1,0:T(8,128)(2,1)} custom-call(bf16[64,8,1792]{2,1,0:T(8,128)(2,1)} %copy-done), custom_call_target="tpu_custom_call" | custom-call | flops 917504 | bytes 3670016 | tf_op jit(solution)/shard_map/sum_spread/pallas_call | solution.py:426
  154.1 9.6 %all-to-all-start.3 = ((bf16[64,8,1792]{2,1,0:T(8,128)(2,1)}), bf16[64,8,1792]{2,1,0:T(8,128)(2,1)S(1)}, u32[]{:S(2)}, u32[]{:S(2)}) async-start(bf16[64,8,1792]{2,1,0:T(8,128)(2,1)} %sum_spread.1), calls=%async_computation.3 | async-start | bytes 3670016 | tf_op jit(solution)/shard_map/all_to_all | solution.py:505
  163.7 1.0 constant_dynamic-update-slice_fusion.1
  164.7 1.0 constant_dynamic-update-slice_fusion
  165.8 0.0 copy-start.7
  165.8 0.0 copy-start.4
  165.8 1.5 collective-permute-start.8
  167.3 2.2 %fusion = f32[512,512]{1,0:T(8,128)S(1)} fusion(bf16[1024,512]{1,0:T(8,128)(2,1)} %bitcast.32, s32[1024]{0:T(1024)S(1)} %eq.10), kind=kOutput, calls=%fused_computation.1 | convolution fusion | flops 537395200 | bytes 2101248 | tf_op jit(solution)/shard_map/dot_general | solution.py:28
  169.5 0.0 collective-permute-done.8
  169.5 0.0 copy-done.7
  169.5 0.0 copy-start.2
  169.5 0.0 copy-start.3
  169.6 0.3 fusion.12
  169.8 0.0 copy-done.4
  169.9 1.1 fusion.4
  171.0 0.1 copy-done.3
  171.1 2.5 %fusion.7 = bf16[512,512]{1,0:T(8,128)(2,1)} fusion(f32[512,512]{1,0:T(8,128)S(1)} %fusion, f32[512,512]{1,0:T(8,128)S(1)} %copy-done.2, bf16[512,512]{1,0:T(8,128)(2,1)S(1)} %collective-permute-done.7, bf16[2,512,512]{2,1,0:T(8,128)(2,1)} %collective-permute-done.6, bf16[2,512,512]{2,1,0:T(8,128)(2,1)} %collective-permute-done.5, ...), kind=kLoop, calls=%fused_computation.10 | loop fusion | flops 3145728 | bytes 5242880 | tf_op jit(solution)/shard_map/convert_element_type | solution.py:547
  173.6 14.6 %all-to-all-done.3 = bf16[64,8,1792]{2,1,0:T(8,128)(2,1)S(1)} async-done(((bf16[64,8,1792]{2,1,0:T(8,128)(2,1)}), bf16[64,8,1792]{2,1,0:T(8,128)(2,1)S(1)}, u32[]{:S(2)}, u32[]{:S(2)}) %all-to-all-start.3) | async-done | bytes 1835040 | tf_op jit(solution)/shard_map/all_to_all | solution.py:505
  188.2 3.2 %collective-permute-start.9 = (bf16[512,1792]{1,0:T(8,128)(2,1)S(1)}, bf16[512,1792]{1,0:T(8,128)(2,1)S(1)}, u32[]{:S(2)}, u32[]{:S(2)}) collective-permute-start(bf16[512,1792]{1,0:T(8,128)(2,1)S(1)} %bitcast.29), channel_id=1, source_target_pairs={{0,32},{32,0},{1,33},{33,1},{2,34},{34,2},{3,35},{35,3},{4,36},{36... | collective-permute-start | bytes 5505032 | tf_op jit(solution)/shard_map/ppermute | solution.py:501
  191.4 2.0 %place.2 = (f32[512,512]{1,0:T(8,128)}, f32[512,1024]{1,0:T(8,128)}, f32[512,1536]{1,0:T(8,128)}, f32[512,512]{1,0:T(8,128)}) custom-call(s32[1]{0:T(128)} %bitcast.core.refs_0_, bf16[512,1792]{1,0:T(8,128)(2,1)S(1)} %bitcast.30), custom_call_target="tpu_custom_call" | custom-call | tf_op jit(solution)/shard_map/place/pallas_call | solution.py:488
  193.4 1.4 collective-permute-done.9.refs_1_
  194.8 2.0 %place.3 = (f32[512,512]{1,0:T(8,128)}, f32[512,1024]{1,0:T(8,128)}, f32[512,1536]{1,0:T(8,128)}, f32[512,512]{1,0:T(8,128)}) custom-call(s32[1]{0:T(128)} %bitcast.core.refs_0_, bf16[512,1792]{1,0:T(8,128)(2,1)S(1)} %collective-permute-done.9.refs_1_, ...), custom_call_target="tpu_custom_call", output_to_operand_aliasing={{0}: (2, {}), {1}: (3, {}), {2}: (4, {}), {3}: (5, {})} | custom-call | tf_op jit(solution)/shard_map/place/pallas_call | solution.py:488
  (7 shorter events, 0.0 us)
Async XLA Ops:
  0.6 16.9 %collective-permute-start.1 = (bf16[512,512]{1,0:T(8,128)(2,1)}, bf16[512,512]{1,0:T(8,128)(2,1)S(1)}, u32[]{:S(2)}, u32[]{:S(2)}) collective-permute-start(bf16[512,512]{1,0:T(8,128)(2,1)} %x0.3), channel_id=1, source_target_pairs={{0,64},{64,0},{1,65},{65,1},{2,66},{66,2},{3,67},{67,3},{4,68},{68... | collective-permute-start | bytes 1572872 | tf_op jit(solution)/shard_map/ppermute | solution.py:501
  2.8 17.4 %collective-permute-start = (bf16[512,512]{1,0:T(8,128)(2,1)}, bf16[512,512]{1,0:T(8,128)(2,1)S(1)}, u32[]{:S(2)}, u32[]{:S(2)}) collective-permute-start(bf16[512,512]{1,0:T(8,128)(2,1)} %x0.3), channel_id=1, source_target_pairs={{0,32},{32,0},{1,33},{33,1},{2,34},{34,2},{3,35},{35,3},{4,36},{36... | collective-permute-start | bytes 1572872 | tf_op jit(solution)/shard_map/ppermute | solution.py:501
  3.7 16.5 %collective-permute-start.3 = (bf16[512,512]{1,0:T(8,128)(2,1)}, bf16[512,512]{1,0:T(8,128)(2,1)S(1)}, u32[]{:S(2)}, u32[]{:S(2)}) collective-permute-start(bf16[512,512]{1,0:T(8,128)(2,1)} %cot0.3), channel_id=1, source_target_pairs={{0,32},{32,0},{1,33},{33,1},{2,34},{34,2},{3,35},{35,3},{4,36},{36... | collective-permute-start | bytes 1572872 | tf_op jit(solution)/shard_map/ppermute | solution.py:501
  7.3 34.5 %all-to-all-start = ((bf16[32,32,512]{2,1,0:T(8,128)(2,1)}), bf16[32,32,512]{2,1,0:T(8,128)(2,1)S(1)}, u32[]{:S(2)}, u32[]{:S(2)}) async-start(bf16[32,32,512]{2,1,0:T(8,128)(2,1)} %bitcast.1), calls=%async_computation | async-start | bytes 2097152 | tf_op jit(solution)/shard_map/all_to_all | solution.py:509
  17.5 2.7 %copy-start.9 = (bf16[512,512]{1,0:T(8,128)(2,1)}, bf16[512,512]{1,0:T(8,128)(2,1)S(1)}, u32[]{:S(2)}) copy-start(bf16[512,512]{1,0:T(8,128)(2,1)S(1)} %collective-permute-done.1.x2) | copy-start | bytes 1572868
  17.5 2.7 %collective-permute-start.2 = (bf16[512,512]{1,0:T(8,128)(2,1)S(1)}, bf16[512,512]{1,0:T(8,128)(2,1)S(1)}, u32[]{:S(2)}, u32[]{:S(2)}) collective-permute-start(bf16[512,512]{1,0:T(8,128)(2,1)S(1)} %collective-permute-done.1.x2), channel_id=1, source_target_pairs={{0,32},{32,0},{1,33},{33,1},{2,34},{34,2},{3,35},{35,3},{4,36},{36... | collective-permute-start | bytes 1572872 | tf_op jit(solution)/shard_map/ppermute | solution.py:501
  20.2 0.8 copy-start.11
  20.2 1.0 copy-start.10
  21.1 0.8 copy-start.12
  41.7 1.0 copy-start.6
  74.2 10.6 %collective-permute-start.4 = (bf16[512,768]{1,0:T(8,128)(2,1)}, bf16[512,768]{1,0:T(8,128)(2,1)S(1)}, u32[]{:S(2)}, u32[]{:S(2)}) collective-permute-start(bf16[512,768]{1,0:T(8,128)(2,1)} %get-tuple-element.48), channel_id=1, source_target_pairs={{0,32},{32,0},{1,33},{33,1},{2,34},{34,2},{3,35},{35,3},{4,36},{36... | collective-permute-start | bytes 2359304 | tf_op jit(solution)/shard_map/ppermute | solution.py:501
  74.4 43.3 %collective-permute-start.5 = (bf16[2,512,512]{2,1,0:T(8,128)(2,1)}, bf16[2,512,512]{2,1,0:T(8,128)(2,1)}, u32[]{:S(2)}, u32[]{:S(2)}) collective-permute-start(bf16[2,512,512]{2,1,0:T(8,128)(2,1)} %get-tuple-element.54), channel_id=1, source_target_pairs={{0,32},{32,0},{1,33},{33,1},{2,34},{34,2},{3,35},{35,3},{4,36},{36... | collective-permute-start | bytes 3145736 | tf_op jit(solution)/shard_map/ppermute | solution.py:501
  74.8 31.7 %all-to-all-start.1 = ((bf16[32,32,512]{2,1,0:T(8,128)(2,1)}), bf16[32,32,512]{2,1,0:T(8,128)(2,1)S(1)}, u32[]{:S(2)}, u32[]{:S(2)}) async-start(bf16[32,32,512]{2,1,0:T(8,128)(2,1)} %bitcast.34), calls=%async_computation.1 | async-start | bytes 2097152 | tf_op jit(solution)/shard_map/all_to_all | solution.py:509
  84.8 0.9 copy-start.8
  106.1 11.6 %copy-start.1 = (bf16[2,512,512]{2,1,0:T(8,128)(2,1)S(1)}, bf16[2,512,512]{2,1,0:T(8,128)(2,1)}, u32[]{:S(2)}) copy-start(bf16[2,512,512]{2,1,0:T(8,128)(2,1)} %get-tuple-element.52) | copy-start | bytes 3145732
  106.1 11.6 %collective-permute-start.6 = (bf16[2,512,512]{2,1,0:T(8,128)(2,1)}, bf16[2,512,512]{2,1,0:T(8,128)(2,1)}, u32[]{:S(2)}, u32[]{:S(2)}) collective-permute-start(bf16[2,512,512]{2,1,0:T(8,128)(2,1)} %get-tuple-element.55), channel_id=1, source_target_pairs={{0,32},{32,0},{1,33},{33,1},{2,34},{34,2},{3,35},{35,3},{4,36},{36... | collective-permute-start | bytes 3145736 | tf_op jit(solution)/shard_map/ppermute | solution.py:501
  106.5 1.0 copy-start.5
  107.5 42.5 %all-to-all-start.2 = ((bf16[64,8,1792]{2,1,0:T(8,128)(2,1)}), bf16[64,8,1792]{2,1,0:T(8,128)(2,1)S(1)}, u32[]{:S(2)}, u32[]{:S(2)}) async-start(bf16[64,8,1792]{2,1,0:T(8,128)(2,1)} %bitcast.31), calls=%async_computation.2 | async-start | bytes 3670016 | tf_op jit(solution)/shard_map/all_to_all | solution.py:505
  119.3 30.7 %collective-permute-start.7 = (bf16[512,512]{1,0:T(8,128)(2,1)S(1)}, bf16[512,512]{1,0:T(8,128)(2,1)S(1)}, u32[]{:S(2)}, u32[]{:S(2)}) collective-permute-start(bf16[512,512]{1,0:T(8,128)(2,1)S(1)} %fusion.10), channel_id=1, source_target_pairs={{0,64},{64,0},{1,65},{65,1},{2,66},{66,2},{3,67},{67,3},{4,68},{68... | collective-permute-start | bytes 1572872 | tf_op jit(solution)/shard_map/ppermute | solution.py:501
  150.0 1.2 copy-start
  154.1 34.1 %all-to-all-start.3 = ((bf16[64,8,1792]{2,1,0:T(8,128)(2,1)}), bf16[64,8,1792]{2,1,0:T(8,128)(2,1)S(1)}, u32[]{:S(2)}, u32[]{:S(2)}) async-start(bf16[64,8,1792]{2,1,0:T(8,128)(2,1)} %sum_spread.1), calls=%async_computation.3 | async-start | bytes 3670016 | tf_op jit(solution)/shard_map/all_to_all | solution.py:505
  165.8 3.8 %copy-start.7 = (bf16[512,512]{1,0:T(8,128)(2,1)S(1)}, bf16[512,512]{1,0:T(8,128)(2,1)}, u32[]{:S(2)}) copy-start(bf16[512,512]{1,0:T(8,128)(2,1)} %wo.3) | copy-start | bytes 1572868
  165.8 4.1 %copy-start.4 = (f32[512,512]{1,0:T(8,128)S(1)}, f32[512,512]{1,0:T(8,128)}, u32[]{:S(2)}) copy-start(f32[512,512]{1,0:T(8,128)} %get-tuple-element.57) | copy-start | bytes 3145732
  165.8 3.7 %collective-permute-start.8 = (bf16[512,256]{1,0:T(8,128)(2,1)S(1)}, bf16[512,256]{1,0:T(8,128)(2,1)S(1)}, u32[]{:S(2)}, u32[]{:S(2)}) collective-permute-start(bf16[512,256]{1,0:T(8,128)(2,1)S(1)} %slice.43), channel_id=1, source_target_pairs={{0,32},{32,0},{1,33},{33,1},{2,34},{34,2},{3,35},{35,3},{4,36},{36... | collective-permute-start | bytes 786440 | tf_op jit(solution)/shard_map/ppermute | solution.py:501
  169.5 1.4 copy-start.2
  169.5 1.5 copy-start.3
  188.2 6.6 %collective-permute-start.9 = (bf16[512,1792]{1,0:T(8,128)(2,1)S(1)}, bf16[512,1792]{1,0:T(8,128)(2,1)S(1)}, u32[]{:S(2)}, u32[]{:S(2)}) collective-permute-start(bf16[512,1792]{1,0:T(8,128)(2,1)S(1)} %bitcast.29), channel_id=1, source_target_pairs={{0,32},{32,0},{1,33},{33,1},{2,34},{34,2},{3,35},{35,3},{4,36},{36... | collective-permute-start | bytes 5505032 | tf_op jit(solution)/shard_map/ppermute | solution.py:501

commit v7 on v6

--- a/solution.py
+++ b/solution.py
@@ -49,11 +49,8 @@
 
     for i in range(3):
         start(wqkv.at[:, pl.ds(pl.multiple_of(off + 512 * i, 128), 128)], w_s.at[:, i * 128 : i * 128 + 128])
-    start(x0, x_s.at[:n, :])
-    for copy in fetch:
-        copy.wait()
-    for i, src in enumerate((x1, x2, x3)):
-        start(src, x_s.at[i * n + n : i * n + 2 * n, :])
+    for i, src in enumerate((x0, x1, x2, x3)):
+        start(src, x_s.at[i * n : i * n + n, :])
     start(wo.at[pl.ds(off, 128), :], wo_s)
     for i, src in enumerate((cot0, cot1)):
         start(src, cot_s.at[i * n : i * n + n, :])
@@ -61,10 +58,12 @@
         start(g_first, grad_s.at[:, :512])
         start(keep, edge_s.at[0])
         start(got, edge_s.at[1])
+    for copy in fetch[:3]:
+        copy.wait()
     wq = w_s[:, :128]
     wkv = w_s[:, 128:]
     for r in chunks:
-        if r.start and r.start % n == 0:
+        if r.start % n == 0:
             fetch[3 + r.start // n].wait()
         kv = dot(x_s[r, :], wkv, NN)
         k_s[r, :] = kv[:, :128].astype(BF)
@@ -380,13 +379,14 @@
     H = pltpu.HBM
     V = pltpu.VMEM
     hbm = pl.BlockSpec(memory_space=pltpu.HBM)
+    vm = pl.BlockSpec(memory_space=pltpu.VMEM)
     sm = pl.BlockSpec(memory_space=pltpu.SMEM)
     table = V(((rows + 1) * 8, 128), F32)
     per_node = V((n * 8, 128), F32)
     return pl.pallas_call(
         edges_kernel,
         out_shape=(H((n, d), F32), H((n, d), F32), H(inc.shape, BF), H((d, 768), BF), H((d, 768), BF)),
-        in_specs=[sm, sm, pl.BlockSpec(memory_space=pltpu.VMEM)] + [hbm] * 5,
+        in_specs=[sm, sm, vm, hbm, vm, hbm, hbm, hbm],
         out_specs=(hbm,) * 5,
         scratch_shapes=[V((rows, d), BF), V((n, d), BF), V(wg.shape, BF), V(ws.shape, BF)]
         + [V((n, d), F32), V((n, d), F32), V(inc.shape, BF), V((2, d, 768), BF), pltpu.SemaphoreType.DMA((10,))]
@@ -395,26 +395,14 @@
         compiler_params=pltpu.CompilerParams(vmem_limit_bytes=56 * MIB),
         cost_estimate=pl.CostEstimate(flops=20 * 10**9, bytes_accessed=8 * MIB, transcendentals=4 * MIB),
         name="edges",
-    )(core, idx, inv, *in_hbm(x, inc, cot, wg, ws))
-
-
-def spread_kernel(got, out, got_s, sum_s, sems):
+    )(core, idx, inv, *in_hbm(x), pltpu.with_memory_space_constraint(inc, pltpu.VMEM), *in_hbm(cot, wg, ws))
+
+
+def spread_kernel(got, out, sum_s, sems):
     chips, _, w = got.shape
-    steps = 8
-    part = chips // steps
-    fetch = [
-        pltpu.make_async_copy(got.at[i * part : i * part + part], got_s.at[i * part : i * part + part], sems.at[i])
-        for i in range(steps)
-    ]
-    for copy in fetch:
-        copy.start()
-    total = jnp.zeros((8, w), F32)
-    for i, copy in enumerate(fetch):
-        copy.wait()
-        for j in range(part):
-            total = total + got_s[i * part + j].astype(F32)
-    sum_s[...] = jnp.broadcast_to(total.astype(BF)[None], sum_s.shape)
-    leave = [pltpu.make_async_copy(sum_s, out.at[i * part : i * part + part], sems.at[i]) for i in range(steps)]
+    part = chips // 8
+    sum_s[...] = jnp.broadcast_to(jnp.sum(got[...].astype(F32), axis=0).astype(BF)[None], sum_s.shape)
+    leave = [pltpu.make_async_copy(sum_s, out.at[i * part : i * part + part], sems.at[i]) for i in range(8)]
     for copy in leave:
         copy.start()
     for copy in leave:
@@ -422,20 +410,15 @@
 
 
 def sum_spread(got):
-    hbm = pl.BlockSpec(memory_space=pltpu.HBM)
     return pl.pallas_call(
         spread_kernel,
         out_shape=pltpu.HBM(got.shape, BF),
-        in_specs=[pl.BlockSpec(memory_space=pl.ANY)],
-        out_specs=hbm,
-        scratch_shapes=[
-            pltpu.VMEM(got.shape, BF),
-            pltpu.VMEM((8,) + got.shape[1:], BF),
-            pltpu.SemaphoreType.DMA((8,)),
-        ],
+        in_specs=[pl.BlockSpec(memory_space=pltpu.VMEM)],
+        out_specs=pl.BlockSpec(memory_space=pltpu.HBM),
+        scratch_shapes=[pltpu.VMEM((8,) + got.shape[1:], BF), pltpu.SemaphoreType.DMA((8,))],
         cost_estimate=pl.CostEstimate(flops=got.size, bytes_accessed=got.size * 4, transcendentals=0),
         name="sum_spread",
-    )(got)
+    )(pltpu.with_memory_space_constraint(got, pltpu.VMEM))
 
 
 def place_kernel(which, *refs):
@@ -540,13 +523,12 @@
     attended = dot(mixed[:n], wo_own, NN) + dot(mixed_sib, wo_sib, NN)
     layer_out = (base + attended).astype(BF)
     pieces = (own_first, own_second, swap(sib_first, "c"), swap(sib_second, "c"))
-    from_far = swap(sum(a[1].astype(F32) for a in pieces).astype(BF), "xl")
-    parts, from_far = lax.optimization_barrier((parts, from_far))
-    feats_grad = (
-        local + sum(a[0].astype(F32) for a in pieces) + from_far.astype(F32) + dot(pick, returned, TN)
-    ).astype(BF)
+    parts, to_far = lax.optimization_barrier((parts, sum(a[1].astype(F32) for a in pieces).astype(BF)))
+    from_far = swap(to_far, "xl")
+    near = local + sum(a[0].astype(F32) for a in pieces) + dot(pick, returned, TN)
     own = chips(sum_spread(parts)).reshape(512, -1)
-    own, layer_out, feats_grad = lax.optimization_barrier((own, layer_out, feats_grad))
+    own, layer_out, near, from_far = lax.optimization_barrier((own, layer_out, near, from_far))
+    feats_grad = (near + from_far.astype(F32)).astype(BF)
     other = swap(own, "c")
     gate_grad, source_grad, qkv_grad, out_grad = place(1, core, other, *place(0, core, own))
     return layer_out, feats_grad, gate_grad, source_grad, qkv_grad, out_grad

time: 200 us -> 189 us (0.945)
  waiting for transfers between devices: 45.5 us -> 37.9 us
  Pallas kernels: 80.1 us -> 77.4 us
  starting transfers between devices: 51 us -> 48.4 us
  matrix products: 6.39 us -> 8.81 us
    ppermute x10, waiting for transfers between devices: 30.9 us -> 21.7 us  [swap(): return lax.ppermute(a, axis, SWAP)]
    all_to_all x2, starting transfers between devices: 19.8 us -> 15.4 us  [chips(): return lax.all_to_all(a, CHIPS, 0, 0, tiled=True)]
    dot_general x4, matrix products: 6.39 us -> 8.81 us  [dot(): return lax.dot_general(a, b, dims, preferred_element_type=F32)]
    unnamed x27 -> x29, local copies, waits for them, and re-layouts: 6.9 us -> 5.72 us
  transfers between devices with their start and end apart: 14 -> 14, of which waited for: 3 -> 5; matrix products, arithmetic and copies ran while one was open for 7% -> 9% of each run, Pallas kernels for 22% -> 23%
where the time goes in v7:
time: 189 us; the launch traced here: 186 us
  Pallas kernels  77.4 us (41%)
  starting transfers between devices  48.4 us (26%)
  waiting for transfers between devices  37.9 us (20%)
  matrix products  8.81 us (5%)
  local copies, waits for them, and re-layouts  8.24 us (4%)
  other arithmetic  4.1 us (2%)
    pallas_call x2, Pallas kernels, attention(): pl.pallas_call(functools.partial(attn_kernel, pair), out_shape=(pltpu.HBM...  38.8 us
    pallas_call x1, Pallas kernels, edges(): pl.pallas_call(edges_kernel, out_shape=(H((n, d), F32), H((n, d), F32), H...  31.4 us
    ppermute x10, waiting for transfers between devices, swap(): return lax.ppermute(a, axis, SWAP)  21.7 us
    all_to_all x2, starting transfers between devices, domains(): lax.all_to_all(a.reshape(32, 32, -1), DOM, 0, 0, tiled=True)  20.2 us
    all_to_all x2, waiting for transfers between devices, chips(): return lax.all_to_all(a, CHIPS, 0, 0, tiled=True)  16.2 us
    all_to_all x2, starting transfers between devices, chips(): return lax.all_to_all(a, CHIPS, 0, 0, tiled=True)  15.4 us
    ppermute x10, starting transfers between devices, swap(): return lax.ppermute(a, axis, SWAP)  12.7 us
    dot_general x4, matrix products, dot(): return lax.dot_general(a, b, dims, preferred_element_type=F32)  8.81 us
  transfers between devices with their start and end apart: 14, of which 5 were waited for; matrix products, arithmetic and copies ran while one was open for 9% of the time, Pallas kernels for 23%

profile of v7, /device:TPU:1, one launch (start us, length us, event | category | flops | bytes accessed | tf_op | source)
XLA Modules:
  0.0 185.8 jit_solution(15759818420045855609)
XLA Ops:
  0.6 2.1 %collective-permute-start.1 = (bf16[512,512]{1,0:T(8,128)(2,1)}, bf16[512,512]{1,0:T(8,128)(2,1)S(1)}, u32[]{:S(2)}, u32[]{:S(2)}) collective-permute-start(bf16[512,512]{1,0:T(8,128)(2,1)} %x0.3), channel_id=1, source_target_pairs={{0,64},{64,0},{1,65},{65,1},{2,66},{66,2},{3,67},{67,3},{4,68},{68... | collective-permute-start | bytes 1572872 | tf_op jit(solution)/shard_map/ppermute | solution.py:484
  2.8 1.0 collective-permute-start
  3.7 0.0 collective-permute-start.3
  3.7 0.8 eq.10
  4.5 2.8 %fusion.2 = bf16[1024,512]{1,0:T(8,128)(2,1)} fusion(bf16[512,512]{1,0:T(8,128)(2,1)} %x0.3, s32[1024]{0:T(1024)S(1)} %eq.10), kind=kOutput, calls=%fused_computation.3 | convolution fusion | flops 537919488 | bytes 1576960 | tf_op jit(solution)/shard_map/dot_general | solution.py:28
  7.3 10.2 %all-to-all-start = ((bf16[32,32,512]{2,1,0:T(8,128)(2,1)}), bf16[32,32,512]{2,1,0:T(8,128)(2,1)S(1)}, u32[]{:S(2)}, u32[]{:S(2)}) async-start(bf16[32,32,512]{2,1,0:T(8,128)(2,1)} %bitcast.1), calls=%async_computation | async-start | bytes 2097152 | tf_op jit(solution)/shard_map/all_to_all | solution.py:492
  17.5 0.0 collective-permute-done.1.x2
  17.5 0.0 copy-start.10
  17.5 1.0 collective-permute-start.2
  18.6 1.6 slots.1
  20.1 0.0 copy-done.10
  20.2 0.0 collective-permute-done.3.cot1
  20.2 0.0 collective-permute-done.x1
  20.2 0.0 copy-start.11
  20.2 0.0 collective-permute-done.2.x3
  20.2 0.8 copy-done.12
  21.0 0.2 copy-done.11
  21.1 0.8 copy-done.13
  21.9 19.2 %attention.2 = (bf16[512,512]{1,0:T(8,128)(2,1)}, bf16[1024,128]{1,0:T(8,128)(2,1)}, bf16[2,512,512]{2,1,0:T(8,128)(2,1)}, bf16[2,512,512]{2,1,0:T(8,128)(2,1)}) custom-call(s32[1]{0:T(128)} %bitcast.core.refs_0_, bf16[512,512]{1,0:T(8,128)(2,1)} %x0.3, bf16[512,512]{1,0:T(8,128)(2,1)} %copy-done.11, bf16[512,512]{1,0:T(8,128)(2,1)} %copy-done.10, ...), custom_call_target="tpu_custom_call" | custom-call | flops 16000000000 | bytes 8388608 | tf_op jit(solution)/shard_map/attention/pallas_call | solution.py:200
  41.1 0.0 all-to-all-done
  41.1 31.4 %edges.1 = (f32[512,512]{1,0:T(8,128)}, f32[512,512]{1,0:T(8,128)}, bf16[1024,512]{1,0:T(8,128)(2,1)}, bf16[512,768]{1,0:T(8,128)(2,1)}, bf16[512,768]{1,0:T(8,128)(2,1)}) custom-call(s32[1]{0:T(128)} %bitcast.core.refs_0_, s32[8,512]{1,0:T(8,128)} %get-tuple-element.45.idx, f32[512,8]{1,0:T(8,128)} %get-tuple-element.46.inv, bf16[512,512]{1,0:T(8,128)(2,1)} %x0.3, ...), custom_call_target="tpu_custom_call" | custom-call | flops 20000000000 | bytes 8388608 | tf_op jit(solution)/shard_map/edges/pallas_call | solution.py:386
  72.6 0.2 collective-permute-start.4
  72.8 10.0 %all-to-all-start.1 = ((bf16[32,32,512]{2,1,0:T(8,128)(2,1)}), bf16[32,32,512]{2,1,0:T(8,128)(2,1)S(1)}, u32[]{:S(2)}, u32[]{:S(2)}) async-start(bf16[32,32,512]{2,1,0:T(8,128)(2,1)} %bitcast.30), calls=%async_computation.1 | async-start | bytes 2097152 | tf_op jit(solution)/shard_map/all_to_all | solution.py:492
  82.7 0.0 collective-permute-done.4.rest_2_
  82.7 0.0 copy-start.9
  82.8 0.9 copy-done.9
  83.6 19.6 %attention.3 = (bf16[512,1792]{1,0:T(8,128)(2,1)}, bf16[1024,128]{1,0:T(8,128)(2,1)}, bf16[2,512,512]{2,1,0:T(8,128)(2,1)}, bf16[2,512,512]{2,1,0:T(8,128)(2,1)}) custom-call(s32[1]{0:T(128)} %bitcast.core.refs_0_, bf16[512,512]{1,0:T(8,128)(2,1)} %x0.3, bf16[512,512]{1,0:T(8,128)(2,1)} %copy-done.11, bf16[512,512]{1,0:T(8,128)(2,1)} %copy-done.10, ...), custom_call_target="tpu_custom_call" | custom-call | flops 16000000000 | bytes 8388608 | tf_op jit(solution)/shard_map/attention/pallas_call | solution.py:200
  103.2 0.0 copy-start.3
  103.3 0.0 all-to-all-done.1
  103.3 0.0 copy-start.1
  103.3 1.0 copy-done.1
  104.3 9.8 %all-to-all-start.2 = ((bf16[64,8,1792]{2,1,0:T(8,128)(2,1)}), bf16[64,8,1792]{2,1,0:T(8,128)(2,1)S(1)}, u32[]{:S(2)}, u32[]{:S(2)}) async-start(bf16[64,8,1792]{2,1,0:T(8,128)(2,1)} %bitcast.28), calls=%async_computation.2 | async-start | bytes 3670016 | tf_op jit(solution)/shard_map/all_to_all | solution.py:488
  114.1 1.4 collective-permute-start.5
  115.5 0.1 collective-permute-start.6
  115.6 2.4 %collective-permute-done.5 = bf16[2,512,512]{2,1,0:T(8,128)(2,1)S(1)} collective-permute-done((bf16[2,512,512]{2,1,0:T(8,128)(2,1)}, bf16[2,512,512]{2,1,0:T(8,128)(2,1)S(1)}, u32[]{:S(2)}, u32[]{:S(2)}) %collective-permute-start.5) | collective-permute-done | bytes 1048608 | tf_op jit(solution)/shard_map/ppermute | solution.py:484
  118.0 1.5 collective-permute-done.6
  119.5 0.0 copy-done.6
  119.5 1.0 copy-done.8
  120.5 0.0 copy-done.3
  120.5 2.1 %fusion.8 = bf16[512,512]{1,0:T(8,128)(2,1)} fusion(bf16[2,512,512]{2,1,0:T(8,128)(2,1)S(1)} %collective-permute-done.6, bf16[2,512,512]{2,1,0:T(8,128)(2,1)S(1)} %collective-permute-done.5, bf16[2,512,512]{2,1,0:T(8,128)(2,1)} %get-tuple-element.54, bf16[2,512,512]{2,1,0:T(8,128)(2,1)S(1)} %copy-done.3), kind=kLoop, calls=%fused_computation.13 | loop fusion | flops 2097152 | bytes 2621440 | tf_op jit(solution)/shard_map/add | solution.py:526
  122.6 16.2 %all-to-all-done.2.got = bf16[64,8,1792]{2,1,0:T(8,128)(2,1)S(1)} async-done(((bf16[64,8,1792]{2,1,0:T(8,128)(2,1)}), bf16[64,8,1792]{2,1,0:T(8,128)(2,1)S(1)}, u32[]{:S(2)}, u32[]{:S(2)}) %all-to-all-start.2) | async-done | bytes 1835040 | tf_op jit(solution)/shard_map/all_to_all | solution.py:488
  138.8 1.6 sum_spread.1
  140.4 5.6 %all-to-all-start.3 = ((bf16[64,8,1792]{2,1,0:T(8,128)(2,1)}), bf16[64,8,1792]{2,1,0:T(8,128)(2,1)S(1)}, u32[]{:S(2)}, u32[]{:S(2)}) async-start(bf16[64,8,1792]{2,1,0:T(8,128)(2,1)} %sum_spread.1), calls=%async_computation.3 | async-start | bytes 3670016 | tf_op jit(solution)/shard_map/all_to_all | solution.py:488
  146.0 0.0 copy-start
  146.0 1.1 constant_dynamic-update-slice_fusion.1
  147.1 1.0 constant_dynamic-update-slice_fusion
  148.1 0.7 slice.43
  148.8 2.3 %collective-permute-start.7 = (bf16[512,256]{1,0:T(8,128)(2,1)}, bf16[512,256]{1,0:T(8,128)(2,1)}, u32[]{:S(2)}, u32[]{:S(2)}) collective-permute-start(bf16[512,256]{1,0:T(8,128)(2,1)} %slice.43), channel_id=1, source_target_pairs={{0,32},{32,0},{1,33},{33,1},{2,34},{34,2},{3,35},{35,3},{4,36},{36... | collective-permute-start | bytes 786440 | tf_op jit(solution)/shard_map/ppermute | solution.py:484
  151.1 1.5 collective-permute-done.7
  152.6 1.5 fusion.10
  154.0 1.5 collective-permute-start.8
  155.5 0.0 copy-done
  155.5 2.0 %fusion.4 = bf16[512,512]{1,0:T(8,128)(2,1)} fusion(f32[512,512]{1,0:T(8,128)S(1)} %copy-done, f32[512,512]{1,0:T(8,128)S(1)} %fusion.10, bf16[1024,256]{1,0:T(8,128)(2,1)S(1)} %constant_dynamic-update-slice_fusion, bf16[2,256,512]{2,1,0:T(8,128)(2,1)} %bitcast.32, s32[]{:T(128)S(6)} %select_n.7), kind=kOutput, calls=%fused_computation.6 | convolution fusion | flops 135004160 | bytes 3145732 | tf_op jit(solution)/shard_map/dot_general | solution.py:28
  157.6 0.0 copy-done.2
  157.6 0.0 copy-done.4
  157.6 0.0 copy-done.7
  157.6 2.5 %fusion.5 = f32[512,512]{1,0:T(8,128)S(1)} fusion(f32[512,512]{1,0:T(8,128)} %get-tuple-element.61, bf16[2,512,512]{2,1,0:T(8,128)(2,1)} %copy-done.8, bf16[2,512,512]{2,1,0:T(8,128)(2,1)S(1)} %copy-done.7, bf16[2,512,512]{2,1,0:T(8,128)(2,1)S(1)} %copy-done.5, bf16[2,512,512]{2,1,0:T(8,128)(2,1)S(1)} %copy-done.4, bf16[1024,512]{1,0:T(8,128)(2,1)S(1)} %bitcast.29, ...), kind=kOutput, calls=%fused_computation.8 | convolution fusion | flops 539754496 | bytes 5246976 | tf_op jit(solution)/shard_map/dot_general | solution.py:28
  160.1 16.3 %collective-permute-done.8 = bf16[512,512]{1,0:T(8,128)(2,1)} collective-permute-done((bf16[512,512]{1,0:T(8,128)(2,1)}, bf16[512,512]{1,0:T(8,128)(2,1)}, u32[]{:S(2)}, u32[]{:S(2)}) %collective-permute-start.8) | collective-permute-done | bytes 524320 | tf_op jit(solution)/shard_map/ppermute | solution.py:484
  176.4 0.0 all-to-all-done.3
  176.4 3.2 %collective-permute-start.9 = (bf16[512,1792]{1,0:T(8,128)(2,1)S(1)}, bf16[512,1792]{1,0:T(8,128)(2,1)S(1)}, u32[]{:S(2)}, u32[]{:S(2)}) collective-permute-start(bf16[512,1792]{1,0:T(8,128)(2,1)S(1)} %bitcast.25), channel_id=1, source_target_pairs={{0,32},{32,0},{1,33},{33,1},{2,34},{34,2},{3,35},{35,3},{4,36},{36... | collective-permute-start | bytes 5505032 | tf_op jit(solution)/shard_map/ppermute | solution.py:484
  179.6 2.0 %place.2 = (f32[512,512]{1,0:T(8,128)}, f32[512,1024]{1,0:T(8,128)}, f32[512,1536]{1,0:T(8,128)}, f32[512,512]{1,0:T(8,128)}) custom-call(s32[1]{0:T(128)} %bitcast.core.refs_0_, bf16[512,1792]{1,0:T(8,128)(2,1)S(1)} %bitcast.26), custom_call_target="tpu_custom_call" | custom-call | tf_op jit(solution)/shard_map/place/pallas_call | solution.py:471
  181.6 2.0 %add_convert_fusion = bf16[512,512]{1,0:T(8,128)(2,1)} fusion(f32[512,512]{1,0:T(8,128)S(1)} %fusion.5, bf16[512,512]{1,0:T(8,128)(2,1)} %collective-permute-done.8), kind=kLoop, calls=%fused_computation.9 | loop fusion | flops 786432 | bytes 2097152 | tf_op jit(solution)/shard_map/convert_element_type | solution.py:531
  183.6 0.0 collective-permute-done.9.refs_1_
  183.6 2.0 %place.3 = (f32[512,512]{1,0:T(8,128)}, f32[512,1024]{1,0:T(8,128)}, f32[512,1536]{1,0:T(8,128)}, f32[512,512]{1,0:T(8,128)}) custom-call(s32[1]{0:T(128)} %bitcast.core.refs_0_, bf16[512,1792]{1,0:T(8,128)(2,1)S(1)} %collective-permute-done.9.refs_1_, ...), custom_call_target="tpu_custom_call", output_to_operand_aliasing={{0}: (2, {}), {1}: (3, {}), {2}: (4, {}), {3}: (5, {})} | custom-call | tf_op jit(solution)/shard_map/place/pallas_call | solution.py:471
  (9 shorter events, 0.0 us)
Async XLA Ops:
  0.6 16.9 %collective-permute-start.1 = (bf16[512,512]{1,0:T(8,128)(2,1)}, bf16[512,512]{1,0:T(8,128)(2,1)S(1)}, u32[]{:S(2)}, u32[]{:S(2)}) collective-permute-start(bf16[512,512]{1,0:T(8,128)(2,1)} %x0.3), channel_id=1, source_target_pairs={{0,64},{64,0},{1,65},{65,1},{2,66},{66,2},{3,67},{67,3},{4,68},{68... | collective-permute-start | bytes 1572872 | tf_op jit(solution)/shard_map/ppermute | solution.py:484
  2.8 17.4 %collective-permute-start = (bf16[512,512]{1,0:T(8,128)(2,1)}, bf16[512,512]{1,0:T(8,128)(2,1)S(1)}, u32[]{:S(2)}, u32[]{:S(2)}) collective-permute-start(bf16[512,512]{1,0:T(8,128)(2,1)} %x0.3), channel_id=1, source_target_pairs={{0,32},{32,0},{1,33},{33,1},{2,34},{34,2},{3,35},{35,3},{4,36},{36... | collective-permute-start | bytes 1572872 | tf_op jit(solution)/shard_map/ppermute | solution.py:484
  3.7 16.4 %collective-permute-start.3 = (bf16[512,512]{1,0:T(8,128)(2,1)}, bf16[512,512]{1,0:T(8,128)(2,1)S(1)}, u32[]{:S(2)}, u32[]{:S(2)}) collective-permute-start(bf16[512,512]{1,0:T(8,128)(2,1)} %cot0.3), channel_id=1, source_target_pairs={{0,32},{32,0},{1,33},{33,1},{2,34},{34,2},{3,35},{35,3},{4,36},{36... | collective-permute-start | bytes 1572872 | tf_op jit(solution)/shard_map/ppermute | solution.py:484
  7.3 33.8 %all-to-all-start = ((bf16[32,32,512]{2,1,0:T(8,128)(2,1)}), bf16[32,32,512]{2,1,0:T(8,128)(2,1)S(1)}, u32[]{:S(2)}, u32[]{:S(2)}) async-start(bf16[32,32,512]{2,1,0:T(8,128)(2,1)} %bitcast.1), calls=%async_computation | async-start | bytes 2097152 | tf_op jit(solution)/shard_map/all_to_all | solution.py:492
  17.5 2.6 %copy-start.10 = (bf16[512,512]{1,0:T(8,128)(2,1)}, bf16[512,512]{1,0:T(8,128)(2,1)S(1)}, u32[]{:S(2)}) copy-start(bf16[512,512]{1,0:T(8,128)(2,1)S(1)} %collective-permute-done.1.x2) | copy-start | bytes 1572868
  17.5 2.7 %collective-permute-start.2 = (bf16[512,512]{1,0:T(8,128)(2,1)S(1)}, bf16[512,512]{1,0:T(8,128)(2,1)S(1)}, u32[]{:S(2)}, u32[]{:S(2)}) collective-permute-start(bf16[512,512]{1,0:T(8,128)(2,1)S(1)} %collective-permute-done.1.x2), channel_id=1, source_target_pairs={{0,32},{32,0},{1,33},{33,1},{2,34},{34,2},{3,35},{35,3},{4,36},{36... | collective-permute-start | bytes 1572872 | tf_op jit(solution)/shard_map/ppermute | solution.py:484
  20.2 0.8 copy-start.12
  20.2 1.0 copy-start.11
  21.1 0.8 copy-start.13
  72.6 10.2 %collective-permute-start.4 = (bf16[512,768]{1,0:T(8,128)(2,1)}, bf16[512,768]{1,0:T(8,128)(2,1)S(1)}, u32[]{:S(2)}, u32[]{:S(2)}) collective-permute-start(bf16[512,768]{1,0:T(8,128)(2,1)} %get-tuple-element.49), channel_id=1, source_target_pairs={{0,32},{32,0},{1,33},{33,1},{2,34},{34,2},{3,35},{35,3},{4,36},{36... | collective-permute-start | bytes 2359304 | tf_op jit(solution)/shard_map/ppermute | solution.py:484
  72.8 30.5 %all-to-all-start.1 = ((bf16[32,32,512]{2,1,0:T(8,128)(2,1)}), bf16[32,32,512]{2,1,0:T(8,128)(2,1)S(1)}, u32[]{:S(2)}, u32[]{:S(2)}) async-start(bf16[32,32,512]{2,1,0:T(8,128)(2,1)} %bitcast.30), calls=%async_computation.1 | async-start | bytes 2097152 | tf_op jit(solution)/shard_map/all_to_all | solution.py:492
  82.7 0.9 copy-start.9
  103.2 17.3 %copy-start.3 = (bf16[2,512,512]{2,1,0:T(8,128)(2,1)S(1)}, bf16[2,512,512]{2,1,0:T(8,128)(2,1)}, u32[]{:S(2)}) copy-start(bf16[2,512,512]{2,1,0:T(8,128)(2,1)} %get-tuple-element.53) | copy-start | bytes 3145732
  103.3 1.0 copy-start.1
  104.3 34.5 %all-to-all-start.2 = ((bf16[64,8,1792]{2,1,0:T(8,128)(2,1)}), bf16[64,8,1792]{2,1,0:T(8,128)(2,1)S(1)}, u32[]{:S(2)}, u32[]{:S(2)}) async-start(bf16[64,8,1792]{2,1,0:T(8,128)(2,1)} %bitcast.28), calls=%async_computation.2 | async-start | bytes 3670016 | tf_op jit(solution)/shard_map/all_to_all | solution.py:488
  114.1 3.9 %collective-permute-start.5 = (bf16[2,512,512]{2,1,0:T(8,128)(2,1)}, bf16[2,512,512]{2,1,0:T(8,128)(2,1)S(1)}, u32[]{:S(2)}, u32[]{:S(2)}) collective-permute-start(bf16[2,512,512]{2,1,0:T(8,128)(2,1)} %get-tuple-element.55), channel_id=1, source_target_pairs={{0,32},{32,0},{1,33},{33,1},{2,34},{34,2},{3,35},{35,3},{4,36},{36... | collective-permute-start | bytes 3145736 | tf_op jit(solution)/shard_map/ppermute | solution.py:484
  115.5 4.0 %collective-permute-start.6 = (bf16[2,512,512]{2,1,0:T(8,128)(2,1)}, bf16[2,512,512]{2,1,0:T(8,128)(2,1)S(1)}, u32[]{:S(2)}, u32[]{:S(2)}) collective-permute-start(bf16[2,512,512]{2,1,0:T(8,128)(2,1)} %get-tuple-element.56), channel_id=1, source_target_pairs={{0,32},{32,0},{1,33},{33,1},{2,34},{34,2},{3,35},{35,3},{4,36},{36... | collective-permute-start | bytes 3145736 | tf_op jit(solution)/shard_map/ppermute | solution.py:484
  118.0 1.5 copy-start.6
  119.5 1.0 copy-start.8
  140.4 36.0 %all-to-all-start.3 = ((bf16[64,8,1792]{2,1,0:T(8,128)(2,1)}), bf16[64,8,1792]{2,1,0:T(8,128)(2,1)S(1)}, u32[]{:S(2)}, u32[]{:S(2)}) async-start(bf16[64,8,1792]{2,1,0:T(8,128)(2,1)} %sum_spread.1), calls=%async_computation.3 | async-start | bytes 3670016 | tf_op jit(solution)/shard_map/all_to_all | solution.py:488
  146.0 9.6 %copy-start = (f32[512,512]{1,0:T(8,128)S(1)}, f32[512,512]{1,0:T(8,128)}, u32[]{:S(2)}) copy-start(f32[512,512]{1,0:T(8,128)} %get-tuple-element.58) | copy-start | bytes 3145732
  148.8 3.8 %collective-permute-start.7 = (bf16[512,256]{1,0:T(8,128)(2,1)}, bf16[512,256]{1,0:T(8,128)(2,1)}, u32[]{:S(2)}, u32[]{:S(2)}) collective-permute-start(bf16[512,256]{1,0:T(8,128)(2,1)} %slice.43), channel_id=1, source_target_pairs={{0,32},{32,0},{1,33},{33,1},{2,34},{34,2},{3,35},{35,3},{4,36},{36... | collective-permute-start | bytes 786440 | tf_op jit(solution)/shard_map/ppermute | solution.py:484
  152.6 5.0 %copy-start.2 = (bf16[32,32,512]{2,1,0:T(8,128)(2,1)S(1)}, bf16[32,32,512]{2,1,0:T(8,128)(2,1)}, u32[]{:S(2)}) copy-start(bf16[32,32,512]{2,1,0:T(8,128)(2,1)} %copy-done.1) | copy-start | bytes 3145732
  152.6 5.0 %copy-start.4 = (bf16[2,512,512]{2,1,0:T(8,128)(2,1)S(1)}, bf16[2,512,512]{2,1,0:T(8,128)(2,1)}, u32[]{:S(2)}) copy-start(bf16[2,512,512]{2,1,0:T(8,128)(2,1)} %get-tuple-element.53) | copy-start | bytes 3145732
  152.6 5.0 %copy-start.5 = (bf16[2,512,512]{2,1,0:T(8,128)(2,1)S(1)}, bf16[2,512,512]{2,1,0:T(8,128)(2,1)}, u32[]{:S(2)}) copy-start(bf16[2,512,512]{2,1,0:T(8,128)(2,1)} %get-tuple-element.54) | copy-start | bytes 3145732
  152.6 5.0 %copy-start.7 = (bf16[2,512,512]{2,1,0:T(8,128)(2,1)S(1)}, bf16[2,512,512]{2,1,0:T(8,128)(2,1)}, u32[]{:S(2)}) copy-start(bf16[2,512,512]{2,1,0:T(8,128)(2,1)} %copy-done.6) | copy-start | bytes 3145732
  154.0 22.3 %collective-permute-start.8 = (bf16[512,512]{1,0:T(8,128)(2,1)}, bf16[512,512]{1,0:T(8,128)(2,1)}, u32[]{:S(2)}, u32[]{:S(2)}) collective-permute-start(bf16[512,512]{1,0:T(8,128)(2,1)} %fusion.8), channel_id=1, source_target_pairs={{0,64},{64,0},{1,65},{65,1},{2,66},{66,2},{3,67},{67,3},{4,68},{68... | collective-permute-start | bytes 1572872 | tf_op jit(solution)/shard_map/ppermute | solution.py:484
  176.4 7.2 %collective-permute-start.9 = (bf16[512,1792]{1,0:T(8,128)(2,1)S(1)}, bf16[512,1792]{1,0:T(8,128)(2,1)S(1)}, u32[]{:S(2)}, u32[]{:S(2)}) collective-permute-start(bf16[512,1792]{1,0:T(8,128)(2,1)S(1)} %bitcast.25), channel_id=1, source_target_pairs={{0,32},{32,0},{1,33},{33,1},{2,34},{34,2},{3,35},{35,3},{4,36},{36... | collective-permute-start | bytes 5505032 | tf_op jit(solution)/shard_map/ppermute | solution.py:484

commit v8 on v7

--- a/solution.py
+++ b/solution.py
@@ -16,7 +16,7 @@
 CK = 256
 QB = 256
 NACC = 2
-UN = 4
+UN = 8
 ALL = ("xl", "c", "z", "y", "xh")
 CHIPS = ("xl", "z", "y", "xh")
 DOM = ("z", "y", "xh")
@@ -197,10 +197,12 @@
     wide = 1792 if pair else 512
     V = pltpu.VMEM
     hbm = pl.BlockSpec(memory_space=pltpu.HBM)
+    vm = pl.BlockSpec(memory_space=pltpu.VMEM)
+    arrived = [pltpu.with_memory_space_constraint(a, pltpu.VMEM) for a in first[2:]]
     return pl.pallas_call(
         functools.partial(attn_kernel, pair),
         out_shape=(pltpu.HBM((512, wide), BF), pltpu.HBM((nq, hw), BF), pltpu.HBM((2, n, d), BF), pltpu.HBM((2, n, d), BF)),
-        in_specs=[pl.BlockSpec(memory_space=pltpu.SMEM)] + [hbm] * (8 + len(first)),
+        in_specs=[pl.BlockSpec(memory_space=pltpu.SMEM)] + [hbm] * (8 + len(first[:2])) + [vm] * len(first[2:]),
         out_specs=(hbm,) * 4,
         scratch_shapes=[V((seq, d), BF), V((nq, d), BF), V((d, 3 * hw), BF), V((hw, d), BF)]
         + [V((512, wide), BF), V((seq, d), BF), V((nq, hw), BF), V((2, 512, 768) if pair else (2, 8, 128), BF)]
@@ -214,7 +216,7 @@
         compiler_params=pltpu.CompilerParams(vmem_limit_bytes=40 * MIB),
         cost_estimate=pl.CostEstimate(flops=16 * 10**9, bytes_accessed=8 * MIB, transcendentals=4 * MIB),
         name="attention",
-    )(core, *in_hbm(*xs, *cots, wqkv, wo, *first))
+    )(core, *in_hbm(*xs, *cots, wqkv, wo, *first[:2]), *arrived)
 
 
 def slots_kernel(slots, mask, idx, inv):
@@ -241,7 +243,7 @@
     accs = rest[16:]
     n, d = cot.shape
     rows = tab.shape[0]
-    R = 128
+    R = 256
     fetch = []
     for src, dst in ((ws_i, ws), (x_i, tab.at[:n, :]), (inc_i, tab.at[n:, :]), (wg_i, wg), (cot_i, cot)):
         fetch.append(pltpu.make_async_copy(src, dst, sems.at[len(fetch)]))

time: 189 us -> 184 us (0.974)
  Pallas kernels: 77.4 us -> 73.5 us
    pallas_call x1, Pallas kernels: 31.4 us -> 27.6 us  [edges(): pl.pallas_call(edges_kernel, out_shape=(H((n, d), F32), H((n, d), F32), H...]
    unnamed x29 -> x27, local copies, waits for them, and re-layouts: 5.72 us -> 4.85 us
where the time goes in v8:
time: 184 us; the launch traced here: 181 us
  Pallas kernels  73.5 us (40%)
  starting transfers between devices  47.7 us (26%)
  waiting for transfers between devices  37.9 us (21%)
  matrix products  8.81 us (5%)
  local copies, waits for them, and re-layouts  7.38 us (4%)
  other arithmetic  4.1 us (2%)
    pallas_call x2, Pallas kernels, attention(): pl.pallas_call(functools.partial(attn_kernel, pair), out_shape=(pltpu.HBM...  38.8 us
    pallas_call x1, Pallas kernels, edges(): pl.pallas_call(edges_kernel, out_shape=(H((n, d), F32), H((n, d), F32), H...  27.6 us
    ppermute x10, waiting for transfers between devices, swap(): return lax.ppermute(a, axis, SWAP)  21.5 us
    all_to_all x2, starting transfers between devices, domains(): lax.all_to_all(a.reshape(32, 32, -1), DOM, 0, 0, tiled=True)  19.7 us
    all_to_all x2, waiting for transfers between devices, chips(): return lax.all_to_all(a, CHIPS, 0, 0, tiled=True)  16.4 us
    all_to_all x2, starting transfers between devices, chips(): return lax.all_to_all(a, CHIPS, 0, 0, tiled=True)  15.2 us
    ppermute x10, starting transfers between devices, swap(): return lax.ppermute(a, axis, SWAP)  12.8 us
    dot_general x4, matrix products, dot(): return lax.dot_general(a, b, dims, preferred_element_type=F32)  8.81 us
  transfers between devices with their start and end apart: 14, of which 5 were waited for; matrix products, arithmetic and copies ran while one was open for 9% of the time, Pallas kernels for 23%

profile of v8, /device:TPU:1, one launch (start us, length us, event | category | flops | bytes accessed | tf_op | source)
XLA Modules:
  0.0 180.5 jit_solution(3188952524647016512)
XLA Ops:
  0.6 2.1 %collective-permute-start.1 = (bf16[512,512]{1,0:T(8,128)(2,1)}, bf16[512,512]{1,0:T(8,128)(2,1)S(1)}, u32[]{:S(2)}, u32[]{:S(2)}) collective-permute-start(bf16[512,512]{1,0:T(8,128)(2,1)} %x0.3), channel_id=1, source_target_pairs={{0,64},{64,0},{1,65},{65,1},{2,66},{66,2},{3,67},{67,3},{4,68},{68... | collective-permute-start | bytes 1572872 | tf_op jit(solution)/shard_map/ppermute | solution.py:486
  2.8 1.0 collective-permute-start
  3.7 0.0 collective-permute-start.3
  3.7 0.8 eq.10
  4.5 2.8 %fusion.2 = bf16[1024,512]{1,0:T(8,128)(2,1)} fusion(bf16[512,512]{1,0:T(8,128)(2,1)} %x0.3, s32[1024]{0:T(1024)S(1)} %eq.10), kind=kOutput, calls=%fused_computation.3 | convolution fusion | flops 537919488 | bytes 1576960 | tf_op jit(solution)/shard_map/dot_general | solution.py:28
  7.3 10.2 %all-to-all-start = ((bf16[32,32,512]{2,1,0:T(8,128)(2,1)}), bf16[32,32,512]{2,1,0:T(8,128)(2,1)S(1)}, u32[]{:S(2)}, u32[]{:S(2)}) async-start(bf16[32,32,512]{2,1,0:T(8,128)(2,1)} %bitcast.1), calls=%async_computation | async-start | bytes 2097152 | tf_op jit(solution)/shard_map/all_to_all | solution.py:494
  17.5 0.0 collective-permute-done.1.x2
  17.5 0.0 copy-start.9
  17.5 1.0 collective-permute-start.2
  18.6 1.6 slots.1
  20.1 0.0 copy-done.9
  20.1 0.0 collective-permute-done.3.cot1
  20.2 0.0 copy-start.11
  20.2 0.0 collective-permute-done.x1
  20.2 0.0 copy-start.10
  20.2 0.0 collective-permute-done.2.x3
  20.2 0.8 copy-done.11
  21.0 0.2 copy-done.10
  21.1 0.8 copy-done.12
  21.9 19.2 %attention.2 = (bf16[512,512]{1,0:T(8,128)(2,1)}, bf16[1024,128]{1,0:T(8,128)(2,1)}, bf16[2,512,512]{2,1,0:T(8,128)(2,1)}, bf16[2,512,512]{2,1,0:T(8,128)(2,1)}) custom-call(s32[1]{0:T(128)} %bitcast.core.refs_0_, bf16[512,512]{1,0:T(8,128)(2,1)} %x0.3, bf16[512,512]{1,0:T(8,128)(2,1)} %copy-done.10, bf16[512,512]{1,0:T(8,128)(2,1)} %copy-done.9, ...), custom_call_target="tpu_custom_call" | custom-call | flops 16000000000 | bytes 8388608 | tf_op jit(solution)/shard_map/attention/pallas_call | solution.py:202
  41.1 0.0 all-to-all-done
  41.1 27.6 %edges.1 = (f32[512,512]{1,0:T(8,128)}, f32[512,512]{1,0:T(8,128)}, bf16[1024,512]{1,0:T(8,128)(2,1)}, bf16[512,768]{1,0:T(8,128)(2,1)}, bf16[512,768]{1,0:T(8,128)(2,1)}) custom-call(s32[1]{0:T(128)} %bitcast.core.refs_0_, s32[8,512]{1,0:T(8,128)} %get-tuple-element.45.idx, f32[512,8]{1,0:T(8,128)} %get-tuple-element.46.inv, bf16[512,512]{1,0:T(8,128)(2,1)} %x0.3, ...), custom_call_target="tpu_custom_call" | custom-call | flops 20000000000 | bytes 8388608 | tf_op jit(solution)/shard_map/edges/pallas_call | solution.py:388
  68.7 0.2 collective-permute-start.4
  68.8 9.5 %all-to-all-start.1 = ((bf16[32,32,512]{2,1,0:T(8,128)(2,1)}), bf16[32,32,512]{2,1,0:T(8,128)(2,1)S(1)}, u32[]{:S(2)}, u32[]{:S(2)}) async-start(bf16[32,32,512]{2,1,0:T(8,128)(2,1)} %bitcast.30), calls=%async_computation.1 | async-start | bytes 2097152 | tf_op jit(solution)/shard_map/all_to_all | solution.py:494
  78.4 0.0 collective-permute-done.4.rest_2_
  78.4 19.6 %attention.3 = (bf16[512,1792]{1,0:T(8,128)(2,1)}, bf16[1024,128]{1,0:T(8,128)(2,1)}, bf16[2,512,512]{2,1,0:T(8,128)(2,1)}, bf16[2,512,512]{2,1,0:T(8,128)(2,1)}) custom-call(s32[1]{0:T(128)} %bitcast.core.refs_0_, bf16[512,512]{1,0:T(8,128)(2,1)} %x0.3, bf16[512,512]{1,0:T(8,128)(2,1)} %copy-done.10, bf16[512,512]{1,0:T(8,128)(2,1)} %copy-done.9, ...), custom_call_target="tpu_custom_call" | custom-call | flops 16000000000 | bytes 8388608 | tf_op jit(solution)/shard_map/attention/pallas_call | solution.py:202
  98.0 0.0 copy-start.3
  98.0 0.0 all-to-all-done.1
  98.0 0.0 copy-start.1
  98.0 1.0 copy-done.1
  99.1 9.8 %all-to-all-start.2 = ((bf16[64,8,1792]{2,1,0:T(8,128)(2,1)}), bf16[64,8,1792]{2,1,0:T(8,128)(2,1)S(1)}, u32[]{:S(2)}, u32[]{:S(2)}) async-start(bf16[64,8,1792]{2,1,0:T(8,128)(2,1)} %bitcast.28), calls=%async_computation.2 | async-start | bytes 3670016 | tf_op jit(solution)/shard_map/all_to_all | solution.py:490
  108.9 1.4 collective-permute-start.5
  110.3 0.1 collective-permute-start.6
  110.4 2.4 %collective-permute-done.5 = bf16[2,512,512]{2,1,0:T(8,128)(2,1)S(1)} collective-permute-done((bf16[2,512,512]{2,1,0:T(8,128)(2,1)}, bf16[2,512,512]{2,1,0:T(8,128)(2,1)S(1)}, u32[]{:S(2)}, u32[]{:S(2)}) %collective-permute-start.5) | collective-permute-done | bytes 1048608 | tf_op jit(solution)/shard_map/ppermute | solution.py:486
  112.8 1.5 collective-permute-done.6
  114.3 0.0 copy-done.6
  114.3 1.0 copy-done.8
  115.2 0.0 copy-done.3
  115.2 2.1 %fusion.8 = bf16[512,512]{1,0:T(8,128)(2,1)} fusion(bf16[2,512,512]{2,1,0:T(8,128)(2,1)S(1)} %collective-permute-done.6, bf16[2,512,512]{2,1,0:T(8,128)(2,1)S(1)} %collective-permute-done.5, bf16[2,512,512]{2,1,0:T(8,128)(2,1)} %get-tuple-element.54, bf16[2,512,512]{2,1,0:T(8,128)(2,1)S(1)} %copy-done.3), kind=kLoop, calls=%fused_computation.13 | loop fusion | flops 2097152 | bytes 2621440 | tf_op jit(solution)/shard_map/add | solution.py:528
  117.3 16.4 %all-to-all-done.2.got = bf16[64,8,1792]{2,1,0:T(8,128)(2,1)S(1)} async-done(((bf16[64,8,1792]{2,1,0:T(8,128)(2,1)}), bf16[64,8,1792]{2,1,0:T(8,128)(2,1)S(1)}, u32[]{:S(2)}, u32[]{:S(2)}) %all-to-all-start.2) | async-done | bytes 1835040 | tf_op jit(solution)/shard_map/all_to_all | solution.py:490
  133.7 1.6 sum_spread.1
  135.3 5.3 %all-to-all-start.3 = ((bf16[64,8,1792]{2,1,0:T(8,128)(2,1)}), bf16[64,8,1792]{2,1,0:T(8,128)(2,1)S(1)}, u32[]{:S(2)}, u32[]{:S(2)}) async-start(bf16[64,8,1792]{2,1,0:T(8,128)(2,1)} %sum_spread.1), calls=%async_computation.3 | async-start | bytes 3670016 | tf_op jit(solution)/shard_map/all_to_all | solution.py:490
  140.6 0.0 copy-start
  140.6 1.1 constant_dynamic-update-slice_fusion.1
  141.7 1.0 constant_dynamic-update-slice_fusion
  142.7 0.7 slice.43
  143.5 2.4 %collective-permute-start.7 = (bf16[512,256]{1,0:T(8,128)(2,1)}, bf16[512,256]{1,0:T(8,128)(2,1)}, u32[]{:S(2)}, u32[]{:S(2)}) collective-permute-start(bf16[512,256]{1,0:T(8,128)(2,1)} %slice.43), channel_id=1, source_target_pairs={{0,32},{32,0},{1,33},{33,1},{2,34},{34,2},{3,35},{35,3},{4,36},{36... | collective-permute-start | bytes 786440 | tf_op jit(solution)/shard_map/ppermute | solution.py:486
  145.8 1.5 collective-permute-done.7
  147.3 1.5 fusion.10
  148.8 1.5 collective-permute-start.8
  150.3 0.0 copy-done
  150.3 2.0 %fusion.4 = bf16[512,512]{1,0:T(8,128)(2,1)} fusion(f32[512,512]{1,0:T(8,128)S(1)} %copy-done, f32[512,512]{1,0:T(8,128)S(1)} %fusion.10, bf16[1024,256]{1,0:T(8,128)(2,1)S(1)} %constant_dynamic-update-slice_fusion, bf16[2,256,512]{2,1,0:T(8,128)(2,1)} %bitcast.32, s32[]{:T(128)S(6)} %select_n.7), kind=kOutput, calls=%fused_computation.6 | convolution fusion | flops 135004160 | bytes 3145732 | tf_op jit(solution)/shard_map/dot_general | solution.py:28
  152.3 0.0 copy-done.2
  152.3 0.0 copy-done.4
  152.3 0.0 copy-done.5
  152.3 0.0 copy-done.7
  152.4 2.5 %fusion.5 = f32[512,512]{1,0:T(8,128)S(1)} fusion(f32[512,512]{1,0:T(8,128)} %get-tuple-element.61, bf16[2,512,512]{2,1,0:T(8,128)(2,1)} %copy-done.8, bf16[2,512,512]{2,1,0:T(8,128)(2,1)S(1)} %copy-done.7, bf16[2,512,512]{2,1,0:T(8,128)(2,1)S(1)} %copy-done.5, bf16[2,512,512]{2,1,0:T(8,128)(2,1)S(1)} %copy-done.4, bf16[1024,512]{1,0:T(8,128)(2,1)S(1)} %bitcast.29, ...), kind=kOutput, calls=%fused_computation.8 | convolution fusion | flops 539754496 | bytes 5246976 | tf_op jit(solution)/shard_map/dot_general | solution.py:28
  154.9 16.0 %collective-permute-done.8 = bf16[512,512]{1,0:T(8,128)(2,1)} collective-permute-done((bf16[512,512]{1,0:T(8,128)(2,1)}, bf16[512,512]{1,0:T(8,128)(2,1)}, u32[]{:S(2)}, u32[]{:S(2)}) %collective-permute-start.8) | collective-permute-done | bytes 524320 | tf_op jit(solution)/shard_map/ppermute | solution.py:486
  170.9 0.0 all-to-all-done.3
  170.9 3.3 %collective-permute-start.9 = (bf16[512,1792]{1,0:T(8,128)(2,1)S(1)}, bf16[512,1792]{1,0:T(8,128)(2,1)S(1)}, u32[]{:S(2)}, u32[]{:S(2)}) collective-permute-start(bf16[512,1792]{1,0:T(8,128)(2,1)S(1)} %bitcast.25), channel_id=1, source_target_pairs={{0,32},{32,0},{1,33},{33,1},{2,34},{34,2},{3,35},{35,3},{4,36},{36... | collective-permute-start | bytes 5505032 | tf_op jit(solution)/shard_map/ppermute | solution.py:486
  174.2 2.0 %place.2 = (f32[512,512]{1,0:T(8,128)}, f32[512,1024]{1,0:T(8,128)}, f32[512,1536]{1,0:T(8,128)}, f32[512,512]{1,0:T(8,128)}) custom-call(s32[1]{0:T(128)} %bitcast.core.refs_0_, bf16[512,1792]{1,0:T(8,128)(2,1)S(1)} %bitcast.26), custom_call_target="tpu_custom_call" | custom-call | tf_op jit(solution)/shard_map/place/pallas_call | solution.py:473
  176.3 2.0 %add_convert_fusion = bf16[512,512]{1,0:T(8,128)(2,1)} fusion(f32[512,512]{1,0:T(8,128)S(1)} %fusion.5, bf16[512,512]{1,0:T(8,128)(2,1)} %collective-permute-done.8), kind=kLoop, calls=%fused_computation.9 | loop fusion | flops 786432 | bytes 2097152 | tf_op jit(solution)/shard_map/convert_element_type | solution.py:533
  178.3 0.0 collective-permute-done.9.refs_1_
  178.3 2.0 %place.3 = (f32[512,512]{1,0:T(8,128)}, f32[512,1024]{1,0:T(8,128)}, f32[512,1536]{1,0:T(8,128)}, f32[512,512]{1,0:T(8,128)}) custom-call(s32[1]{0:T(128)} %bitcast.core.refs_0_, bf16[512,1792]{1,0:T(8,128)(2,1)S(1)} %collective-permute-done.9.refs_1_, ...), custom_call_target="tpu_custom_call", output_to_operand_aliasing={{0}: (2, {}), {1}: (3, {}), {2}: (4, {}), {3}: (5, {})} | custom-call | tf_op jit(solution)/shard_map/place/pallas_call | solution.py:473
  (7 shorter events, 0.0 us)
Async XLA Ops:
  0.6 16.9 %collective-permute-start.1 = (bf16[512,512]{1,0:T(8,128)(2,1)}, bf16[512,512]{1,0:T(8,128)(2,1)S(1)}, u32[]{:S(2)}, u32[]{:S(2)}) collective-permute-start(bf16[512,512]{1,0:T(8,128)(2,1)} %x0.3), channel_id=1, source_target_pairs={{0,64},{64,0},{1,65},{65,1},{2,66},{66,2},{3,67},{67,3},{4,68},{68... | collective-permute-start | bytes 1572872 | tf_op jit(solution)/shard_map/ppermute | solution.py:486
  2.8 17.4 %collective-permute-start = (bf16[512,512]{1,0:T(8,128)(2,1)}, bf16[512,512]{1,0:T(8,128)(2,1)S(1)}, u32[]{:S(2)}, u32[]{:S(2)}) collective-permute-start(bf16[512,512]{1,0:T(8,128)(2,1)} %x0.3), channel_id=1, source_target_pairs={{0,32},{32,0},{1,33},{33,1},{2,34},{34,2},{3,35},{35,3},{4,36},{36... | collective-permute-start | bytes 1572872 | tf_op jit(solution)/shard_map/ppermute | solution.py:486
  3.7 16.4 %collective-permute-start.3 = (bf16[512,512]{1,0:T(8,128)(2,1)}, bf16[512,512]{1,0:T(8,128)(2,1)S(1)}, u32[]{:S(2)}, u32[]{:S(2)}) collective-permute-start(bf16[512,512]{1,0:T(8,128)(2,1)} %cot0.3), channel_id=1, source_target_pairs={{0,32},{32,0},{1,33},{33,1},{2,34},{34,2},{3,35},{35,3},{4,36},{36... | collective-permute-start | bytes 1572872 | tf_op jit(solution)/shard_map/ppermute | solution.py:486
  7.3 33.8 %all-to-all-start = ((bf16[32,32,512]{2,1,0:T(8,128)(2,1)}), bf16[32,32,512]{2,1,0:T(8,128)(2,1)S(1)}, u32[]{:S(2)}, u32[]{:S(2)}) async-start(bf16[32,32,512]{2,1,0:T(8,128)(2,1)} %bitcast.1), calls=%async_computation | async-start | bytes 2097152 | tf_op jit(solution)/shard_map/all_to_all | solution.py:494
  17.5 2.6 %copy-start.9 = (bf16[512,512]{1,0:T(8,128)(2,1)}, bf16[512,512]{1,0:T(8,128)(2,1)S(1)}, u32[]{:S(2)}) copy-start(bf16[512,512]{1,0:T(8,128)(2,1)S(1)} %collective-permute-done.1.x2) | copy-start | bytes 1572868
  17.5 2.7 %collective-permute-start.2 = (bf16[512,512]{1,0:T(8,128)(2,1)S(1)}, bf16[512,512]{1,0:T(8,128)(2,1)S(1)}, u32[]{:S(2)}, u32[]{:S(2)}) collective-permute-start(bf16[512,512]{1,0:T(8,128)(2,1)S(1)} %collective-permute-done.1.x2), channel_id=1, source_target_pairs={{0,32},{32,0},{1,33},{33,1},{2,34},{34,2},{3,35},{35,3},{4,36},{36... | collective-permute-start | bytes 1572872 | tf_op jit(solution)/shard_map/ppermute | solution.py:486
  20.2 0.8 copy-start.11
  20.2 1.0 copy-start.10
  21.1 0.8 copy-start.12
  68.7 9.7 %collective-permute-start.4 = (bf16[512,768]{1,0:T(8,128)(2,1)}, bf16[512,768]{1,0:T(8,128)(2,1)S(1)}, u32[]{:S(2)}, u32[]{:S(2)}) collective-permute-start(bf16[512,768]{1,0:T(8,128)(2,1)} %get-tuple-element.49), channel_id=1, source_target_pairs={{0,32},{32,0},{1,33},{33,1},{2,34},{34,2},{3,35},{35,3},{4,36},{36... | collective-permute-start | bytes 2359304 | tf_op jit(solution)/shard_map/ppermute | solution.py:486
  68.8 29.2 %all-to-all-start.1 = ((bf16[32,32,512]{2,1,0:T(8,128)(2,1)}), bf16[32,32,512]{2,1,0:T(8,128)(2,1)S(1)}, u32[]{:S(2)}, u32[]{:S(2)}) async-start(bf16[32,32,512]{2,1,0:T(8,128)(2,1)} %bitcast.30), calls=%async_computation.1 | async-start | bytes 2097152 | tf_op jit(solution)/shard_map/all_to_all | solution.py:494
  98.0 17.2 %copy-start.3 = (bf16[2,512,512]{2,1,0:T(8,128)(2,1)S(1)}, bf16[2,512,512]{2,1,0:T(8,128)(2,1)}, u32[]{:S(2)}) copy-start(bf16[2,512,512]{2,1,0:T(8,128)(2,1)} %get-tuple-element.53) | copy-start | bytes 3145732
  98.0 1.0 copy-start.1
  99.1 34.7 %all-to-all-start.2 = ((bf16[64,8,1792]{2,1,0:T(8,128)(2,1)}), bf16[64,8,1792]{2,1,0:T(8,128)(2,1)S(1)}, u32[]{:S(2)}, u32[]{:S(2)}) async-start(bf16[64,8,1792]{2,1,0:T(8,128)(2,1)} %bitcast.28), calls=%async_computation.2 | async-start | bytes 3670016 | tf_op jit(solution)/shard_map/all_to_all | solution.py:490
  108.9 3.9 %collective-permute-start.5 = (bf16[2,512,512]{2,1,0:T(8,128)(2,1)}, bf16[2,512,512]{2,1,0:T(8,128)(2,1)S(1)}, u32[]{:S(2)}, u32[]{:S(2)}) collective-permute-start(bf16[2,512,512]{2,1,0:T(8,128)(2,1)} %get-tuple-element.55), channel_id=1, source_target_pairs={{0,32},{32,0},{1,33},{33,1},{2,34},{34,2},{3,35},{35,3},{4,36},{36... | collective-permute-start | bytes 3145736 | tf_op jit(solution)/shard_map/ppermute | solution.py:486
  110.3 4.0 %collective-permute-start.6 = (bf16[2,512,512]{2,1,0:T(8,128)(2,1)}, bf16[2,512,512]{2,1,0:T(8,128)(2,1)S(1)}, u32[]{:S(2)}, u32[]{:S(2)}) collective-permute-start(bf16[2,512,512]{2,1,0:T(8,128)(2,1)} %get-tuple-element.56), channel_id=1, source_target_pairs={{0,32},{32,0},{1,33},{33,1},{2,34},{34,2},{3,35},{35,3},{4,36},{36... | collective-permute-start | bytes 3145736 | tf_op jit(solution)/shard_map/ppermute | solution.py:486
  112.8 1.5 copy-start.6
  114.3 1.0 copy-start.8
  135.3 35.6 %all-to-all-start.3 = ((bf16[64,8,1792]{2,1,0:T(8,128)(2,1)}), bf16[64,8,1792]{2,1,0:T(8,128)(2,1)S(1)}, u32[]{:S(2)}, u32[]{:S(2)}) async-start(bf16[64,8,1792]{2,1,0:T(8,128)(2,1)} %sum_spread.1), calls=%async_computation.3 | async-start | bytes 3670016 | tf_op jit(solution)/shard_map/all_to_all | solution.py:490
  140.6 9.7 %copy-start = (f32[512,512]{1,0:T(8,128)S(1)}, f32[512,512]{1,0:T(8,128)}, u32[]{:S(2)}) copy-start(f32[512,512]{1,0:T(8,128)} %get-tuple-element.58) | copy-start | bytes 3145732
  143.5 3.9 %collective-permute-start.7 = (bf16[512,256]{1,0:T(8,128)(2,1)}, bf16[512,256]{1,0:T(8,128)(2,1)}, u32[]{:S(2)}, u32[]{:S(2)}) collective-permute-start(bf16[512,256]{1,0:T(8,128)(2,1)} %slice.43), channel_id=1, source_target_pairs={{0,32},{32,0},{1,33},{33,1},{2,34},{34,2},{3,35},{35,3},{4,36},{36... | collective-permute-start | bytes 786440 | tf_op jit(solution)/shard_map/ppermute | solution.py:486
  147.3 5.0 %copy-start.2 = (bf16[32,32,512]{2,1,0:T(8,128)(2,1)S(1)}, bf16[32,32,512]{2,1,0:T(8,128)(2,1)}, u32[]{:S(2)}) copy-start(bf16[32,32,512]{2,1,0:T(8,128)(2,1)} %copy-done.1) | copy-start | bytes 3145732
  147.3 5.0 %copy-start.4 = (bf16[2,512,512]{2,1,0:T(8,128)(2,1)S(1)}, bf16[2,512,512]{2,1,0:T(8,128)(2,1)}, u32[]{:S(2)}) copy-start(bf16[2,512,512]{2,1,0:T(8,128)(2,1)} %get-tuple-element.53) | copy-start | bytes 3145732
  147.3 5.0 %copy-start.5 = (bf16[2,512,512]{2,1,0:T(8,128)(2,1)S(1)}, bf16[2,512,512]{2,1,0:T(8,128)(2,1)}, u32[]{:S(2)}) copy-start(bf16[2,512,512]{2,1,0:T(8,128)(2,1)} %get-tuple-element.54) | copy-start | bytes 3145732
  147.3 5.0 %copy-start.7 = (bf16[2,512,512]{2,1,0:T(8,128)(2,1)S(1)}, bf16[2,512,512]{2,1,0:T(8,128)(2,1)}, u32[]{:S(2)}) copy-start(bf16[2,512,512]{2,1,0:T(8,128)(2,1)} %copy-done.6) | copy-start | bytes 3145732
  148.8 22.1 %collective-permute-start.8 = (bf16[512,512]{1,0:T(8,128)(2,1)}, bf16[512,512]{1,0:T(8,128)(2,1)}, u32[]{:S(2)}, u32[]{:S(2)}) collective-permute-start(bf16[512,512]{1,0:T(8,128)(2,1)} %fusion.8), channel_id=1, source_target_pairs={{0,64},{64,0},{1,65},{65,1},{2,66},{66,2},{3,67},{67,3},{4,68},{68... | collective-permute-start | bytes 1572872 | tf_op jit(solution)/shard_map/ppermute | solution.py:486
  170.9 7.3 %collective-permute-start.9 = (bf16[512,1792]{1,0:T(8,128)(2,1)S(1)}, bf16[512,1792]{1,0:T(8,128)(2,1)S(1)}, u32[]{:S(2)}, u32[]{:S(2)}) collective-permute-start(bf16[512,1792]{1,0:T(8,128)(2,1)S(1)} %bitcast.25), channel_id=1, source_target_pairs={{0,32},{32,0},{1,33},{33,1},{2,34},{34,2},{3,35},{35,3},{4,36},{36... | collective-permute-start | bytes 5505032 | tf_op jit(solution)/shard_map/ppermute | solution.py:486
